TPU v7x, 32 devices: a whole 2x2x4 slice. The times are simulated.
32 devices in a mesh: groups: 2 (over y), section: 4 (over z), sector: 4 (over x, core).
Axes of the slice: x: 2, y: 2, z: 4, core: 2. Of those that a mesh axis runs over, the one named last changes fastest.
Arguments:
- env_left: bfloat16 [8, 8, 30, 128, 128], P(('groups', 'section'), 'sector'), parts along dimension 0, may hold values from -0.5 to 0.5
- env_right: bfloat16 [8, 8, 30, 128, 128], P(('groups', 'section'), 'sector'), parts along dimension 0, may hold values from -0.5 to 0.5
- edge_left: bfloat16 [8, 8, 128, 128], P(('groups', 'section'), 'sector'), parts along dimension 0, may hold values from -0.5 to 0.5
- edge_right: bfloat16 [8, 8, 128, 128], P(('groups', 'section'), 'sector'), parts along dimension 0, may hold values from -0.5 to 0.5
- wave_blocks: bfloat16 [8, 8, 128, 128], P(('groups', 'section'), 'sector'), parts along dimension 0, may hold values from -12 to 12
- mpo_coef: float32 [8, 8, 30], P(('groups', 'section'), 'sector'), parts along dimension 0, may hold values from -4 to 4
- onsite: float32 [8, 8], P(('groups', 'section'), 'sector'), parts along dimension 0, may hold values from 1 to 4
- routes: int32 [8, 8, 30], P(('groups', 'section'), 'sector'), parts along dimension 0, may hold values from 0 to 7
- sector_sizes: int32 [16], P(('groups', 'sector')), parts along dimension 0, may hold values from 64 to 128
Outputs:
- first_image: bfloat16 [8, 8, 128, 128], P(('groups', 'section'), 'sector'), parts along dimension 0
- second_image: bfloat16 [8, 8, 128, 128], P(('groups', 'section'), 'sector'), parts along dimension 0
There are 2 independent parts, one for each index of `groups`. A program takes and returns all parts, laid end to end along the dimension named above; each array names one. Nothing has to cross between parts.
All inputs are finite; a program needn't handle non-finite values.
Results may differ from a plain program's by a relative error of at most 0.0069.
Values may be sent and summed in bfloat16 or wider, within the bound.
No kernel may reach another device: no remote copies, remote signals or barrier semaphores. Data moves between devices by JAX's collectives and lax.ppermute only.
A program may use at most 64 MiB of HBM per device.

v0:
```python
import jax
import jax.numpy as jnp
from jax import lax
from jax.sharding import PartitionSpec as P

epsilon = 1e-06


def shifted(x, axis, by):
    devices = lax.axis_size(axis)
    pairs = [(i, i + by) for i in range(devices) if 0 <= i + by < devices]
    return lax.ppermute(x, axis, pairs)


def apply_hamiltonian(
    vector, new_left, new_right, live_mask, weight, energy, routes, block_total, owner_index
):
    per_device = vector.shape[0]
    masked = jnp.where(live_mask, vector, jnp.zeros_like(vector))
    right_half = jnp.einsum(
        "kab,kwcb->kwac", masked, new_right, preferred_element_type=jnp.float32
    ).astype(jnp.bfloat16)
    contrib = jnp.einsum(
        "kwab,kwbc->kwac", new_left, right_half, preferred_element_type=jnp.float32
    )
    target_ids = lax.iota(jnp.int32, block_total)
    selector = jnp.where(routes[:, :, None] == target_ids[None, None, :], weight[:, :, None], 0.0)
    summed_all = lax.psum(
        jnp.einsum("kwj,kwab->jab", selector, contrib, precision=lax.Precision.HIGHEST), "sector"
    )
    summed = lax.dynamic_slice_in_dim(summed_all, owner_index * per_device, per_device, 0)
    total = summed + energy[:, None, None] * masked.astype(jnp.float32)
    return jnp.where(live_mask, total, jnp.zeros_like(total))


def body(
    env_left, env_right, edge_left, edge_right, wave_blocks, mpo_coef, onsite, routes, sector_sizes
):
    left_env = env_left[0]
    right_env = env_right[0]
    left_edge = edge_left[0]
    right_edge = edge_right[0]
    wave_local = wave_blocks[0]
    per_device = wave_local.shape[0]
    block_size = wave_local.shape[1]
    channels = left_env.shape[1]
    section_count = lax.axis_size("section")
    section_index = lax.axis_index("section")
    owner_index = lax.axis_index("sector")
    block_total = per_device * lax.axis_size("sector")
    inner_left = jnp.einsum(
        "kba,kwbc->kwac", left_edge, left_env, preferred_element_type=jnp.float32
    ).astype(jnp.bfloat16)
    passed_left = jnp.einsum(
        "kwac,kcd->kwad", inner_left, left_edge, preferred_element_type=jnp.float32
    ).astype(jnp.bfloat16)
    from_left = shifted(passed_left, "section", 1)
    inner_right = jnp.einsum(
        "kab,kwbc->kwac", right_edge, right_env, preferred_element_type=jnp.float32
    ).astype(jnp.bfloat16)
    passed_right = jnp.einsum(
        "kwac,kdc->kwad", inner_right, right_edge, preferred_element_type=jnp.float32
    ).astype(jnp.bfloat16)
    from_right = shifted(passed_right, "section", -1)
    new_left = jnp.where(section_index == 0, left_env, from_left)
    new_right = jnp.where(section_index == section_count - 1, right_env, from_right)
    position = jnp.arange(block_size, dtype=jnp.int32)
    alive = position[None, :] < sector_sizes[:, None]
    live_mask = alive[:, :, None] & alive[:, None, :]
    weight = mpo_coef[0] * channels ** (-0.5)
    energy = onsite[0]
    route_local = routes[0]
    image1 = apply_hamiltonian(
        wave_local,
        new_left,
        new_right,
        live_mask,
        weight,
        energy,
        route_local,
        block_total,
        owner_index,
    )
    masked_wave = jnp.where(live_mask, wave_local, jnp.zeros_like(wave_local)).astype(jnp.float32)
    correlation, squares = lax.psum(
        (jnp.sum(masked_wave * image1), jnp.sum(masked_wave * masked_wave)), "sector"
    )
    ritz_value = correlation / (squares + epsilon)
    resid = image1 - ritz_value * masked_wave
    resid_sq = lax.psum(jnp.sum(resid * resid), "sector")
    correction = (resid * jnp.sqrt(squares / (resid_sq + epsilon))).astype(jnp.bfloat16)
    image2 = apply_hamiltonian(
        correction,
        new_left,
        new_right,
        live_mask,
        weight,
        energy,
        route_local,
        block_total,
        owner_index,
    )
    return (image1.astype(jnp.bfloat16)[None], image2.astype(jnp.bfloat16)[None])


def solution(mesh):
    in_specs = (
        P(("groups", "section"), "sector", None, None, None),
        P(("groups", "section"), "sector", None, None, None),
        P(("groups", "section"), "sector", None, None),
        P(("groups", "section"), "sector", None, None),
        P(("groups", "section"), "sector", None, None),
        P(("groups", "section"), "sector", None),
        P(("groups", "section"), "sector"),
        P(("groups", "section"), "sector", None),
        P(("groups", "sector")),
    )
    out_specs = (
        P(("groups", "section"), "sector", None, None),
        P(("groups", "section"), "sector", None, None),
    )
    return jax.shard_map(body, mesh=mesh, in_specs=in_specs, out_specs=out_specs, check_vma=False)
```

profile of v0, /device:TPU:0, one launch (start us, length us, event | category | flops | bytes accessed | tf_op | source)
XLA Modules:
  0.0 188.5 jit_solution(6028755382348427703)
XLA Ops:
  7.2 0.0 copy-start
  7.2 0.0 copy-start.1
  7.2 0.0 all-reduce.4.cloned.1.call-start
  7.2 0.8 copy-done
  8.0 4.0 %fusion.35 = bf16[2,30,128,128]{3,2,1,0:T(8,128)(2,1)} fusion(bf16[1,2,30,128,128]{4,3,2,1,0:T(8,128)(2,1)} %param.10, bf16[1,2,128,128]{3,2,1,0:T(8,128)(2,1)S(1)} %copy-done), kind=kOutput, calls=%fused_computation.23 | convolution fusion | flops 505282560 | bytes 3997696 | tf_op jit(solution)/shard_map/kwac,kdc->kwad/dot_general | solution.py:61
  12.0 1.4 collective-permute-start.1
  13.5 2.5 %fusion.30 = bf16[2,30,128,128]{3,2,1,0:T(8,128)(2,1)} fusion(bf16[1,2,30,128,128]{4,3,2,1,0:T(8,128)(2,1)S(1)} %copy-done.1, bf16[1,2,128,128]{3,2,1,0:T(8,128)(2,1)S(1)} %copy-done.3), kind=kOutput, calls=%fused_computation.22 | convolution fusion | flops 505282560 | bytes 3997696 | tf_op jit(solution)/shard_map/kwac,kcd->kwad/dot_general | solution.py:54
  16.0 6.8 %collective-permute-start = (bf16[2,30,128,128]{3,2,1,0:T(8,128)(2,1)}, bf16[2,30,128,128]{3,2,1,0:T(8,128)(2,1)}, u32[]{:S(2)}, u32[]{:S(2)}) collective-permute-start(bf16[2,30,128,128]{3,2,1,0:T(8,128)(2,1)} %fusion.30), channel_id=1, source_target_pairs={{0,4},{4,8},{8,12},{1,5},{5,9},{9,13},{2,6},{6,10},{10,14},{3,7},{... | collective-permute-start | bytes 5898248 | tf_op jit(solution)/shard_map/ppermute | solution.py:12
  22.8 0.1 iota_compare_fusion.3
  22.9 0.1 copy.11
  23.0 0.0 copy-done.6
  23.0 0.2 fusion.72
  23.3 0.0 copy-start.4
  23.3 36.9 %collective-permute-done.1 = bf16[2,30,128,128]{3,2,1,0:T(8,128)(2,1)} collective-permute-done((bf16[2,30,128,128]{3,2,1,0:T(8,128)(2,1)}, bf16[2,30,128,128]{3,2,1,0:T(8,128)(2,1)}, u32[]{:S(2)}, u32[]{:S(2)}) %collective-permute-start.1) | collective-permute-done | bytes 1966112 | tf_op jit(solution)/shard_map/ppermute | solution.py:12
  60.2 3.7 %collective-permute-done = bf16[2,30,128,128]{3,2,1,0:T(8,128)(2,1)} collective-permute-done((bf16[2,30,128,128]{3,2,1,0:T(8,128)(2,1)}, bf16[2,30,128,128]{3,2,1,0:T(8,128)(2,1)}, u32[]{:S(2)}, u32[]{:S(2)}) %collective-permute-start) | collective-permute-done | bytes 1966112 | tf_op jit(solution)/shard_map/ppermute | solution.py:12
  63.9 6.0 %fusion.16 = f32[2,30,128,128]{3,2,1,0:T(8,128)} fusion(bf16[2,30,128,128]{3,2,1,0:T(8,128)(2,1)} %collective-permute-done, bf16[1,2,30,128,128]{4,3,2,1,0:T(8,128)(2,1)S(1)} %copy-done.1, pred[]{:T(512)S(6)} %eq.32, bf16[2,30,128,128]{3,2,1,0:T(8,128)(2,1)} %collective-permute-done.1, bf16[1,2,30,128,128]{4,3,2,1,0:T(8,128)(2,1)} %param.10, pred[]{:T(512)S(6)} %eq.33, ...), kind=kOutput, calls=%fused_computation.17 | convolution fusion | flops 506265600 | bytes 11862018 | tf_op jit(solution)/shard_map/kwab,kwbc->kwac/dot_general | solution.py:23
  69.9 7.2 %fusion.40 = f32[8,128,128]{2,0,1:T(8,128)} fusion(f32[2,30,128,128]{3,2,1,0:T(8,128)} %fusion.16, f32[2,30]{1,0:T(2,128)S(1)} %multiply_bitcast_fusion, s32[2,30]{1,0:T(2,128)S(1)} %bitcast.83), kind=kOutput, calls=%fused_computation.24 | convolution fusion | flops 94372800 | bytes 4456928 | tf_op jit(solution)/shard_map/kwj,kwab->jab/dot_general | solution.py:29
  77.1 0.0 all-reduce.4.cloned.1.call-update
  77.1 0.0 all-reduce.6.cloned.1.call-start
  77.2 36.8 %all-reduce.4.cloned.1.call-done = f32[8,128,128]{2,0,1:T(8,128)} async-done(((f32[8,128,128]{2,0,1:T(8,128)}), f32[8,128,128]{2,0,1:T(8,128)}) %all-reduce.4.cloned.1.call-update) | async-done | bytes 524304 | tf_op jit(solution)/shard_map/psum | solution.py:28
  114.0 2.0 %fusion.47 = (f32[]{:T(128)}, f32[]{:T(128)}, f32[2,128,128]{2,0,1:T(2,128)S(1)}) fusion(f32[2]{0:T(128)S(1)} %bitcast.85, f32[8,128,128]{2,0,1:T(8,128)} %all-reduce.4.cloned.1.call-done, s32[]{:T(128)S(6)} %select_n.44, pred[2,128]{1,0:T(4,128)(4,1)S(1)} %iota_compare_fusion.3, pred[2,128]{0,1:T(8,128)(4,1)S(1)} %copy.11, ...), kind=kLoop, calls=%fused_computation.35 | loop fusion | flops 327678 | bytes 328212 | tf_op jit(solution)/shard_map/reduce_sum | solution.py:86
  115.9 6.4 %all-reduce = (f32[]{:T(128)}, f32[]{:T(128)}) all-reduce(f32[]{:T(128)} %get-tuple-element.5, f32[]{:T(128)} %get-tuple-element.4), channel_id=1, replica_groups=mesh['groups'=2,'section'=4,'sector'=4] {'sector'}, use_global_device_ids=true, to_apply=%region_4.5 | all-reduce | flops 2 | bytes 16 | tf_op jit(solution)/shard_map/psum | solution.py:85
  123.6 0.8 multiply_reduce_fusion
  124.4 6.5 %psum.38 = f32[]{:T(128)} all-reduce(f32[]{:T(128)} %get-tuple-element.9), channel_id=1, replica_groups=mesh['groups'=2,'section'=4,'sector'=4] {'sector'}, use_global_device_ids=true, to_apply=%region_6.7 | all-reduce | flops 1 | bytes 8 | tf_op jit(solution)/shard_map/psum | solution.py:90
  132.3 0.2 and_select_fusion.1
  132.6 6.0 %fusion.12 = f32[2,30,128,128]{3,2,1,0:T(8,128)} fusion(bf16[2,30,128,128]{3,2,1,0:T(8,128)(2,1)} %collective-permute-done, bf16[1,2,30,128,128]{4,3,2,1,0:T(8,128)(2,1)S(1)} %copy-done.1, pred[]{:T(512)S(6)} %eq.32, bf16[2,30,128,128]{3,2,1,0:T(8,128)(2,1)} %collective-permute-done.1, bf16[1,2,30,128,128]{4,3,2,1,0:T(8,128)(2,1)} %param.10, pred[]{:T(512)S(6)} %eq.33, ...), kind=kOutput, calls=%fused_computation.14 | convolution fusion | flops 506265600 | bytes 11862018 | tf_op jit(solution)/shard_map/kwab,kwbc->kwac/dot_general | solution.py:23
  138.6 7.1 %fusion.43 = f32[8,128,128]{2,0,1:T(8,128)} fusion(f32[2,30,128,128]{3,2,1,0:T(8,128)} %fusion.12, f32[2,30]{1,0:T(2,128)S(1)} %multiply_bitcast_fusion, s32[2,30]{1,0:T(2,128)S(1)} %bitcast.84), kind=kOutput, calls=%fused_computation.25 | convolution fusion | flops 94372800 | bytes 4456928 | tf_op jit(solution)/shard_map/kwj,kwab->jab/dot_general | solution.py:29
  145.7 0.0 all-reduce.6.cloned.1.call-update
  145.8 0.6 copy.13
  146.4 33.4 %all-reduce.6.cloned.1.call-done = f32[8,128,128]{2,0,1:T(8,128)} async-done(((f32[8,128,128]{2,0,1:T(8,128)}), f32[8,128,128]{2,0,1:T(8,128)}) %all-reduce.6.cloned.1.call-update) | async-done | bytes 524304 | tf_op jit(solution)/shard_map/psum | solution.py:28
  179.8 1.3 fusion.59
  181.1 0.6 copy.14
  (12 shorter events, 0.0 us)
Async XLA Ops:
  7.2 0.8 copy-start
  7.2 6.3 %copy-start.1 = (bf16[1,2,30,128,128]{4,3,2,1,0:T(8,128)(2,1)S(1)}, bf16[1,2,30,128,128]{4,3,2,1,0:T(8,128)(2,1)}, u32[]{:S(2)}) copy-start(bf16[1,2,30,128,128]{4,3,2,1,0:T(8,128)(2,1)} %param.9) | copy-start | bytes 5898244
  7.2 6.3 %copy-start.3 = (bf16[1,2,128,128]{3,2,1,0:T(8,128)(2,1)S(1)}, bf16[1,2,128,128]{3,2,1,0:T(8,128)(2,1)}, u32[]{:S(2)}) copy-start(bf16[1,2,128,128]{3,2,1,0:T(8,128)(2,1)} %param.11) | copy-start | bytes 196612
  7.2 106.7 %all-reduce.4.cloned.1.call-start = ((), (), s32[]{:S(2)}) async-start(), calls=%async_computation | async-start | bytes 1048576 | tf_op jit(solution)/shard_map/psum | solution.py:28
  12.0 10.8 %copy-start.7 = (s32[2]{0:T(128)S(1)}, s32[2]{0:T(128)}, u32[]{:S(2)}) copy-start(s32[2]{0:T(128)} %param.17) | copy-start | bytes 28
  12.0 11.0 %copy-start.6 = (f32[1,2,30]{2,1,0:T(2,128)S(1)}, f32[1,2,30]{2,1,0:T(2,128)}, u32[]{:S(2)}) copy-start(f32[1,2,30]{2,1,0:T(2,128)} %param.14) | copy-start | bytes 724
  12.0 11.0 %copy-start.2 = (bf16[1,2,128,128]{3,2,1,0:T(8,128)(2,1)S(1)}, bf16[1,2,128,128]{3,2,1,0:T(8,128)(2,1)}, u32[]{:S(2)}) copy-start(bf16[1,2,128,128]{3,2,1,0:T(8,128)(2,1)} %param.13) | copy-start | bytes 196612
  12.0 48.2 %collective-permute-start.1 = (bf16[2,30,128,128]{3,2,1,0:T(8,128)(2,1)}, bf16[2,30,128,128]{3,2,1,0:T(8,128)(2,1)}, u32[]{:S(2)}, u32[]{:S(2)}) collective-permute-start(bf16[2,30,128,128]{3,2,1,0:T(8,128)(2,1)} %fusion.35), channel_id=1, source_target_pairs={{4,0},{8,4},{12,8},{5,1},{9,5},{13,9},{6,2},{10,6},{14,10},{7,3},{... | collective-permute-start | bytes 5898248 | tf_op jit(solution)/shard_map/ppermute | solution.py:12
  16.0 47.9 %collective-permute-start = (bf16[2,30,128,128]{3,2,1,0:T(8,128)(2,1)}, bf16[2,30,128,128]{3,2,1,0:T(8,128)(2,1)}, u32[]{:S(2)}, u32[]{:S(2)}) collective-permute-start(bf16[2,30,128,128]{3,2,1,0:T(8,128)(2,1)} %fusion.30), channel_id=1, source_target_pairs={{0,4},{4,8},{8,12},{1,5},{5,9},{9,13},{2,6},{6,10},{10,14},{3,7},{... | collective-permute-start | bytes 5898248 | tf_op jit(solution)/shard_map/ppermute | solution.py:12
  23.3 46.7 %copy-start.4 = (s32[1,2,30]{2,1,0:T(2,128)S(1)}, s32[1,2,30]{2,1,0:T(2,128)}, u32[]{:S(2)}) copy-start(s32[1,2,30]{2,1,0:T(2,128)} %param.16) | copy-start | bytes 724
  69.9 44.0 %copy-start.5 = (f32[1,2]{1,0:T(1,128)S(1)}, f32[1,2]{1,0:T(1,128)}, u32[]{:S(2)}) copy-start(f32[1,2]{1,0:T(1,128)} %param.15) | copy-start | bytes 28
  77.1 102.7 %all-reduce.6.cloned.1.call-start = ((), (), s32[]{:S(2)}) async-start(), calls=%async_computation.1 | async-start | bytes 1048576 | tf_op jit(solution)/shard_map/psum | solution.py:28
Sparse Core Ops, SparseCore 0:
  77.2 36.6 all-reduce.3
  145.9 33.8 all-reduce.5
where the time goes:
time: 189 us
  waiting for transfers between devices  111 us (59%)
  matrix products  32.9 us (17%)
  between operations  16.8 us (9%)
  blocking collectives  12.9 us (7%)
  starting transfers between devices  8.33 us (4%)
  other arithmetic  4.59 us (2%)
  local copies, waits for them, and re-layouts  2.22 us (1%)
    psum x2, waiting for transfers between devices, apply_hamiltonian(): lax.psum(jnp.einsum('kwj,kwab->jab', selector, contrib, precision=lax.Pre...  70.2 us
    ppermute x2, waiting for transfers between devices, shifted(): return lax.ppermute(x, axis, pairs)  40.6 us
    dot_general x2, matrix products, apply_hamiltonian(): jnp.einsum('kwj,kwab->jab', selector, contrib, precision=lax.Precision.HI...  14.3 us
    dot_general x2, matrix products, apply_hamiltonian(): jnp.einsum('kwab,kwbc->kwac', new_left, right_half, preferred_element_typ...  12.1 us
    ppermute x2, starting transfers between devices, shifted(): return lax.ppermute(x, axis, pairs)  8.25 us
    psum x1, blocking collectives, body(): resid_sq = lax.psum(jnp.sum(resid * resid), 'sector')  6.54 us
    psum x1, blocking collectives, body(): lax.psum((jnp.sum(masked_wave * image1), jnp.sum(masked_wave * masked_wav...  6.37 us
    dot_general x1, matrix products, body(): jnp.einsum('kwac,kdc->kwad', inner_right, right_edge, preferred_element_t...  4 us
  transfers between devices with their start and end apart: 4, of which 4 were waited for; matrix products, arithmetic and copies ran while one was open for 2% of the time, Pallas kernels for 0%

commit v1 on v0

v1 whole, which is shorter than its diff:
```python
import functools

import jax
import jax.numpy as jnp
from jax import lax
from jax.experimental import pallas as pl
from jax.experimental.pallas import tpu as pltpu
from jax.sharding import PartitionSpec as P

epsilon = 1e-06
VMEM_BYTES = 24 * 1024 * 1024
EXTRA = 16

f32 = jnp.float32
bf16 = jnp.bfloat16

VM = pl.BlockSpec(memory_space=pltpu.VMEM)
SM = pl.BlockSpec(memory_space=pltpu.SMEM)
HB = pl.BlockSpec(memory_space=pl.ANY)


def call(kernel, outs, in_specs, scratch=(), aliases=None, flops=0, moved=0, out_specs=None):
    return pl.pallas_call(
        kernel,
        out_shape=outs,
        in_specs=in_specs,
        out_specs=[VM] * len(outs) if out_specs is None else out_specs,
        scratch_shapes=list(scratch),
        input_output_aliases=aliases or {},
        compiler_params=pltpu.CompilerParams(vmem_limit_bytes=VMEM_BYTES),
        cost_estimate=pl.CostEstimate(flops=flops, bytes_accessed=moved, transcendentals=0),
    )


def dot(a, b):
    return jnp.dot(a, b, preferred_element_type=f32)


def dot_t(a, b):
    return lax.dot_general(a, b, (((1,), (1,)), ((), ())), preferred_element_type=f32)


def chunk_sizes(channels):
    first = max(1, channels // 10)
    last = max(1, channels // 6)
    middle = channels - first - last
    return [c for c in (first, middle, last) if c > 0]


def grow_kernel(start, count, left_hbm, right_hbm, edge_l, edge_r, out_l, out_r, buf_l, buf_r, sems):
    copies = [
        pltpu.make_async_copy(src.at[0, :, pl.ds(start, count)], dst, sems.at[i])
        for i, (src, dst) in enumerate(((left_hbm, buf_l), (right_hbm, buf_r)))
    ]
    for c in copies:
        c.start()
    for c in copies:
        c.wait()
    for k in range(buf_l.shape[0]):
        e = edge_l[0, k]
        e_t = e.T
        f = edge_r[0, k]

        def step(w, carry):
            inner = dot(e_t, buf_l[k, w]).astype(bf16)
            out_l[k, w] = dot(inner, e).astype(bf16)
            inner = dot(f, buf_r[k, w]).astype(bf16)
            out_r[k, w] = dot_t(inner, f).astype(bf16)
            return carry

        lax.fori_loop(0, count, step, 0, unroll=3 if count % 3 == 0 else 1)


def grow(env_left, env_right, edge_left, edge_right, start, count):
    _, pd, _, b, _ = env_left.shape
    block = jax.ShapeDtypeStruct((pd, count, b, b), bf16)
    buf = pltpu.VMEM((pd, count, b, b), bf16)
    return call(
        functools.partial(grow_kernel, start, count),
        [block, block],
        [HB, HB, VM, VM],
        [buf, buf, pltpu.SemaphoreType.DMA((2,))],
        flops=8 * pd * count * b**3,
        moved=8 * pd * count * b * b,
    )(env_left, env_right, edge_left, edge_right)


def live_of(size, shape):
    rows = lax.broadcasted_iota(jnp.int32, shape, 0) < size
    cols = lax.broadcasted_iota(jnp.int32, shape, 1) < size
    return rows & cols


def mask_kernel(wave, sizes, out):
    for k in range(wave.shape[1]):
        v = wave[0, k].astype(f32)
        out[k] = jnp.where(live_of(sizes[k], v.shape), v, 0.0).astype(bf16)


def mask_wave(wave, sizes):
    _, pd, b, _ = wave.shape
    return call(mask_kernel, [jax.ShapeDtypeStruct((pd, b, b), bf16)], [VM, SM], moved=4 * pd * b * b)(wave, sizes)[0]


def apply_block(left, right, lead, start, count, m, k, acc, coef, routes, scale):
    for w in range(count):
        t = dot(left[k, lead + w], m).astype(bf16)
        contrib = dot_t(t, right[k, lead + w])
        j = routes[0, k, start + w]
        acc[j] += contrib * (coef[0, k, start + w] * scale)


def select_copy(flag, own, got, dst, sem, start, count, lead):
    @pl.when(flag)
    def _():
        pltpu.make_async_copy(own.at[0, :, pl.ds(start, count)], dst, sem).start()

    @pl.when(jnp.logical_not(flag))
    def _():
        pltpu.make_async_copy(got.at[:, pl.ds(lead, count)], dst, sem).start()


def wait_copy(got, dst, sem, lead, count):
    pltpu.make_async_copy(got.at[:, pl.ds(lead, count)], dst, sem).wait()


def three_terms(x, rows):
    hi = x.astype(bf16).astype(f32)
    mid = (x - hi).astype(bf16).astype(f32)
    low = x - hi - mid
    place = lax.broadcasted_iota(jnp.int32, (EXTRA, 128), 0)
    return jnp.where(place == 0, hi, jnp.where(place == 1, mid, jnp.where(place == 2, low, 0.0))).astype(bf16)


def from_terms(rows):
    return jnp.sum(rows.astype(f32), axis=0, keepdims=True)


def total_of(x):
    return jnp.sum(jnp.sum(x, axis=0, keepdims=True), axis=1, keepdims=True)


def split_halves(acc, groups, pd, b, bit, send, keep, extra):
    for i in range(groups // 2):
        for q in range(pd):
            kept = acc[(2 * i + bit) * pd + q]
            sent = acc[(2 * i + 1 - bit) * pd + q]
            keep[i * pd + q] = kept
            send[pl.ds((i * pd + q) * b, b)] = sent.astype(bf16)
    send[pl.ds(groups // 2 * pd * b, EXTRA)] = three_terms(extra, EXTRA)


def first_kernel(
    chunk, is_first, is_last, groups, scale,
    left_own, right_own, left_got, right_got, m, coef, routes, *rest
):
    start, count = chunk
    rest = list(rest)
    acc_in = None if is_first else rest.pop(0)
    if is_last:
        gathered, onsite = rest.pop(0), rest.pop(0)
        send, keep, squares_out, corr_out = [rest.pop(0) for _ in range(4)]
    else:
        acc_out = rest.pop(0)
    buf_l, buf_r, acc, sems = rest
    pd, b = m.shape[0], m.shape[1]
    section = lax.axis_index("section")
    at_start = section == 0
    at_end = section == lax.axis_size("section") - 1
    select_copy(at_start, left_own, left_got, buf_l, sems.at[0], start, count, 0)
    select_copy(at_end, right_own, right_got, buf_r, sems.at[1], start, count, 0)
    if is_first:
        acc[...] = jnp.zeros_like(acc)
    else:
        acc[...] = acc_in[...]
    wait_copy(left_got, buf_l, sems.at[0], 0, count)
    wait_copy(right_got, buf_r, sems.at[1], 0, count)
    unit = 3 if count % 3 == 0 else (5 if count % 5 == 0 else (2 if count % 2 == 0 else 1))
    for k in range(pd):
        mk = m[k]

        def step(s, carry):
            apply_block(buf_l, buf_r, s * unit, start + s * unit, unit, mk, k, acc, coef, routes, scale)
            return carry

        lax.fori_loop(0, count // unit, step, 0)
    if not is_last:
        acc_out[...] = acc[...]
        return
    me = lax.axis_index("sector")
    corr = jnp.zeros((b, b), f32)
    squares = jnp.zeros((b, b), f32)
    for j in range(groups * pd):
        g = gathered[j].astype(f32)
        corr += g * acc[j]
        squares += g * g
    for k in range(pd):
        g = m[k].astype(f32)
        corr += onsite[0, k] * (g * g)
    corr = total_of(corr)
    squares_out[...] = jnp.broadcast_to(total_of(squares), squares_out.shape)
    corr_out[...] = jnp.broadcast_to(corr, corr_out.shape)
    split_halves(acc, groups, pd, b, lax.rem(me, 2), send, keep, corr)


def first_apply(chunk, is_first, is_last, groups, channels, arrays, acc_in, extra):
    start, count = chunk
    left_own, right_own, left_got, right_got, m, coef, routes = arrays
    pd, b, _ = m.shape
    total = jax.ShapeDtypeStruct((groups * pd, b, b), f32)
    args = [left_own, right_own, left_got, right_got, m, coef, routes]
    specs = [HB, HB, HB, HB, VM, SM, SM]
    if not is_first:
        args.append(acc_in)
        specs.append(VM)
    if is_last:
        args += list(extra)
        specs += [VM, SM]
        outs = exchange_shapes(groups, pd, b) + [jax.ShapeDtypeStruct((8, 128), f32)] * 2
    else:
        outs = [total]
    buf = pltpu.VMEM((pd, count, b, b), bf16)
    return call(
        functools.partial(first_kernel, chunk, is_first, is_last, groups, channels ** (-0.5)),
        outs,
        specs,
        [buf, buf, pltpu.VMEM((groups * pd, b, b), f32), pltpu.SemaphoreType.DMA((2,))],
        flops=4 * pd * count * b**3,
        moved=4 * pd * count * b * b,
    )(*args)


def exchange_shapes(groups, pd, b):
    half = groups // 2 * pd
    return [
        jax.ShapeDtypeStruct((half * b + EXTRA, b), bf16),
        jax.ShapeDtypeStruct((half, b, b), f32),
    ]


def combine_kernel(groups, stage, pd, keep_in, got, extra_in, send, keep, extra_out, acc):
    b = keep_in.shape[1]
    me = lax.axis_index("sector")
    for i in range(groups * pd):
        acc[i] = keep_in[i] + got[pl.ds(i * b, b)].astype(f32)
    extra = extra_in[0:1, 0:1] + from_terms(got[pl.ds(groups * pd * b, EXTRA)])[:, 0:1]
    extra_out[...] = jnp.broadcast_to(extra, extra_out.shape)
    bit = lax.rem(lax.div(me, 2**stage), 2)
    split_halves(acc, groups, pd, b, bit, send, keep, extra)


def combine(groups, stage, pd, keep, got, extra):
    b = keep.shape[1]
    return call(
        functools.partial(combine_kernel, groups, stage, pd),
        exchange_shapes(groups, pd, b) + [jax.ShapeDtypeStruct((8, 128), f32)],
        [VM, VM, VM],
        [pltpu.VMEM((groups * pd, b, b), f32)],
        flops=groups * pd * b * b,
        moved=8 * groups * pd * b * b,
    )(keep, got, extra)


def exchange(sectors, pd, send, keep, extra):
    stage = 0
    groups = sectors
    while True:
        got = lax.ppermute(send, "sector", [(i, i ^ (1 << stage)) for i in range(sectors)])
        groups //= 2
        stage += 1
        if groups == 1:
            return keep, got, extra
        send, keep, extra = combine(groups, stage, pd, keep, got, extra)


def second_kernel(
    bounds, groups, scale,
    left_own, right_own, *rest
):
    n = len(bounds)
    left_got, right_got = rest[:n], rest[n : 2 * n]
    (m, coef, routes, onsite, sizes, keep_in, got, corr_in, squares_in,
     image_out, resid_out, send, keep, sq_out, buf_l, buf_r, acc, sems) = rest[2 * n :]
    pd, b = m.shape[0], m.shape[1]
    section = lax.axis_index("section")
    at_start = section == 0
    at_end = section == lax.axis_size("section") - 1
    for i, (start, count) in enumerate(bounds):
        dst = pl.ds(start, count)
        select_copy(at_start, left_own, left_got[i], buf_l.at[:, dst], sems.at[0, i], start, count, 0)
        select_copy(at_end, right_own, right_got[i], buf_r.at[:, dst], sems.at[1, i], start, count, 0)
    acc[...] = jnp.zeros_like(acc)
    squares = squares_in[0:1, 0:1]
    corr = corr_in[0:1, 0:1] + from_terms(got[pl.ds(pd * b, EXTRA)])[:, 0:1]
    ritz = corr / (squares + epsilon)
    sums = jnp.zeros((b, b), f32)
    for k in range(pd):
        g = m[k].astype(f32)
        summed = keep_in[k] + got[pl.ds(k * b, b)].astype(f32) + onsite[0, k] * g
        image = jnp.where(live_of(sizes[k], (b, b)), summed, 0.0)
        image_out[0, k] = image.astype(bf16)
        resid = image - ritz * g
        resid_out[k] = resid.astype(bf16)
        sums += resid * resid
    total = total_of(sums)
    sq_out[...] = jnp.broadcast_to(total, sq_out.shape)
    for i, (start, count) in enumerate(bounds):
        dst = pl.ds(start, count)
        wait_copy(left_got[i], buf_l.at[:, dst], sems.at[0, i], 0, count)
        wait_copy(right_got[i], buf_r.at[:, dst], sems.at[1, i], 0, count)
        unit = 3 if count % 3 == 0 else (5 if count % 5 == 0 else (2 if count % 2 == 0 else 1))
        for k in range(pd):
            mk = resid_out[k]

            def step(s, carry):
                at = start + s * unit
                apply_block(buf_l, buf_r, at, at, unit, mk, k, acc, coef, routes, scale)
                return carry

            lax.fori_loop(0, count // unit, step, 0)
    me = lax.axis_index("sector")
    split_halves(acc, groups, pd, b, lax.rem(me, 2), send, keep, total)


def second_apply(bounds, groups, channels, left_own, right_own, lefts, rights, m, coef, routes, onsite, sizes, keep, got, corr, squares):
    pd, b, _ = m.shape
    n = len(bounds)
    block = jax.ShapeDtypeStruct((1, pd, b, b), bf16)
    buf = pltpu.VMEM((pd, channels, b, b), bf16)
    return call(
        functools.partial(second_kernel, bounds, groups, channels ** (-0.5)),
        [block, jax.ShapeDtypeStruct((pd, b, b), bf16)]
        + exchange_shapes(groups, pd, b)
        + [jax.ShapeDtypeStruct((8, 128), f32)],
        [HB] * (2 + 2 * n) + [VM, SM, SM, SM, SM, VM, VM, VM, VM],
        [buf, buf, pltpu.VMEM((groups * pd, b, b), f32), pltpu.SemaphoreType.DMA((2, n))],
        flops=4 * pd * channels * b**3,
        moved=4 * pd * channels * b * b,
    )(left_own, right_own, *lefts, *rights, m, coef, routes, onsite, sizes, keep, got, corr, squares)


def final_kernel(resid, onsite, sizes, keep, got, sq_in, squares_in, out):
    pd, b = resid.shape[0], resid.shape[1]
    sq = sq_in[0:1, 0:1] + from_terms(got[pl.ds(pd * b, EXTRA)])[:, 0:1]
    alpha = jnp.sqrt(squares_in[0:1, 0:1] / (sq + epsilon))
    for k in range(pd):
        summed = keep[k] + got[pl.ds(k * b, b)].astype(f32) + onsite[0, k] * resid[k].astype(f32)
        out[0, k] = jnp.where(live_of(sizes[k], (b, b)), alpha * summed, 0.0).astype(bf16)


def final(resid, onsite, sizes, keep, got, sq, squares):
    pd, b, _ = resid.shape
    return call(
        final_kernel,
        [jax.ShapeDtypeStruct((1, pd, b, b), bf16)],
        [VM, SM, SM, VM, VM, VM, VM],
        moved=8 * pd * b * b,
    )(resid, onsite, sizes, keep, got, sq, squares)[0]


def gather_waves(sectors, m):
    me = lax.axis_index("sector")
    held = m[None]
    for stage in range(sectors.bit_length() - 1):
        step = 1 << stage
        other = lax.ppermute(held, "sector", [(i, i ^ step) for i in range(sectors)])
        mine_low = (me & step) == 0
        low = jnp.where(mine_low, held, other)
        high = jnp.where(mine_low, other, held)
        held = jnp.concatenate([low, high], axis=0)
    return held.reshape((-1,) + m.shape[1:])


def body(
    env_left, env_right, edge_left, edge_right, wave_blocks, mpo_coef, onsite, routes, sector_sizes
):
    channels = env_left.shape[2]
    sections = lax.axis_size("section")
    sectors = lax.axis_size("sector")
    pd = wave_blocks.shape[1]
    sizes = chunk_sizes(channels)
    bounds = []
    at = 0
    for c in sizes:
        bounds.append((at, c))
        at += c
    up = [(i, i + 1) for i in range(sections - 1)]
    down = [(i + 1, i) for i in range(sections - 1)]
    lefts, rights = [], []
    for start, count in bounds:
        gl, gr = grow(env_left, env_right, edge_left, edge_right, start, count)
        lefts.append(lax.ppermute(gl, "section", up))
        rights.append(lax.ppermute(gr, "section", down))
    m = mask_wave(wave_blocks, sector_sizes)
    gathered = gather_waves(sectors, m)
    acc = None
    for i, chunk in enumerate(bounds):
        is_last = i == len(bounds) - 1
        res = first_apply(
            chunk, i == 0, is_last, sectors, channels,
            (env_left, env_right, lefts[i], rights[i], m, mpo_coef, routes), acc, (gathered, onsite),
        )
        acc = res[0]
    send, keep, squares, corr = res
    keep, got, corr = exchange(sectors, pd, send, keep, corr)
    image1, resid, send, keep, sq = second_apply(
        bounds, sectors, channels, env_left, env_right, lefts, rights, m, mpo_coef, routes, onsite,
        sector_sizes, keep, got, corr, squares,
    )
    keep, got, sq = exchange(sectors, pd, send, keep, sq)
    image2 = final(resid, onsite, sector_sizes, keep, got, sq, squares)
    return (image1, image2)


def solution(mesh):
    in_specs = (
        P(("groups", "section"), "sector", None, None, None),
        P(("groups", "section"), "sector", None, None, None),
        P(("groups", "section"), "sector", None, None),
        P(("groups", "section"), "sector", None, None),
        P(("groups", "section"), "sector", None, None),
        P(("groups", "section"), "sector", None),
        P(("groups", "section"), "sector"),
        P(("groups", "section"), "sector", None),
        P(("groups", "sector")),
    )
    out_specs = (
        P(("groups", "section"), "sector", None, None),
        P(("groups", "section"), "sector", None, None),
    )
    return jax.shard_map(body, mesh=mesh, in_specs=in_specs, out_specs=out_specs, check_vma=False)
```

time: 189 us -> 103 us (0.54)
  waiting for transfers between devices: 111 us -> 20.7 us
  Pallas kernels: 0 us -> 45 us
  matrix products: 32.9 us -> 0 us
  between operations: 16.8 us -> 0.92 us
  starting transfers between devices: 8.33 us -> 22.4 us
  blocking collectives: 12.9 us -> 0 us
  local copies, waits for them, and re-layouts: 2.22 us -> 10.1 us
  other arithmetic: 4.59 us -> 2.52 us
    psum x2 -> x0, waiting for transfers between devices: 70.2 us -> none  [apply_hamiltonian(): lax.psum(jnp.einsum('kwj,kwab->jab', selector, contrib, precision=lax.Pre...]
    pallas_call x0 -> x11, Pallas kernels: none -> 45 us  [the longest x3 21.1 us: grow(): call(functools.partial(grow_kernel, start, count), [block, block], [HB, H...]
    dot_general x6 -> x0, matrix products: 32.9 us -> none  [the longest x2 14.3 us: apply_hamiltonian(): jnp.einsum('kwj,kwab->jab', selector, contrib, precision=lax.Precision.HI...]
    ppermute x2 -> x12, waiting for transfers between devices: 40.6 us -> 20.7 us  [the longest x3 11.8 us: body(): lefts.append(lax.ppermute(gl, 'section', up))]
    ppermute x2 -> x12, starting transfers between devices: 8.25 us -> 22.4 us  [the longest x3 13.7 us: body(): lefts.append(lax.ppermute(gl, 'section', up))]
    psum x2 -> x0, blocking collectives: 12.9 us -> none  [the longest x1 6.54 us: body(): resid_sq = lax.psum(jnp.sum(resid * resid), 'sector')]
    unnamed x18 -> x38, local copies, waits for them, and re-layouts: 2.08 us -> 10.1 us
    reduce_sum x2 -> x0, other arithmetic: 2.81 us -> none  [the longest x1 1.98 us: body(): jnp.sum(masked_wave * image1)]
  transfers between devices with their start and end apart: 4 -> 12, of which waited for: 4 -> 6; matrix products, arithmetic and copies ran while one was open for 2% -> 2% of each run, Pallas kernels for 0% -> 16%
where the time goes in v1:
time: 103 us; the launch traced here: 102 us
  Pallas kernels  45 us (44%)
  starting transfers between devices  22.4 us (22%)
  waiting for transfers between devices  20.7 us (20%)
  local copies, waits for them, and re-layouts  10.1 us (10%)
  other arithmetic  2.52 us (2%)
    pallas_call x3, Pallas kernels, grow(): call(functools.partial(grow_kernel, start, count), [block, block], [HB, H...  21.1 us
    ppermute x3, starting transfers between devices, body(): lefts.append(lax.ppermute(gl, 'section', up))  13.7 us
    pallas_call x3, Pallas kernels, first_apply(): call(functools.partial(first_kernel, chunk, is_first, is_last, groups, ch...  11.9 us
    ppermute x3, waiting for transfers between devices, body(): lefts.append(lax.ppermute(gl, 'section', up))  11.8 us
    unnamed x38, local copies, waits for them, and re-layouts  10.1 us
    pallas_call x1, Pallas kernels, second_apply(): call(functools.partial(second_kernel, bounds, groups, channels ** (-0.5))...  10 us
    ppermute x4, waiting for transfers between devices, exchange(): lax.ppermute(send, 'sector', [(i, i ^ 1 << stage) for i in range(sectors)])  8.3 us
    ppermute x3, starting transfers between devices, body(): rights.append(lax.ppermute(gr, 'section', down))  3.85 us
  transfers between devices with their start and end apart: 12, of which 6 were waited for; matrix products, arithmetic and copies ran while one was open for 2% of the time, Pallas kernels for 16%

profile of v1, /device:TPU:0, one launch (start us, length us, event | category | flops | bytes accessed | tf_op | source)
XLA Modules:
  0.0 101.7 jit_solution(15389906734858808930)
XLA Ops:
  0.6 1.5 %copy-done = bf16[1,2,30,128,128]{4,3,2,1,0:T(8,128)(2,1)S(1)} copy-done((bf16[1,2,30,128,128]{4,3,2,1,0:T(8,128)(2,1)S(1)}, bf16[1,2,30,128,128]{4,3,2,1,0:T(8,128)(2,1)}, u32[]{:S(2)}) %copy-start) | copy-done | bytes 1966104
  2.2 1.5 %copy-done.2 = bf16[1,2,30,128,128]{4,3,2,1,0:T(8,128)(2,1)S(1)} copy-done((bf16[1,2,30,128,128]{4,3,2,1,0:T(8,128)(2,1)S(1)}, bf16[1,2,30,128,128]{4,3,2,1,0:T(8,128)(2,1)}, u32[]{:S(2)}) %copy-start.2) | copy-done | bytes 1966104
  3.7 0.8 copy-done.6
  4.6 0.8 copy-done.8
  5.4 15.2 %shard_map.105 = (bf16[2,22,128,128]{3,2,1,0:T(8,128)(2,1)}, bf16[2,22,128,128]{3,2,1,0:T(8,128)(2,1)}) custom-call(bf16[1,2,30,128,128]{4,3,2,1,0:T(8,128)(2,1)S(1)} %copy-done, bf16[1,2,30,128,128]{4,3,2,1,0:T(8,128)(2,1)S(1)} %copy-done.2, bf16[1,2,128,128]{3,2,1,0:T(8,128)(2,1)S(1)} %copy-done.6, bf16[1,2,128,128]{3,2,1,0:T(8,128)(2,1)S(1)} %copy-done.8), custom_call_target="tpu_custom_call" | custom-call | flops 738197504 | bytes 5767168 | tf_op jit(solution)/shard_map/pallas_call | solution.py:78
  20.7 5.0 %collective-permute-start.1 = (bf16[2,22,128,128]{3,2,1,0:T(8,128)(2,1)}, bf16[2,22,128,128]{3,2,1,0:T(8,128)(2,1)S(1)}, u32[]{:S(2)}, u32[]{:S(2)}) collective-permute-start(bf16[2,22,128,128]{3,2,1,0:T(8,128)(2,1)} %get-tuple-element.24), channel_id=1, source_target_pairs={{0,4},{4,8},{8,12},{1,5},{5,9},{9,13},{2,6},{6,10},{10,14},{3,7},{... | collective-permute-start | bytes 4325384 | tf_op jit(solution)/shard_map/ppermute | solution.py:392
  25.7 1.3 %collective-permute-start.4 = (bf16[2,22,128,128]{3,2,1,0:T(8,128)(2,1)}, bf16[2,22,128,128]{3,2,1,0:T(8,128)(2,1)}, u32[]{:S(2)}, u32[]{:S(2)}) collective-permute-start(bf16[2,22,128,128]{3,2,1,0:T(8,128)(2,1)} %get-tuple-element.27), channel_id=1, source_target_pairs={{4,0},{8,4},{12,8},{5,1},{9,5},{13,9},{6,2},{10,6},{14,10},{7,3},{... | collective-permute-start | bytes 4325384 | tf_op jit(solution)/shard_map/ppermute | solution.py:393
  27.7 1.9 %shard_map.104 = (bf16[2,3,128,128]{3,2,1,0:T(8,128)(2,1)}, bf16[2,3,128,128]{3,2,1,0:T(8,128)(2,1)S(1)}) custom-call(bf16[1,2,30,128,128]{4,3,2,1,0:T(8,128)(2,1)S(1)} %copy-done.1, bf16[1,2,30,128,128]{4,3,2,1,0:T(8,128)(2,1)S(1)} %copy-done.2, bf16[1,2,128,128]{3,2,1,0:T(8,128)(2,1)S(1)} %copy-done.6, bf16[1,2,128,128]{3,2,1,0:T(8,128)(2,1)S(1)} %copy-done.8), custom_call_target="tpu_custom_call" | custom-call | flops 100663296 | bytes 786432 | tf_op jit(solution)/shard_map/pallas_call | solution.py:78
  30.3 5.2 %collective-permute-start = (bf16[2,3,128,128]{3,2,1,0:T(8,128)(2,1)}, bf16[2,3,128,128]{3,2,1,0:T(8,128)(2,1)}, u32[]{:S(2)}, u32[]{:S(2)}) collective-permute-start(bf16[2,3,128,128]{3,2,1,0:T(8,128)(2,1)} %get-tuple-element.23), channel_id=1, source_target_pairs={{0,4},{4,8},{8,12},{1,5},{5,9},{9,13},{2,6},{6,10},{10,14},{3,7},{... | collective-permute-start | bytes 589832 | tf_op jit(solution)/shard_map/ppermute | solution.py:392
  35.5 0.9 broadcast_select_fusion.3
  37.0 1.5 %collective-permute-start.7 = (bf16[2,2,128,128]{3,2,1,0:T(8,128)(2,1)}, bf16[2,2,128,128]{3,2,1,0:T(8,128)(2,1)}, u32[]{:S(2)}, u32[]{:S(2)}) collective-permute-start(bf16[2,2,128,128]{3,2,1,0:T(8,128)(2,1)} %pad_maximum_fusion.1), channel_id=1, source_target_pairs={{0,2},{1,3},{2,0},{3,1},{4,6},{5,7},{6,4},{7,5},{8,10},{9,11},{10,... | collective-permute-start | bytes 393224 | tf_op jit(solution)/shard_map/ppermute | solution.py:366
  38.5 1.5 %copy-done.3 = bf16[1,2,30,128,128]{4,3,2,1,0:T(8,128)(2,1)S(1)} copy-done((bf16[1,2,30,128,128]{4,3,2,1,0:T(8,128)(2,1)S(1)}, bf16[1,2,30,128,128]{4,3,2,1,0:T(8,128)(2,1)}, u32[]{:S(2)}) %copy-start.3) | copy-done | bytes 1966104
  40.1 0.8 copy-done.9
  40.9 3.9 %shard_map.106 = (bf16[2,5,128,128]{3,2,1,0:T(8,128)(2,1)}, bf16[2,5,128,128]{3,2,1,0:T(8,128)(2,1)S(1)}) custom-call(bf16[1,2,30,128,128]{4,3,2,1,0:T(8,128)(2,1)S(1)} %copy-done.1, bf16[1,2,30,128,128]{4,3,2,1,0:T(8,128)(2,1)S(1)} %copy-done.3, bf16[1,2,128,128]{3,2,1,0:T(8,128)(2,1)S(1)} %copy-done.7, bf16[1,2,128,128]{3,2,1,0:T(8,128)(2,1)S(1)} %copy-done.9), custom_call_target="tpu_custom_call" | custom-call | flops 167772160 | bytes 1310720 | tf_op jit(solution)/shard_map/pallas_call | solution.py:78
  44.9 0.7 copy-done.15
  45.6 3.5 %collective-permute-start.2 = (bf16[2,5,128,128]{3,2,1,0:T(8,128)(2,1)}, bf16[2,5,128,128]{3,2,1,0:T(8,128)(2,1)}, u32[]{:S(2)}, u32[]{:S(2)}) collective-permute-start(bf16[2,5,128,128]{3,2,1,0:T(8,128)(2,1)} %get-tuple-element.25), channel_id=1, source_target_pairs={{0,4},{4,8},{8,12},{1,5},{5,9},{9,13},{2,6},{6,10},{10,14},{3,7},{... | collective-permute-start | bytes 983048 | tf_op jit(solution)/shard_map/ppermute | solution.py:392
  49.1 1.3 %collective-permute-start.3 = (bf16[2,3,128,128]{3,2,1,0:T(8,128)(2,1)}, bf16[2,3,128,128]{3,2,1,0:T(8,128)(2,1)S(1)}, u32[]{:S(2)}, u32[]{:S(2)}) collective-permute-start(bf16[2,3,128,128]{3,2,1,0:T(8,128)(2,1)} %copy-done.16), channel_id=1, source_target_pairs={{4,0},{8,4},{12,8},{5,1},{9,5},{13,9},{6,2},{10,6},{14,10},{7,3},{... | collective-permute-start | bytes 589832 | tf_op jit(solution)/shard_map/ppermute | solution.py:393
  50.3 11.8 %collective-permute-done.left_got.rest_0_ = bf16[2,3,128,128]{3,2,1,0:T(8,128)(2,1)} collective-permute-done((bf16[2,3,128,128]{3,2,1,0:T(8,128)(2,1)}, bf16[2,3,128,128]{3,2,1,0:T(8,128)(2,1)}, u32[]{:S(2)}, u32[]{:S(2)}) %collective-permute-start) | collective-permute-done | bytes 196640 | tf_op jit(solution)/shard_map/ppermute | solution.py:392
  62.1 1.3 %collective-permute-start.5 = (bf16[2,5,128,128]{3,2,1,0:T(8,128)(2,1)}, bf16[2,5,128,128]{3,2,1,0:T(8,128)(2,1)S(1)}, u32[]{:S(2)}, u32[]{:S(2)}) collective-permute-start(bf16[2,5,128,128]{3,2,1,0:T(8,128)(2,1)} %copy-done.15), channel_id=1, source_target_pairs={{4,0},{8,4},{12,8},{5,1},{9,5},{13,9},{6,2},{10,6},{14,10},{7,3},{... | collective-permute-start | bytes 983048 | tf_op jit(solution)/shard_map/ppermute | solution.py:393
  63.4 1.0 broadcast_select_fusion.1
  65.1 1.5 %copy-done.4 = bf16[1,2,30,128,128]{4,3,2,1,0:T(8,128)(2,1)S(1)} copy-done((bf16[1,2,30,128,128]{4,3,2,1,0:T(8,128)(2,1)S(1)}, bf16[1,2,30,128,128]{4,3,2,1,0:T(8,128)(2,1)}, u32[]{:S(2)}) %copy-start.4) | copy-done | bytes 1966104
  66.6 1.6 %shard_map.108.rest_0_ = f32[8,128,128]{2,1,0:T(8,128)S(1)} custom-call(bf16[1,2,30,128,128]{4,3,2,1,0:T(8,128)(2,1)S(1)} %copy-done.1, bf16[1,2,30,128,128]{4,3,2,1,0:T(8,128)(2,1)S(1)} %copy-done.4, bf16[2,3,128,128]{3,2,1,0:T(8,128)(2,1)} %collective-permute-done.left_got.rest_0_, bf16[2,3,128,128]{3,2,1,0:T(8,128)(2,1)S(1)} %collective-permute-done.3.right_got.rest_3_, ...), custom_call_target="tpu_custom_call" | custom-call | flops 50331648 | bytes 393216 | tf_op jit(solution)/shard_map/pallas_call | solution.py:223
  68.3 8.4 %shard_map.109.rest_0_ = f32[8,128,128]{2,1,0:T(8,128)S(1)} custom-call(bf16[1,2,30,128,128]{4,3,2,1,0:T(8,128)(2,1)S(1)} %copy-done.1, bf16[1,2,30,128,128]{4,3,2,1,0:T(8,128)(2,1)S(1)} %copy-done.4, bf16[2,22,128,128]{3,2,1,0:T(8,128)(2,1)S(1)} %collective-permute-done.1.left_got.rest_1_, ...), custom_call_target="tpu_custom_call" | custom-call | flops 369098752 | bytes 2883584 | tf_op jit(solution)/shard_map/pallas_call | solution.py:223
  76.8 1.9 %shard_map.110 = (bf16[528,128]{1,0:T(8,128)(2,1)S(1)}, f32[4,128,128]{2,1,0:T(8,128)S(1)}, f32[8,128]{1,0:T(8,128)S(1)}, f32[8,128]{1,0:T(8,128)S(1)}) custom-call(bf16[1,2,30,128,128]{4,3,2,1,0:T(8,128)(2,1)S(1)} %copy-done.1, bf16[1,2,30,128,128]{4,3,2,1,0:T(8,128)(2,1)S(1)} %copy-done.4, ...), custom_call_target="tpu_custom_call" | custom-call | flops 83886080 | bytes 655360 | tf_op jit(solution)/shard_map/pallas_call | solution.py:223
  78.7 1.3 %collective-permute-done.8.got = bf16[528,128]{1,0:T(8,128)(2,1)S(1)} collective-permute-done((bf16[528,128]{1,0:T(8,128)(2,1)S(1)}, bf16[528,128]{1,0:T(8,128)(2,1)S(1)}, u32[]{:S(2)}, u32[]{:S(2)}) %collective-permute-start.8) | collective-permute-done | bytes 135200 | tf_op jit(solution)/shard_map/ppermute | solution.py:268
  80.1 1.6 %collective-permute-start.9 = (bf16[272,128]{1,0:T(8,128)(2,1)S(1)}, bf16[272,128]{1,0:T(8,128)(2,1)S(1)}, u32[]{:S(2)}, u32[]{:S(2)}) collective-permute-start(bf16[272,128]{1,0:T(8,128)(2,1)S(1)} %get-tuple-element.33), channel_id=1, source_target_pairs={{0,2},{1,3},{2,0},{3,1},{4,6},{5,7},{6,4},{7,5},{8,10},{9,11},{10,... | collective-permute-start | bytes 208904 | tf_op jit(solution)/shard_map/ppermute | solution.py:268
  81.7 2.8 %collective-permute-done.9.rest_12_ = bf16[272,128]{1,0:T(8,128)(2,1)S(1)} collective-permute-done((bf16[272,128]{1,0:T(8,128)(2,1)S(1)}, bf16[272,128]{1,0:T(8,128)(2,1)S(1)}, u32[]{:S(2)}, u32[]{:S(2)}) %collective-permute-start.9) | collective-permute-done | bytes 69664 | tf_op jit(solution)/shard_map/ppermute | solution.py:268
  84.5 10.0 %shard_map.112 = (bf16[1,2,128,128]{3,2,1,0:T(8,128)(2,1)}, bf16[2,128,128]{2,1,0:T(8,128)(2,1)S(1)}, bf16[528,128]{1,0:T(8,128)(2,1)S(1)}, f32[4,128,128]{2,1,0:T(8,128)S(1)}, f32[8,128]{1,0:T(8,128)S(1)}) custom-call(bf16[1,2,30,128,128]{4,3,2,1,0:T(8,128)(2,1)S(1)} %copy-done.1, bf16[1,2,30,128,128]{4,3,2,1,0:T(8,128)(2,1)S(1)} %copy-done.5, ...), custom_call_target="tpu_custom_call" | custom-call | flops 503316480 | bytes 3932160 | tf_op jit(solution)/shard_map/pallas_call | solution.py:330
  94.6 1.3 %collective-permute-done.10.got = bf16[528,128]{1,0:T(8,128)(2,1)S(1)} collective-permute-done((bf16[528,128]{1,0:T(8,128)(2,1)S(1)}, bf16[528,128]{1,0:T(8,128)(2,1)S(1)}, u32[]{:S(2)}, u32[]{:S(2)}) %collective-permute-start.10) | collective-permute-done | bytes 135200 | tf_op jit(solution)/shard_map/ppermute | solution.py:268
  96.0 1.6 %collective-permute-start.11 = (bf16[272,128]{1,0:T(8,128)(2,1)S(1)}, bf16[272,128]{1,0:T(8,128)(2,1)S(1)}, u32[]{:S(2)}, u32[]{:S(2)}) collective-permute-start(bf16[272,128]{1,0:T(8,128)(2,1)S(1)} %get-tuple-element.42), channel_id=1, source_target_pairs={{0,2},{1,3},{2,0},{3,1},{4,6},{5,7},{6,4},{7,5},{8,10},{9,11},{10,... | collective-permute-start | bytes 208904 | tf_op jit(solution)/shard_map/ppermute | solution.py:268
  97.6 2.8 %collective-permute-done.11.got = bf16[272,128]{1,0:T(8,128)(2,1)S(1)} collective-permute-done((bf16[272,128]{1,0:T(8,128)(2,1)S(1)}, bf16[272,128]{1,0:T(8,128)(2,1)S(1)}, u32[]{:S(2)}, u32[]{:S(2)}) %collective-permute-start.11) | collective-permute-done | bytes 69664 | tf_op jit(solution)/shard_map/ppermute | solution.py:268
  100.4 1.3 %shard_map.114 = bf16[1,2,128,128]{3,2,1,0:T(8,128)(2,1)} custom-call(bf16[2,128,128]{2,1,0:T(8,128)(2,1)S(1)} %get-tuple-element.37.resid, f32[1,2]{1,0:T(1,128)S(1)} %copy-done.14, s32[2]{0:T(128)S(1)} %copy-done.13, f32[2,128,128]{2,1,0:T(8,128)S(1)} %get-tuple-element.41.keep, bf16[272,128]{1,0:T(8,128)(2,1)S(1)} %collective-permute-done.11.got, ...), custom_call_target="tpu_custom_call" | custom-call | bytes 262144 | tf_op jit(solution)/shard_map/pallas_call | solution.py:353
  (45 shorter events, 3.0 us)
Async XLA Ops:
  0.6 1.5 %copy-start = (bf16[1,2,30,128,128]{4,3,2,1,0:T(8,128)(2,1)S(1)}, bf16[1,2,30,128,128]{4,3,2,1,0:T(8,128)(2,1)}, u32[]{:S(2)}) copy-start(bf16[1,2,30,128,128]{4,3,2,1,0:T(8,128)(2,1)} %left_own.7) | copy-start | bytes 5898244
  2.2 1.5 %copy-start.2 = (bf16[1,2,30,128,128]{4,3,2,1,0:T(8,128)(2,1)S(1)}, bf16[1,2,30,128,128]{4,3,2,1,0:T(8,128)(2,1)}, u32[]{:S(2)}) copy-start(bf16[1,2,30,128,128]{4,3,2,1,0:T(8,128)(2,1)} %right_own.7) | copy-start | bytes 5898244
  3.7 0.8 copy-start.6
  4.6 0.8 copy-start.8
  5.4 21.6 %copy-start.10 = (bf16[1,2,128,128]{3,2,1,0:T(8,128)(2,1)S(1)}, bf16[1,2,128,128]{3,2,1,0:T(8,128)(2,1)}, u32[]{:S(2)}) copy-start(bf16[1,2,128,128]{3,2,1,0:T(8,128)(2,1)} %wave.1) | copy-start | bytes 196612
  5.4 21.6 %copy-start.13 = (s32[2]{0:T(128)S(1)}, s32[2]{0:T(128)}, u32[]{:S(2)}) copy-start(s32[2]{0:T(128)} %sizes.3) | copy-start | bytes 28
  5.4 22.3 %copy-start.1 = (bf16[1,2,30,128,128]{4,3,2,1,0:T(8,128)(2,1)S(1)}, bf16[1,2,30,128,128]{4,3,2,1,0:T(8,128)(2,1)}, u32[]{:S(2)}) copy-start(bf16[1,2,30,128,128]{4,3,2,1,0:T(8,128)(2,1)} %left_own.7) | copy-start | bytes 5898244
  20.7 47.6 %collective-permute-start.1 = (bf16[2,22,128,128]{3,2,1,0:T(8,128)(2,1)}, bf16[2,22,128,128]{3,2,1,0:T(8,128)(2,1)S(1)}, u32[]{:S(2)}, u32[]{:S(2)}) collective-permute-start(bf16[2,22,128,128]{3,2,1,0:T(8,128)(2,1)} %get-tuple-element.24), channel_id=1, source_target_pairs={{0,4},{4,8},{8,12},{1,5},{5,9},{9,13},{2,6},{6,10},{10,14},{3,7},{... | collective-permute-start | bytes 4325384 | tf_op jit(solution)/shard_map/ppermute | solution.py:392
  25.7 42.6 %collective-permute-start.4 = (bf16[2,22,128,128]{3,2,1,0:T(8,128)(2,1)}, bf16[2,22,128,128]{3,2,1,0:T(8,128)(2,1)}, u32[]{:S(2)}, u32[]{:S(2)}) collective-permute-start(bf16[2,22,128,128]{3,2,1,0:T(8,128)(2,1)} %get-tuple-element.27), channel_id=1, source_target_pairs={{4,0},{8,4},{12,8},{5,1},{9,5},{13,9},{6,2},{10,6},{14,10},{7,3},{... | collective-permute-start | bytes 4325384 | tf_op jit(solution)/shard_map/ppermute | solution.py:393
  27.6 10.9 %copy-start.7 = (bf16[1,2,128,128]{3,2,1,0:T(8,128)(2,1)S(1)}, bf16[1,2,128,128]{3,2,1,0:T(8,128)(2,1)}, u32[]{:S(2)}) copy-start(bf16[1,2,128,128]{3,2,1,0:T(8,128)(2,1)} %edge_l.5) | copy-start | bytes 196612
  27.6 7.9 %collective-permute-start.6 = (bf16[1,2,128,128]{3,2,1,0:T(8,128)(2,1)S(1)}, bf16[1,2,128,128]{3,2,1,0:T(8,128)(2,1)}, u32[]{:S(2)}, u32[]{:S(2)}) collective-permute-start(bf16[1,2,128,128]{3,2,1,0:T(8,128)(2,1)S(1)} %bitcast.4), channel_id=1, source_target_pairs={{0,1},{1,0},{2,3},{3,2},{4,5},{5,4},{6,7},{7,6},{8,9},{9,8},{10,11... | collective-permute-start | bytes 196616 | tf_op jit(solution)/shard_map/ppermute | solution.py:366
  29.6 0.7 copy-start.16
  30.3 31.9 %collective-permute-start = (bf16[2,3,128,128]{3,2,1,0:T(8,128)(2,1)}, bf16[2,3,128,128]{3,2,1,0:T(8,128)(2,1)}, u32[]{:S(2)}, u32[]{:S(2)}) collective-permute-start(bf16[2,3,128,128]{3,2,1,0:T(8,128)(2,1)} %get-tuple-element.23), channel_id=1, source_target_pairs={{0,4},{4,8},{8,12},{1,5},{5,9},{9,13},{2,6},{6,10},{10,14},{3,7},{... | collective-permute-start | bytes 589832 | tf_op jit(solution)/shard_map/ppermute | solution.py:392
  36.3 0.7 copy-start.17
  36.3 0.7 copy-start.18
  37.0 12.0 %collective-permute-start.7 = (bf16[2,2,128,128]{3,2,1,0:T(8,128)(2,1)}, bf16[2,2,128,128]{3,2,1,0:T(8,128)(2,1)}, u32[]{:S(2)}, u32[]{:S(2)}) collective-permute-start(bf16[2,2,128,128]{3,2,1,0:T(8,128)(2,1)} %pad_maximum_fusion.1), channel_id=1, source_target_pairs={{0,2},{1,3},{2,0},{3,1},{4,6},{5,7},{6,4},{7,5},{8,10},{9,11},{10,... | collective-permute-start | bytes 393224 | tf_op jit(solution)/shard_map/ppermute | solution.py:366
  38.5 1.5 %copy-start.3 = (bf16[1,2,30,128,128]{4,3,2,1,0:T(8,128)(2,1)S(1)}, bf16[1,2,30,128,128]{4,3,2,1,0:T(8,128)(2,1)}, u32[]{:S(2)}) copy-start(bf16[1,2,30,128,128]{4,3,2,1,0:T(8,128)(2,1)} %right_own.7) | copy-start | bytes 5898244
  40.1 0.8 copy-start.9
  40.9 24.1 %copy-start.11 = (f32[1,2,30]{2,1,0:T(2,128)S(1)}, f32[1,2,30]{2,1,0:T(2,128)}, u32[]{:S(2)}) copy-start(f32[1,2,30]{2,1,0:T(2,128)} %rest_7_.1) | copy-start | bytes 724
  40.9 24.1 %copy-start.12 = (s32[1,2,30]{2,1,0:T(2,128)S(1)}, s32[1,2,30]{2,1,0:T(2,128)}, u32[]{:S(2)}) copy-start(s32[1,2,30]{2,1,0:T(2,128)} %rest_8_.1) | copy-start | bytes 724
  44.9 0.7 copy-start.15
  45.6 31.1 %collective-permute-start.2 = (bf16[2,5,128,128]{3,2,1,0:T(8,128)(2,1)}, bf16[2,5,128,128]{3,2,1,0:T(8,128)(2,1)}, u32[]{:S(2)}, u32[]{:S(2)}) collective-permute-start(bf16[2,5,128,128]{3,2,1,0:T(8,128)(2,1)} %get-tuple-element.25), channel_id=1, source_target_pairs={{0,4},{4,8},{8,12},{1,5},{5,9},{9,13},{2,6},{6,10},{10,14},{3,7},{... | collective-permute-start | bytes 983048 | tf_op jit(solution)/shard_map/ppermute | solution.py:392
  49.1 16.0 %collective-permute-start.3 = (bf16[2,3,128,128]{3,2,1,0:T(8,128)(2,1)}, bf16[2,3,128,128]{3,2,1,0:T(8,128)(2,1)S(1)}, u32[]{:S(2)}, u32[]{:S(2)}) collective-permute-start(bf16[2,3,128,128]{3,2,1,0:T(8,128)(2,1)} %copy-done.16), channel_id=1, source_target_pairs={{4,0},{8,4},{12,8},{5,1},{9,5},{13,9},{6,2},{10,6},{14,10},{7,3},{... | collective-permute-start | bytes 589832 | tf_op jit(solution)/shard_map/ppermute | solution.py:393
  62.1 14.6 %collective-permute-start.5 = (bf16[2,5,128,128]{3,2,1,0:T(8,128)(2,1)}, bf16[2,5,128,128]{3,2,1,0:T(8,128)(2,1)S(1)}, u32[]{:S(2)}, u32[]{:S(2)}) collective-permute-start(bf16[2,5,128,128]{3,2,1,0:T(8,128)(2,1)} %copy-done.15), channel_id=1, source_target_pairs={{4,0},{8,4},{12,8},{5,1},{9,5},{13,9},{6,2},{10,6},{14,10},{7,3},{... | collective-permute-start | bytes 983048 | tf_op jit(solution)/shard_map/ppermute | solution.py:393
  65.1 1.5 %copy-start.4 = (bf16[1,2,30,128,128]{4,3,2,1,0:T(8,128)(2,1)S(1)}, bf16[1,2,30,128,128]{4,3,2,1,0:T(8,128)(2,1)}, u32[]{:S(2)}) copy-start(bf16[1,2,30,128,128]{4,3,2,1,0:T(8,128)(2,1)} %right_own.7) | copy-start | bytes 5898244
  68.2 8.5 %copy-start.14 = (f32[1,2]{1,0:T(1,128)S(1)}, f32[1,2]{1,0:T(1,128)}, u32[]{:S(2)}) copy-start(f32[1,2]{1,0:T(1,128)} %onsite.1) | copy-start | bytes 28
  76.8 7.8 %copy-start.5 = (bf16[1,2,30,128,128]{4,3,2,1,0:T(8,128)(2,1)S(1)}, bf16[1,2,30,128,128]{4,3,2,1,0:T(8,128)(2,1)}, u32[]{:S(2)}) copy-start(bf16[1,2,30,128,128]{4,3,2,1,0:T(8,128)(2,1)} %right_own.7) | copy-start | bytes 5898244
  78.6 1.4 %collective-permute-start.8 = (bf16[528,128]{1,0:T(8,128)(2,1)S(1)}, bf16[528,128]{1,0:T(8,128)(2,1)S(1)}, u32[]{:S(2)}, u32[]{:S(2)}) collective-permute-start(bf16[528,128]{1,0:T(8,128)(2,1)S(1)} %get-tuple-element.30), channel_id=1, source_target_pairs={{0,1},{1,0},{2,3},{3,2},{4,5},{5,4},{6,7},{7,6},{8,9},{9,8},{10,11... | collective-permute-start | bytes 405512 | tf_op jit(solution)/shard_map/ppermute | solution.py:268
  80.1 4.4 %collective-permute-start.9 = (bf16[272,128]{1,0:T(8,128)(2,1)S(1)}, bf16[272,128]{1,0:T(8,128)(2,1)S(1)}, u32[]{:S(2)}, u32[]{:S(2)}) collective-permute-start(bf16[272,128]{1,0:T(8,128)(2,1)S(1)} %get-tuple-element.33), channel_id=1, source_target_pairs={{0,2},{1,3},{2,0},{3,1},{4,6},{5,7},{6,4},{7,5},{8,10},{9,11},{10,... | collective-permute-start | bytes 208904 | tf_op jit(solution)/shard_map/ppermute | solution.py:268
  94.5 1.4 %collective-permute-start.10 = (bf16[528,128]{1,0:T(8,128)(2,1)S(1)}, bf16[528,128]{1,0:T(8,128)(2,1)S(1)}, u32[]{:S(2)}, u32[]{:S(2)}) collective-permute-start(bf16[528,128]{1,0:T(8,128)(2,1)S(1)} %get-tuple-element.39), channel_id=1, source_target_pairs={{0,1},{1,0},{2,3},{3,2},{4,5},{5,4},{6,7},{7,6},{8,9},{9,8},{10,11... | collective-permute-start | bytes 405512 | tf_op jit(solution)/shard_map/ppermute | solution.py:268
  96.0 4.4 %collective-permute-start.11 = (bf16[272,128]{1,0:T(8,128)(2,1)S(1)}, bf16[272,128]{1,0:T(8,128)(2,1)S(1)}, u32[]{:S(2)}, u32[]{:S(2)}) collective-permute-start(bf16[272,128]{1,0:T(8,128)(2,1)S(1)} %get-tuple-element.42), channel_id=1, source_target_pairs={{0,2},{1,3},{2,0},{3,1},{4,6},{5,7},{6,4},{7,5},{8,10},{9,11},{10,... | collective-permute-start | bytes 208904 | tf_op jit(solution)/shard_map/ppermute | solution.py:268

commit v2 on v1

v2 whole, which is shorter than its diff:
```python
import functools

import jax
import jax.numpy as jnp
from jax import lax
from jax.experimental import pallas as pl
from jax.experimental.pallas import tpu as pltpu
from jax.sharding import PartitionSpec as P

epsilon = 1e-06
VMEM_BYTES = 16 * 1024 * 1024
VMEM_LARGE = 56 * 1024 * 1024
EXTRA = 16

f32 = jnp.float32
bf16 = jnp.bfloat16

VM = pl.BlockSpec(memory_space=pltpu.VMEM)
SM = pl.BlockSpec(memory_space=pltpu.SMEM)
HB = pl.BlockSpec(memory_space=pltpu.HBM)


def call(kernel, outs, in_specs, scratch=(), aliases=None, flops=0, moved=0, out_specs=None, vmem=VMEM_BYTES):
    return pl.pallas_call(
        kernel,
        out_shape=outs,
        in_specs=in_specs,
        out_specs=[VM] * len(outs) if out_specs is None else out_specs,
        scratch_shapes=list(scratch),
        input_output_aliases=aliases or {},
        compiler_params=pltpu.CompilerParams(vmem_limit_bytes=vmem),
        cost_estimate=pl.CostEstimate(flops=flops, bytes_accessed=moved, transcendentals=0),
    )


def dot(a, b):
    return jnp.dot(a, b, preferred_element_type=f32)


def dot_t(a, b):
    return lax.dot_general(a, b, (((1,), (1,)), ((), ())), preferred_element_type=f32)


def chunk_sizes(channels):
    first, last = max(1, channels // 5), max(1, channels * 2 // 15)
    return [c for c in (first, channels - first - last, last) if c > 0]


def unit_of(count, most=11):
    return max(u for u in range(1, most + 1) if count % u == 0)


def grow_kernel(bounds, left_hbm, right_hbm, edge_l_hbm, edge_r_hbm, *rest):
    n = len(bounds)
    rest = rest[-6 * n - 6 :]
    token, rest = rest[0], rest[1:]
    outs, bufs, results = rest[: 2 * n], rest[2 * n : 4 * n], rest[4 * n : 6 * n]
    edge_l, edge_r, edge_sems, in_sems, out_sems = rest[6 * n :]
    pd, b = edge_l.shape[0], edge_l.shape[1]
    edges = [
        pltpu.make_async_copy(edge_l_hbm.at[0], edge_l, edge_sems.at[0]),
        pltpu.make_async_copy(edge_r_hbm.at[0], edge_r, edge_sems.at[1]),
    ]
    for c in edges:
        c.start()
    loads = {}
    for i, (start, count) in enumerate(bounds):
        for k in range(pd):
            for side, src in enumerate((left_hbm, right_hbm)):
                c = pltpu.make_async_copy(
                    src.at[0, k, pl.ds(start, count)], bufs[2 * i + side].at[k], in_sems.at[i, k, side]
                )
                c.start()
                loads[i, k, side] = c
    for c in edges:
        c.wait()
    sends = []
    for i, (start, count) in enumerate(bounds):
        unit = unit_of(count)
        buf_l, buf_r = bufs[2 * i], bufs[2 * i + 1]
        res_l, res_r = results[2 * i], results[2 * i + 1]
        for k in range(pd):
            e = edge_l[k]
            e_t = e.T
            f = edge_r[k]
            loads[i, k, 0].wait()
            loads[i, k, 1].wait()

            def step(s, carry):
                at = s * unit
                left = [dot(e_t, buf_l[k, at + u]).astype(bf16) for u in range(unit)]
                right = [dot(f, buf_r[k, at + u]).astype(bf16) for u in range(unit)]
                grown = dot(jnp.concatenate(left, axis=0), e).astype(bf16)
                res_l[k, pl.ds(at, unit)] = grown.reshape(unit, b, b)
                for u in range(unit):
                    res_r[k, at + u] = dot_t(f, right[u]).astype(bf16)
                return carry

            if count == unit:
                step(0, 0)
            else:
                lax.fori_loop(0, count // unit, step, 0)
            for side, res in enumerate((res_l, res_r)):
                c = pltpu.make_async_copy(res.at[k], outs[2 * i + side].at[k], out_sems.at[i, k, side])
                c.start()
                sends.append(c)
    token[...] = jnp.zeros_like(token)
    for c in sends:
        c.wait()


def grow(env_left, env_right, edge_left, edge_right, bounds, after, vmem):
    _, pd, _, b, _ = env_left.shape
    n = len(bounds)
    counts = [c for _, c in bounds for _ in range(2)]
    total = sum(c for _, c in bounds)
    blocks = [pltpu.VMEM((pd, c, b, b), bf16) for c in counts]
    edge = pltpu.VMEM((pd, b, b), bf16)
    res = call(
        functools.partial(grow_kernel, bounds),
        [jax.ShapeDtypeStruct((8, 128), f32)] + [jax.ShapeDtypeStruct((pd, c, b, b), bf16) for c in counts],
        [HB] * (4 + len(after)),
        blocks + blocks + [
            edge, edge, pltpu.SemaphoreType.DMA((2,)),
            pltpu.SemaphoreType.DMA((n, pd, 2)), pltpu.SemaphoreType.DMA((n, pd, 2)),
        ],
        flops=8 * pd * total * b**3,
        moved=8 * pd * total * b * b,
        out_specs=[VM] + [HB] * (2 * n),
        vmem=vmem,
    )(env_left, env_right, edge_left, edge_right, *after)
    return res[0], [(res[2 * i + 1], res[2 * i + 2]) for i in range(n)]


def gate_kernel(*refs):
    refs[-1][...] = jnp.zeros_like(refs[-1])


def gate(arrays, after):
    *held, token = call(
        gate_kernel,
        [jax.ShapeDtypeStruct(a.shape, a.dtype) for a in arrays] + [jax.ShapeDtypeStruct((8, 128), f32)],
        [HB] * (len(arrays) + len(after)),
        aliases={i: i for i in range(len(arrays))},
        out_specs=[HB] * len(arrays) + [VM],
        vmem=VMEM_LARGE,
    )(*arrays, *after)
    return held, token


def own_kernel(left_hbm, right_hbm, after, out_l, out_r, sem):
    section = lax.axis_index("section")
    at_start = section == 0
    at_end = section == lax.axis_size("section") - 1
    pd, channels = out_l.shape[0], out_l.shape[1]

    @pl.when(at_start)
    def _():
        c = pltpu.make_async_copy(left_hbm.at[0], out_l, sem)
        c.start()
        c.wait()

    @pl.when(jnp.logical_not(at_start))
    def _():
        out_l[...] = jnp.zeros_like(out_l)

    @pl.when(at_end)
    def _():
        c = pltpu.make_async_copy(right_hbm.at[0], out_r, sem)
        c.start()
        c.wait()
        for k in range(pd):

            def step(w, carry):
                out_r[k, w] = out_r[k, w].T
                return carry

            lax.fori_loop(0, channels, step, 0)

    @pl.when(jnp.logical_not(at_end))
    def _():
        out_r[...] = jnp.zeros_like(out_r)


def own_ends(env_left, env_right, after):
    _, pd, channels, b, _ = env_left.shape
    shape = jax.ShapeDtypeStruct((pd, channels, b, b), bf16)
    return call(
        own_kernel, [shape, shape], [HB, HB, HB], [pltpu.SemaphoreType.DMA],
        flops=pd * channels * b * b, moved=4 * pd * channels * b * b,
    )(env_left, env_right, after)


def live_of(size, shape):
    rows = lax.broadcasted_iota(jnp.int32, shape, 0) < size
    cols = lax.broadcasted_iota(jnp.int32, shape, 1) < size
    return rows & cols


def mask_kernel(wave, sizes, after, out):
    for k in range(wave.shape[1]):
        v = wave[0, k].astype(f32)
        out[k] = jnp.where(live_of(sizes[k], v.shape), v, 0.0).astype(bf16)


def mask_wave(wave, sizes, after):
    _, pd, b, _ = wave.shape
    return call(mask_kernel, [jax.ShapeDtypeStruct((pd, b, b), bf16)], [VM, SM, HB], moved=4 * pd * b * b)(wave, sizes, after)[0]


def apply_blocks(load, count, vectors, first, acc, coef, routes, scale, unit):
    pd, b = len(vectors), vectors[0].shape[0]

    def step(s, carry):
        at = s * unit
        loaded = [load(k, at, unit) for k in range(pd)]
        halves = [dot(loaded[k][0].reshape(unit * b, b), vectors[k]).astype(bf16) for k in range(pd)]
        for k in range(pd):
            for u in range(unit):
                contrib = dot(halves[k][u * b : (u + 1) * b], loaded[k][1][u])
                j = routes[0, k, first + at + u]
                acc[j] += contrib * (coef[0, k, first + at + u] * scale)
        return carry

    if count == unit:
        step(0, 0)
    else:
        lax.fori_loop(0, count // unit, step, 0)


def three_terms(x, rows):
    hi = x.astype(bf16).astype(f32)
    mid = (x - hi).astype(bf16).astype(f32)
    low = x - hi - mid
    place = lax.broadcasted_iota(jnp.int32, (EXTRA, 128), 0)
    return jnp.where(place == 0, hi, jnp.where(place == 1, mid, jnp.where(place == 2, low, 0.0))).astype(bf16)


def from_terms(rows):
    return jnp.sum(rows.astype(f32), axis=0, keepdims=True)


def total_of(x):
    return jnp.sum(jnp.sum(x, axis=0, keepdims=True), axis=1, keepdims=True)


def split_halves(acc, groups, pd, b, bit, send, keep, extra):
    for i in range(groups // 2):
        for q in range(pd):
            kept = acc[(2 * i + bit) * pd + q]
            sent = acc[(2 * i + 1 - bit) * pd + q]
            keep[i * pd + q] = kept
            send[pl.ds((i * pd + q) * b, b)] = sent.astype(bf16)
    send[pl.ds(groups // 2 * pd * b, EXTRA)] = three_terms(extra, EXTRA)


def first_kernel(
    chunk, is_first, is_last, groups, scale,
    own_l, own_r, got_l, got_r, m, coef, routes, *rest
):
    start, count = chunk
    rest = list(rest)
    acc_in = None if is_first else rest.pop(0)
    if is_last:
        onsite = rest.pop(0)
        pieces = []
        at = 1
        while at < groups:
            pieces.append(rest.pop(0))
            at += pieces[-1].shape[0]
        new_l, new_r, send, keep, squares_out, corr_out, acc = rest
    else:
        new_l, new_r, acc = rest
    pd, b = m.shape[0], m.shape[1]
    if is_first:
        acc[...] = jnp.zeros_like(acc)
    else:
        acc[...] = acc_in[...]

    def load(k, at, unit):
        here, there = pl.ds(at, unit), pl.ds(start + at, unit)
        left = got_l[k, here] + own_l[k, there]
        right = got_r[k, here] + own_r[k, there]
        new_l[k, here] = left
        new_r[k, here] = right
        return left, right

    apply_blocks(load, count, [m[k] for k in range(pd)], start, acc, coef, routes, scale, unit_of(count))
    if not is_last:
        return
    me = lax.axis_index("sector")
    corr = jnp.zeros((b, b), f32)
    squares = jnp.zeros((b, b), f32)
    for k in range(pd):
        g = m[k].astype(f32)
        corr += g * (acc[me * pd + k] + onsite[0, k] * g)
        squares += g * g
    distance = 1
    for piece in pieces:
        for i in range(piece.shape[0]):
            owner = lax.bitwise_xor(me, distance)
            for k in range(pd):
                g = piece[i, k].astype(f32)
                corr += g * acc[owner * pd + k]
                squares += g * g
            distance += 1
    corr = total_of(corr)
    squares_out[...] = jnp.broadcast_to(total_of(squares), squares_out.shape)
    corr_out[...] = jnp.broadcast_to(corr, corr_out.shape)
    split_halves(acc, groups, pd, b, lax.rem(me, 2), send, keep, corr)


def first_apply(chunk, is_first, is_last, groups, channels, arrays, acc_in, extra):
    start, count = chunk
    m = arrays[4]
    pd, b, _ = m.shape
    total = jax.ShapeDtypeStruct((groups * pd, b, b), f32)
    block = jax.ShapeDtypeStruct((pd, count, b, b), bf16)
    args = list(arrays)
    specs = [VM, VM, VM, VM, VM, SM, SM]
    if not is_first:
        args.append(acc_in)
        specs.append(VM)
    scratch = []
    if is_last:
        args += list(extra)
        specs += [SM] + [VM] * (len(extra) - 1)
        outs = [block, block] + exchange_shapes(groups, pd, b) + [jax.ShapeDtypeStruct((8, 128), f32)] * 2
        scratch = [pltpu.VMEM((groups * pd, b, b), f32)]
    else:
        outs = [block, block, total]
    return call(
        functools.partial(first_kernel, chunk, is_first, is_last, groups, channels ** (-0.5)),
        outs,
        specs,
        scratch,
        flops=4 * pd * count * b**3,
        moved=4 * pd * count * b * b,
    )(*args)


def exchange_shapes(groups, pd, b):
    half = groups // 2 * pd
    return [
        jax.ShapeDtypeStruct((half * b + EXTRA, b), bf16),
        jax.ShapeDtypeStruct((half, b, b), f32),
    ]


def combine_kernel(groups, stage, pd, keep_in, got, extra_in, send, keep, extra_out, acc):
    b = keep_in.shape[1]
    me = lax.axis_index("sector")
    for i in range(groups * pd):
        acc[i] = keep_in[i] + got[pl.ds(i * b, b)].astype(f32)
    extra = extra_in[0:1, 0:1] + from_terms(got[pl.ds(groups * pd * b, EXTRA)])[:, 0:1]
    extra_out[...] = jnp.broadcast_to(extra, extra_out.shape)
    bit = lax.rem(lax.div(me, 2**stage), 2)
    split_halves(acc, groups, pd, b, bit, send, keep, extra)


def combine(groups, stage, pd, keep, got, extra):
    b = keep.shape[1]
    return call(
        functools.partial(combine_kernel, groups, stage, pd),
        exchange_shapes(groups, pd, b) + [jax.ShapeDtypeStruct((8, 128), f32)],
        [VM, VM, VM],
        [pltpu.VMEM((groups * pd, b, b), f32)],
        flops=groups * pd * b * b,
        moved=8 * groups * pd * b * b,
    )(keep, got, extra)


def exchange(sectors, pd, send, keep, extra):
    stage = 0
    groups = sectors
    while True:
        got = lax.ppermute(send, "sector", [(i, i ^ (1 << stage)) for i in range(sectors)])
        groups //= 2
        stage += 1
        if groups == 1:
            return keep, got, extra
        send, keep, extra = combine(groups, stage, pd, keep, got, extra)


def second_kernel(bounds, groups, scale, *rest):
    n = len(bounds)
    lefts, rights = rest[:n], rest[n : 2 * n]
    (m, coef, routes, onsite, sizes, keep_in, got, corr_in, squares_in,
     image_out, resid_out, send, keep, sq_out, acc) = rest[2 * n :]
    pd, b = m.shape[0], m.shape[1]
    acc[...] = jnp.zeros_like(acc)
    squares = squares_in[0:1, 0:1]
    corr = corr_in[0:1, 0:1] + from_terms(got[pl.ds(pd * b, EXTRA)])[:, 0:1]
    ritz = corr / (squares + epsilon)
    sums = jnp.zeros((b, b), f32)
    for k in range(pd):
        g = m[k].astype(f32)
        summed = keep_in[k] + got[pl.ds(k * b, b)].astype(f32) + onsite[0, k] * g
        image = jnp.where(live_of(sizes[k], (b, b)), summed, 0.0)
        image_out[0, k] = image.astype(bf16)
        resid = image - ritz * g
        resid_out[k] = resid.astype(bf16)
        sums += resid * resid
    total = total_of(sums)
    sq_out[...] = jnp.broadcast_to(total, sq_out.shape)
    vectors = [resid_out[k] for k in range(pd)]
    for i, (start, count) in enumerate(bounds):

        def load(k, at, unit):
            return lefts[i][k, pl.ds(at, unit)], rights[i][k, pl.ds(at, unit)]

        apply_blocks(load, count, vectors, start, acc, coef, routes, scale, unit_of(count))
    me = lax.axis_index("sector")
    split_halves(acc, groups, pd, b, lax.rem(me, 2), send, keep, total)


def second_apply(bounds, groups, channels, lefts, rights, m, coef, routes, onsite, sizes, keep, got, corr, squares):
    pd, b, _ = m.shape
    n = len(bounds)
    block = jax.ShapeDtypeStruct((1, pd, b, b), bf16)
    return call(
        functools.partial(second_kernel, bounds, groups, channels ** (-0.5)),
        [block, jax.ShapeDtypeStruct((pd, b, b), bf16)]
        + exchange_shapes(groups, pd, b)
        + [jax.ShapeDtypeStruct((8, 128), f32)],
        [VM] * (2 * n) + [VM, SM, SM, SM, SM, VM, VM, VM, VM],
        [pltpu.VMEM((groups * pd, b, b), f32)],
        flops=4 * pd * channels * b**3,
        moved=4 * pd * channels * b * b,
    )(*lefts, *rights, m, coef, routes, onsite, sizes, keep, got, corr, squares)


def final_kernel(resid, onsite, sizes, keep, got, sq_in, squares_in, out):
    pd, b = resid.shape[0], resid.shape[1]
    sq = sq_in[0:1, 0:1] + from_terms(got[pl.ds(pd * b, EXTRA)])[:, 0:1]
    alpha = jnp.sqrt(squares_in[0:1, 0:1] / (sq + epsilon))
    for k in range(pd):
        summed = keep[k] + got[pl.ds(k * b, b)].astype(f32) + onsite[0, k] * resid[k].astype(f32)
        out[0, k] = jnp.where(live_of(sizes[k], (b, b)), alpha * summed, 0.0).astype(bf16)


def final(resid, onsite, sizes, keep, got, sq, squares):
    pd, b, _ = resid.shape
    return call(
        final_kernel,
        [jax.ShapeDtypeStruct((1, pd, b, b), bf16)],
        [VM, SM, SM, VM, VM, VM, VM],
        moved=8 * pd * b * b,
    )(resid, onsite, sizes, keep, got, sq, squares)[0]


def gather_waves(sectors, m):
    held, pieces = m[None], []
    step = 1
    while step < sectors:
        other = lax.ppermute(held, "sector", [(i, i ^ step) for i in range(sectors)])
        pieces.append(other)
        step *= 2
        if step < sectors:
            held = jnp.concatenate([held, other], axis=0)
    return pieces


def body(
    env_left, env_right, edge_left, edge_right, wave_blocks, mpo_coef, onsite, routes, sector_sizes
):
    channels = env_left.shape[2]
    sections = lax.axis_size("section")
    sectors = lax.axis_size("sector")
    pd = wave_blocks.shape[1]
    bounds, at = [], 0
    for c in chunk_sizes(channels):
        bounds.append((at, c))
        at += c
    up = [(i, i + 1) for i in range(sections - 1)]
    down = [(i + 1, i) for i in range(sections - 1)]
    def pass_on(grown):
        return lax.ppermute(grown[0], "section", up), lax.ppermute(grown[1], "section", down)

    token, (head,) = grow(env_left, env_right, edge_left, edge_right, bounds[:1], (), VMEM_LARGE)
    got = [pass_on(head)]
    _, (middle, last) = grow(env_left, env_right, edge_left, edge_right, bounds[1:], (token,), VMEM_LARGE)
    grown, token = gate((*middle, *last), got[0])
    got.append(pass_on(grown[:2]))
    m = mask_wave(wave_blocks, sector_sizes, token)
    got.append(pass_on(gate(grown[2:], (m,))[0]))
    pieces = gather_waves(sectors, m)
    own_l, own_r = own_ends(env_left, env_right, m)
    acc, lefts, rights = None, [], []
    for i, chunk in enumerate(bounds):
        is_last = i == len(bounds) - 1
        res = first_apply(
            chunk, i == 0, is_last, sectors, channels,
            (own_l, own_r, got[i][0], got[i][1], m, mpo_coef, routes), acc, (onsite, *pieces),
        )
        lefts.append(res[0])
        rights.append(res[1])
        acc = res[2]
    send, keep, squares, corr = res[2:]
    keep, summed, corr = exchange(sectors, pd, send, keep, corr)
    image1, resid, send, keep, sq = second_apply(
        bounds, sectors, channels, lefts, rights, m, mpo_coef, routes, onsite,
        sector_sizes, keep, summed, corr, squares,
    )
    keep, summed, sq = exchange(sectors, pd, send, keep, sq)
    image2 = final(resid, onsite, sector_sizes, keep, summed, sq, squares)
    return (image1, image2)


def solution(mesh):
    in_specs = (
        P(("groups", "section"), "sector", None, None, None),
        P(("groups", "section"), "sector", None, None, None),
        P(("groups", "section"), "sector", None, None),
        P(("groups", "section"), "sector", None, None),
        P(("groups", "section"), "sector", None, None),
        P(("groups", "section"), "sector", None),
        P(("groups", "section"), "sector"),
        P(("groups", "section"), "sector", None),
        P(("groups", "sector")),
    )
    out_specs = (
        P(("groups", "section"), "sector", None, None),
        P(("groups", "section"), "sector", None, None),
    )
    return jax.shard_map(body, mesh=mesh, in_specs=in_specs, out_specs=out_specs, check_vma=False)
```

time: 103 us -> 80.8 us (0.78)
  Pallas kernels: 45 us -> 20.8 us
  waiting for transfers between devices: 20.7 us -> 32.7 us
  local copies, waits for them, and re-layouts: 10.1 us -> 3.37 us
  other arithmetic: 2.52 us -> 0.86 us
    ppermute x6, waiting for transfers between devices: 12.4 us -> 24.3 us  [the longest x3 14.8 us: pass_on(): lax.ppermute(grown[0], 'section', up)]
    pallas_call x4 -> x6, Pallas kernels: 21.6 us -> 12.7 us  [the longest x2 10.3 us: grow(): call(functools.partial(grow_kernel, bounds), [jax.ShapeDtypeStruct((8, 12...]
    pallas_call x3, Pallas kernels: 11.9 us -> 4 us  [first_apply(): call(functools.partial(first_kernel, chunk, is_first, is_last, groups, ch...]
    pallas_call x1, Pallas kernels: 10 us -> 2.77 us  [second_apply(): call(functools.partial(second_kernel, bounds, groups, channels ** (-0.5))...]
    unnamed x38 -> x30, local copies, waits for them, and re-layouts: 10.1 us -> 3.37 us
    select_n x2 -> x0, other arithmetic: 1.82 us -> none  [gather_waves(): low = jnp.where(mine_low, held, other)]
  transfers between devices with their start and end apart: 12 -> 12, of which waited for: 6 -> 9; matrix products, arithmetic and copies ran while one was open for 2% -> 1% of each run, Pallas kernels for 16% -> 14%
where the time goes in v2:
time: 80.8 us; the launch traced here: 80.4 us
  waiting for transfers between devices  32.7 us (40%)
  starting transfers between devices  21.8 us (27%)
  Pallas kernels  20.8 us (26%)
  local copies, waits for them, and re-layouts  3.37 us (4%)
  other arithmetic  0.86 us (1%)
  between operations  0.85 us (1%)
    ppermute x3, waiting for transfers between devices, pass_on(): lax.ppermute(grown[0], 'section', up)  14.8 us
    ppermute x3, starting transfers between devices, pass_on(): lax.ppermute(grown[0], 'section', up)  13.2 us
    pallas_call x2, Pallas kernels, grow(): call(functools.partial(grow_kernel, bounds), [jax.ShapeDtypeStruct((8, 12...  10.3 us
    ppermute x3, waiting for transfers between devices, pass_on(): lax.ppermute(grown[1], 'section', down)  9.47 us
    ppermute x4, waiting for transfers between devices, exchange(): lax.ppermute(send, 'sector', [(i, i ^ 1 << stage) for i in range(sectors)])  8.34 us
    pallas_call x3, Pallas kernels, first_apply(): call(functools.partial(first_kernel, chunk, is_first, is_last, groups, ch...  4 us
    ppermute x3, starting transfers between devices, pass_on(): lax.ppermute(grown[1], 'section', down)  3.88 us
    unnamed x30, local copies, waits for them, and re-layouts  3.37 us
  transfers between devices with their start and end apart: 12, of which 9 were waited for; matrix products, arithmetic and copies ran while one was open for 1% of the time, Pallas kernels for 14%

profile of v2, /device:TPU:0, one launch (start us, length us, event | category | flops | bytes accessed | tf_op | source)
XLA Modules:
  0.0 80.4 jit_solution(3981674626381341376)
XLA Ops:
  0.6 3.5 %shard_map.104 = (f32[8,128]{1,0:T(8,128)}, bf16[2,6,128,128]{3,2,1,0:T(8,128)(2,1)}, bf16[2,6,128,128]{3,2,1,0:T(8,128)(2,1)}) custom-call(bf16[1,2,30,128,128]{4,3,2,1,0:T(8,128)(2,1)} %left_hbm.5, bf16[1,2,30,128,128]{4,3,2,1,0:T(8,128)(2,1)} %right_hbm.5, bf16[1,2,128,128]{3,2,1,0:T(8,128)(2,1)} %edge_l_hbm.3, bf16[1,2,128,128]{3,2,1,0:T(8,128)(2,1)} %edge_r_hbm.3), custom_call_target="tpu_custom_call" | custom-call | flops 201326592 | bytes 1572864 | tf_op jit(solution)/shard_map/pallas_call | solution.py:119
  4.2 5.0 %collective-permute-start = (bf16[2,6,128,128]{3,2,1,0:T(8,128)(2,1)}, bf16[2,6,128,128]{3,2,1,0:T(8,128)(2,1)S(1)}, u32[]{:S(2)}, u32[]{:S(2)}) collective-permute-start(bf16[2,6,128,128]{3,2,1,0:T(8,128)(2,1)} %get-tuple-element.46), channel_id=1, source_target_pairs={{0,4},{4,8},{8,12},{1,5},{5,9},{9,13},{2,6},{6,10},{10,14},{3,7},{... | collective-permute-start | bytes 1179656 | tf_op jit(solution)/shard_map/ppermute | solution.py:478
  9.1 1.3 %collective-permute-start.1 = (bf16[2,6,128,128]{3,2,1,0:T(8,128)(2,1)}, bf16[2,6,128,128]{3,2,1,0:T(8,128)(2,1)S(1)}, u32[]{:S(2)}, u32[]{:S(2)}) collective-permute-start(bf16[2,6,128,128]{3,2,1,0:T(8,128)(2,1)} %get-tuple-element.47), channel_id=1, source_target_pairs={{4,0},{8,4},{12,8},{5,1},{9,5},{13,9},{6,2},{10,6},{14,10},{7,3},{... | collective-permute-start | bytes 1179656 | tf_op jit(solution)/shard_map/ppermute | solution.py:478
  10.4 6.8 %shard_map.105 = (f32[8,128]{1,0:T(8,128)}, bf16[2,20,128,128]{3,2,1,0:T(8,128)(2,1)}, bf16[2,20,128,128]{3,2,1,0:T(8,128)(2,1)}, bf16[2,4,128,128]{3,2,1,0:T(8,128)(2,1)}, bf16[2,4,128,128]{3,2,1,0:T(8,128)(2,1)}) custom-call(bf16[1,2,30,128,128]{4,3,2,1,0:T(8,128)(2,1)} %left_hbm.5, bf16[1,2,30,128,128]{4,3,2,1,0:T(8,128)(2,1)} %right_hbm.5, ...), custom_call_target="tpu_custom_call" | custom-call | flops 805306368 | bytes 6291456 | tf_op jit(solution)/shard_map/pallas_call | solution.py:119
  17.8 4.0 %collective-permute-done.1.refs_5_.got_r = bf16[2,6,128,128]{3,2,1,0:T(8,128)(2,1)S(1)} collective-permute-done((bf16[2,6,128,128]{3,2,1,0:T(8,128)(2,1)}, bf16[2,6,128,128]{3,2,1,0:T(8,128)(2,1)S(1)}, u32[]{:S(2)}, u32[]{:S(2)}) %collective-permute-start.1) | collective-permute-done | bytes 393248 | tf_op jit(solution)/shard_map/ppermute | solution.py:478
  21.8 0.7 copy-done.7
  22.5 0.6 shard_map.106
  23.1 3.7 %collective-permute-start.2 = (bf16[2,20,128,128]{3,2,1,0:T(8,128)(2,1)}, bf16[2,20,128,128]{3,2,1,0:T(8,128)(2,1)S(1)}, u32[]{:S(2)}, u32[]{:S(2)}) collective-permute-start(bf16[2,20,128,128]{3,2,1,0:T(8,128)(2,1)} %get-tuple-element.52), channel_id=1, source_target_pairs={{0,4},{4,8},{8,12},{1,5},{5,9},{9,13},{2,6},{6,10},{10,14},{3,7},{... | collective-permute-start | bytes 3932168 | tf_op jit(solution)/shard_map/ppermute | solution.py:478
  26.8 1.3 %collective-permute-start.3 = (bf16[2,20,128,128]{3,2,1,0:T(8,128)(2,1)}, bf16[2,20,128,128]{3,2,1,0:T(8,128)(2,1)S(1)}, u32[]{:S(2)}, u32[]{:S(2)}) collective-permute-start(bf16[2,20,128,128]{3,2,1,0:T(8,128)(2,1)} %get-tuple-element.53), channel_id=1, source_target_pairs={{4,0},{8,4},{12,8},{5,1},{9,5},{13,9},{6,2},{10,6},{14,10},{7,3},{... | collective-permute-start | bytes 3932168 | tf_op jit(solution)/shard_map/ppermute | solution.py:478
  28.1 0.7 copy-done.14
  28.8 0.6 shard_map.107.after.m.refs_2_.rest_6_
  30.0 0.6 shard_map.111
  30.6 4.5 %collective-permute-start.4 = (bf16[2,4,128,128]{3,2,1,0:T(8,128)(2,1)}, bf16[2,4,128,128]{3,2,1,0:T(8,128)(2,1)S(1)}, u32[]{:S(2)}, u32[]{:S(2)}) collective-permute-start(bf16[2,4,128,128]{3,2,1,0:T(8,128)(2,1)} %get-tuple-element.58), channel_id=1, source_target_pairs={{0,4},{4,8},{8,12},{1,5},{5,9},{9,13},{2,6},{6,10},{10,14},{3,7},{... | collective-permute-start | bytes 786440 | tf_op jit(solution)/shard_map/ppermute | solution.py:478
  35.2 1.3 %collective-permute-start.5 = (bf16[2,4,128,128]{3,2,1,0:T(8,128)(2,1)}, bf16[2,4,128,128]{3,2,1,0:T(8,128)(2,1)S(1)}, u32[]{:S(2)}, u32[]{:S(2)}) collective-permute-start(bf16[2,4,128,128]{3,2,1,0:T(8,128)(2,1)} %get-tuple-element.59), channel_id=1, source_target_pairs={{4,0},{8,4},{12,8},{5,1},{9,5},{13,9},{6,2},{10,6},{14,10},{7,3},{... | collective-permute-start | bytes 786440 | tf_op jit(solution)/shard_map/ppermute | solution.py:478
  36.5 0.9 %pad_maximum_fusion = bf16[2,2,128,128]{3,2,1,0:T(8,128)(2,1)S(1)} fusion(bf16[1,2,128,128]{3,2,1,0:T(8,128)(2,1)S(1)} %collective-permute-done.6.rest_2_, bf16[1,2,128,128]{3,2,1,0:T(8,128)(2,1)} %bitcast.2), kind=kLoop, calls=%fused_computation | loop fusion | flops 65536 | bytes 262144 | tf_op jit(solution)/shard_map/concatenate | solution.py:460
  37.3 1.6 %collective-permute-start.7 = (bf16[2,2,128,128]{3,2,1,0:T(8,128)(2,1)S(1)}, bf16[2,2,128,128]{3,2,1,0:T(8,128)(2,1)S(1)}, u32[]{:S(2)}, u32[]{:S(2)}) collective-permute-start(bf16[2,2,128,128]{3,2,1,0:T(8,128)(2,1)S(1)} %pad_maximum_fusion), channel_id=1, source_target_pairs={{0,2},{1,3},{2,0},{3,1},{4,6},{5,7},{6,4},{7,5},{8,10},{9,11},{10,... | collective-permute-start | bytes 393224 | tf_op jit(solution)/shard_map/ppermute | solution.py:456
  38.9 0.8 %copy-done.3 = bf16[2,128,128]{2,1,0:T(8,128)(2,1)S(1)} copy-done((bf16[2,128,128]{2,1,0:T(8,128)(2,1)S(1)}, bf16[2,128,128]{2,1,0:T(8,128)(2,1)}, u32[]{:S(2)}) %copy-start.3) | copy-done | bytes 65560
  39.8 0.6 shard_map.108
  40.9 1.0 %shard_map.109 = (bf16[2,6,128,128]{3,2,1,0:T(8,128)(2,1)S(1)}, bf16[2,6,128,128]{3,2,1,0:T(8,128)(2,1)S(1)}, f32[8,128,128]{2,1,0:T(8,128)S(1)}) custom-call(bf16[2,30,128,128]{3,2,1,0:T(8,128)(2,1)S(1)} %get-tuple-element.49.own_l, bf16[2,30,128,128]{3,2,1,0:T(8,128)(2,1)S(1)} %get-tuple-element.50.own_r, bf16[2,6,128,128]{3,2,1,0:T(8,128)(2,1)S(1)} %copy-done.6, ...), custom_call_target="tpu_custom_call" | custom-call | flops 100663296 | bytes 786432 | tf_op jit(solution)/shard_map/pallas_call | solution.py:332
  41.9 14.3 %collective-permute-done.2.got_l = bf16[2,20,128,128]{3,2,1,0:T(8,128)(2,1)S(1)} collective-permute-done((bf16[2,20,128,128]{3,2,1,0:T(8,128)(2,1)}, bf16[2,20,128,128]{3,2,1,0:T(8,128)(2,1)S(1)}, u32[]{:S(2)}, u32[]{:S(2)}) %collective-permute-start.2) | collective-permute-done | bytes 1310752 | tf_op jit(solution)/shard_map/ppermute | solution.py:478
  56.3 4.4 %collective-permute-done.3.got_r = bf16[2,20,128,128]{3,2,1,0:T(8,128)(2,1)S(1)} collective-permute-done((bf16[2,20,128,128]{3,2,1,0:T(8,128)(2,1)}, bf16[2,20,128,128]{3,2,1,0:T(8,128)(2,1)S(1)}, u32[]{:S(2)}, u32[]{:S(2)}) %collective-permute-start.3) | collective-permute-done | bytes 1310752 | tf_op jit(solution)/shard_map/ppermute | solution.py:478
  60.6 1.9 %shard_map.110 = (bf16[2,20,128,128]{3,2,1,0:T(8,128)(2,1)S(1)}, bf16[2,20,128,128]{3,2,1,0:T(8,128)(2,1)S(1)}, f32[8,128,128]{2,1,0:T(8,128)S(1)}) custom-call(bf16[2,30,128,128]{3,2,1,0:T(8,128)(2,1)S(1)} %get-tuple-element.49.own_l, bf16[2,30,128,128]{3,2,1,0:T(8,128)(2,1)S(1)} %get-tuple-element.50.own_r, ...), custom_call_target="tpu_custom_call" | custom-call | flops 335544320 | bytes 2621440 | tf_op jit(solution)/shard_map/pallas_call | solution.py:332
  62.5 1.1 %collective-permute-done.5.got_r = bf16[2,4,128,128]{3,2,1,0:T(8,128)(2,1)S(1)} collective-permute-done((bf16[2,4,128,128]{3,2,1,0:T(8,128)(2,1)}, bf16[2,4,128,128]{3,2,1,0:T(8,128)(2,1)S(1)}, u32[]{:S(2)}, u32[]{:S(2)}) %collective-permute-start.5) | collective-permute-done | bytes 262176 | tf_op jit(solution)/shard_map/ppermute | solution.py:478
  63.6 1.1 %shard_map.112 = (bf16[2,4,128,128]{3,2,1,0:T(8,128)(2,1)S(1)}, bf16[2,4,128,128]{3,2,1,0:T(8,128)(2,1)S(1)}, bf16[528,128]{1,0:T(8,128)(2,1)S(1)}, f32[4,128,12...) custom-call(bf16[2,30,128,128]{3,2,1,0:T(8,128)(2,1)S(1)} %get-tuple-element.49.own_l, ...), custom_call_target="tpu_custom_call" | custom-call | flops 67108864 | bytes 524288 | tf_op jit(solution)/shard_map/pallas_call | solution.py:332
  64.7 1.3 %collective-permute-done.8.got = bf16[528,128]{1,0:T(8,128)(2,1)S(1)} collective-permute-done((bf16[528,128]{1,0:T(8,128)(2,1)S(1)}, bf16[528,128]{1,0:T(8,128)(2,1)S(1)}, u32[]{:S(2)}, u32[]{:S(2)}) %collective-permute-start.8) | collective-permute-done | bytes 135200 | tf_op jit(solution)/shard_map/ppermute | solution.py:377
  66.2 1.6 %collective-permute-start.9 = (bf16[272,128]{1,0:T(8,128)(2,1)S(1)}, bf16[272,128]{1,0:T(8,128)(2,1)S(1)}, u32[]{:S(2)}, u32[]{:S(2)}) collective-permute-start(bf16[272,128]{1,0:T(8,128)(2,1)S(1)} %get-tuple-element.69), channel_id=1, source_target_pairs={{0,2},{1,3},{2,0},{3,1},{4,6},{5,7},{6,4},{7,5},{8,10},{9,11},{10,... | collective-permute-start | bytes 208904 | tf_op jit(solution)/shard_map/ppermute | solution.py:377
  67.7 2.8 %collective-permute-done.9.rest_12_ = bf16[272,128]{1,0:T(8,128)(2,1)S(1)} collective-permute-done((bf16[272,128]{1,0:T(8,128)(2,1)S(1)}, bf16[272,128]{1,0:T(8,128)(2,1)S(1)}, u32[]{:S(2)}, u32[]{:S(2)}) %collective-permute-start.9) | collective-permute-done | bytes 69664 | tf_op jit(solution)/shard_map/ppermute | solution.py:377
  70.5 2.8 %shard_map.114 = (bf16[1,2,128,128]{3,2,1,0:T(8,128)(2,1)}, bf16[2,128,128]{2,1,0:T(8,128)(2,1)S(1)}, bf16[528,128]{1,0:T(8,128)(2,1)S(1)}, f32[4,128,128]{2,1,0:T(8,128)S(1)}, f32[8,128]{1,0:T(8,128)S(1)}) custom-call(bf16[2,6,128,128]{3,2,1,0:T(8,128)(2,1)S(1)} %get-tuple-element.51.rest_0_, bf16[2,20,128,128]{3,2,1,0:T(8,128)(2,1)S(1)} %get-tuple-element.55.rest_1_, ...), custom_call_target="tpu_custom_call" | custom-call | flops 503316480 | bytes 3932160 | tf_op jit(solution)/shard_map/pallas_call | solution.py:421
  73.3 1.4 %collective-permute-done.10.got = bf16[528,128]{1,0:T(8,128)(2,1)S(1)} collective-permute-done((bf16[528,128]{1,0:T(8,128)(2,1)S(1)}, bf16[528,128]{1,0:T(8,128)(2,1)S(1)}, u32[]{:S(2)}, u32[]{:S(2)}) %collective-permute-start.10) | collective-permute-done | bytes 135200 | tf_op jit(solution)/shard_map/ppermute | solution.py:377
  74.7 1.5 %collective-permute-start.11 = (bf16[272,128]{1,0:T(8,128)(2,1)S(1)}, bf16[272,128]{1,0:T(8,128)(2,1)S(1)}, u32[]{:S(2)}, u32[]{:S(2)}) collective-permute-start(bf16[272,128]{1,0:T(8,128)(2,1)S(1)} %get-tuple-element.78), channel_id=1, source_target_pairs={{0,2},{1,3},{2,0},{3,1},{4,6},{5,7},{6,4},{7,5},{8,10},{9,11},{10,... | collective-permute-start | bytes 208904 | tf_op jit(solution)/shard_map/ppermute | solution.py:377
  76.3 2.8 %collective-permute-done.11.got = bf16[272,128]{1,0:T(8,128)(2,1)S(1)} collective-permute-done((bf16[272,128]{1,0:T(8,128)(2,1)S(1)}, bf16[272,128]{1,0:T(8,128)(2,1)S(1)}, u32[]{:S(2)}, u32[]{:S(2)}) %collective-permute-start.11) | collective-permute-done | bytes 69664 | tf_op jit(solution)/shard_map/ppermute | solution.py:377
  79.1 1.3 %shard_map.116 = bf16[1,2,128,128]{3,2,1,0:T(8,128)(2,1)} custom-call(bf16[2,128,128]{2,1,0:T(8,128)(2,1)S(1)} %get-tuple-element.73.resid, f32[1,2]{1,0:T(1,128)S(1)} %copy-done.13, s32[2]{0:T(128)S(1)} %copy-done.12, f32[2,128,128]{2,1,0:T(8,128)S(1)} %get-tuple-element.77.keep, bf16[272,128]{1,0:T(8,128)(2,1)S(1)} %collective-permute-done.11.got, ...), custom_call_target="tpu_custom_call" | custom-call | bytes 262144 | tf_op jit(solution)/shard_map/pallas_call | solution.py:444
  (36 shorter events, 1.9 us)
Async XLA Ops:
  4.2 13.6 %collective-permute-start = (bf16[2,6,128,128]{3,2,1,0:T(8,128)(2,1)}, bf16[2,6,128,128]{3,2,1,0:T(8,128)(2,1)S(1)}, u32[]{:S(2)}, u32[]{:S(2)}) collective-permute-start(bf16[2,6,128,128]{3,2,1,0:T(8,128)(2,1)} %get-tuple-element.46), channel_id=1, source_target_pairs={{0,4},{4,8},{8,12},{1,5},{5,9},{9,13},{2,6},{6,10},{10,14},{3,7},{... | collective-permute-start | bytes 1179656 | tf_op jit(solution)/shard_map/ppermute | solution.py:478
  9.1 12.7 %collective-permute-start.1 = (bf16[2,6,128,128]{3,2,1,0:T(8,128)(2,1)}, bf16[2,6,128,128]{3,2,1,0:T(8,128)(2,1)S(1)}, u32[]{:S(2)}, u32[]{:S(2)}) collective-permute-start(bf16[2,6,128,128]{3,2,1,0:T(8,128)(2,1)} %get-tuple-element.47), channel_id=1, source_target_pairs={{4,0},{8,4},{12,8},{5,1},{9,5},{13,9},{6,2},{10,6},{14,10},{7,3},{... | collective-permute-start | bytes 1179656 | tf_op jit(solution)/shard_map/ppermute | solution.py:478
  10.4 17.7 %copy-start.9 = (bf16[1,2,128,128]{3,2,1,0:T(8,128)(2,1)S(1)}, bf16[1,2,128,128]{3,2,1,0:T(8,128)(2,1)}, u32[]{:S(2)}) copy-start(bf16[1,2,128,128]{3,2,1,0:T(8,128)(2,1)} %wave.1) | copy-start | bytes 196612
  17.8 4.0 %copy-start.5 = (bf16[2,6,128,128]{3,2,1,0:T(8,128)(2,1)}, bf16[2,6,128,128]{3,2,1,0:T(8,128)(2,1)S(1)}, u32[]{:S(2)}) copy-start(bf16[2,6,128,128]{3,2,1,0:T(8,128)(2,1)S(1)} %collective-permute-done.refs_4_.got_l) | copy-start | bytes 1179652
  21.8 0.7 copy-start.7
  22.5 5.6 %copy-start.12 = (s32[2]{0:T(128)S(1)}, s32[2]{0:T(128)}, u32[]{:S(2)}) copy-start(s32[2]{0:T(128)} %sizes.3) | copy-start | bytes 28
  22.5 16.4 %copy-start = (bf16[1,2,30,128,128]{4,3,2,1,0:T(8,128)(2,1)S(1)}, bf16[1,2,30,128,128]{4,3,2,1,0:T(8,128)(2,1)}, u32[]{:S(2)}) copy-start(bf16[1,2,30,128,128]{4,3,2,1,0:T(8,128)(2,1)} %left_hbm.5) | copy-start | bytes 5898244
  22.5 16.4 %copy-start.1 = (bf16[1,2,30,128,128]{4,3,2,1,0:T(8,128)(2,1)S(1)}, bf16[1,2,30,128,128]{4,3,2,1,0:T(8,128)(2,1)}, u32[]{:S(2)}) copy-start(bf16[1,2,30,128,128]{4,3,2,1,0:T(8,128)(2,1)} %right_hbm.5) | copy-start | bytes 5898244
  23.1 33.1 %collective-permute-start.2 = (bf16[2,20,128,128]{3,2,1,0:T(8,128)(2,1)}, bf16[2,20,128,128]{3,2,1,0:T(8,128)(2,1)S(1)}, u32[]{:S(2)}, u32[]{:S(2)}) collective-permute-start(bf16[2,20,128,128]{3,2,1,0:T(8,128)(2,1)} %get-tuple-element.52), channel_id=1, source_target_pairs={{0,4},{4,8},{8,12},{1,5},{5,9},{9,13},{2,6},{6,10},{10,14},{3,7},{... | collective-permute-start | bytes 3932168 | tf_op jit(solution)/shard_map/ppermute | solution.py:478
  26.8 33.8 %collective-permute-start.3 = (bf16[2,20,128,128]{3,2,1,0:T(8,128)(2,1)}, bf16[2,20,128,128]{3,2,1,0:T(8,128)(2,1)S(1)}, u32[]{:S(2)}, u32[]{:S(2)}) collective-permute-start(bf16[2,20,128,128]{3,2,1,0:T(8,128)(2,1)} %get-tuple-element.53), channel_id=1, source_target_pairs={{4,0},{8,4},{12,8},{5,1},{9,5},{13,9},{6,2},{10,6},{14,10},{7,3},{... | collective-permute-start | bytes 3932168 | tf_op jit(solution)/shard_map/ppermute | solution.py:478
  28.1 0.7 copy-start.14
  29.4 0.6 copy-start.2
  29.4 7.1 %collective-permute-start.6 = (bf16[1,2,128,128]{3,2,1,0:T(8,128)(2,1)S(1)}, bf16[1,2,128,128]{3,2,1,0:T(8,128)(2,1)S(1)}, u32[]{:S(2)}, u32[]{:S(2)}) collective-permute-start(bf16[1,2,128,128]{3,2,1,0:T(8,128)(2,1)S(1)} %bitcast.1), channel_id=1, source_target_pairs={{0,1},{1,0},{2,3},{3,2},{4,5},{5,4},{6,7},{7,6},{8,9},{9,8},{10,11... | collective-permute-start | bytes 196616 | tf_op jit(solution)/shard_map/ppermute | solution.py:456
  30.6 31.9 %collective-permute-start.4 = (bf16[2,4,128,128]{3,2,1,0:T(8,128)(2,1)}, bf16[2,4,128,128]{3,2,1,0:T(8,128)(2,1)S(1)}, u32[]{:S(2)}, u32[]{:S(2)}) collective-permute-start(bf16[2,4,128,128]{3,2,1,0:T(8,128)(2,1)} %get-tuple-element.58), channel_id=1, source_target_pairs={{0,4},{4,8},{8,12},{1,5},{5,9},{9,13},{2,6},{6,10},{10,14},{3,7},{... | collective-permute-start | bytes 786440 | tf_op jit(solution)/shard_map/ppermute | solution.py:478
  35.2 28.4 %collective-permute-start.5 = (bf16[2,4,128,128]{3,2,1,0:T(8,128)(2,1)}, bf16[2,4,128,128]{3,2,1,0:T(8,128)(2,1)S(1)}, u32[]{:S(2)}, u32[]{:S(2)}) collective-permute-start(bf16[2,4,128,128]{3,2,1,0:T(8,128)(2,1)} %get-tuple-element.59), channel_id=1, source_target_pairs={{4,0},{8,4},{12,8},{5,1},{9,5},{13,9},{6,2},{10,6},{14,10},{7,3},{... | collective-permute-start | bytes 786440 | tf_op jit(solution)/shard_map/ppermute | solution.py:478
  37.3 25.1 %collective-permute-start.7 = (bf16[2,2,128,128]{3,2,1,0:T(8,128)(2,1)S(1)}, bf16[2,2,128,128]{3,2,1,0:T(8,128)(2,1)S(1)}, u32[]{:S(2)}, u32[]{:S(2)}) collective-permute-start(bf16[2,2,128,128]{3,2,1,0:T(8,128)(2,1)S(1)} %pad_maximum_fusion), channel_id=1, source_target_pairs={{0,2},{1,3},{2,0},{3,1},{4,6},{5,7},{6,4},{7,5},{8,10},{9,11},{10,... | collective-permute-start | bytes 393224 | tf_op jit(solution)/shard_map/ppermute | solution.py:456
  38.9 0.8 %copy-start.3 = (bf16[2,128,128]{2,1,0:T(8,128)(2,1)S(1)}, bf16[2,128,128]{2,1,0:T(8,128)(2,1)}, u32[]{:S(2)}) copy-start(bf16[2,128,128]{2,1,0:T(8,128)(2,1)} %copy-done.2) | copy-start | bytes 196612
  39.7 0.8 %copy-start.4 = (bf16[2,128,128]{2,1,0:T(8,128)(2,1)S(1)}, bf16[2,128,128]{2,1,0:T(8,128)(2,1)}, u32[]{:S(2)}) copy-start(bf16[2,128,128]{2,1,0:T(8,128)(2,1)} %copy-done.2) | copy-start | bytes 196612
  39.7 1.0 %copy-start.6 = (bf16[2,6,128,128]{3,2,1,0:T(8,128)(2,1)S(1)}, bf16[2,6,128,128]{3,2,1,0:T(8,128)(2,1)}, u32[]{:S(2)}) copy-start(bf16[2,6,128,128]{3,2,1,0:T(8,128)(2,1)} %copy-done.5) | copy-start | bytes 1179652
  39.8 1.1 %copy-start.8 = (bf16[2,6,128,128]{3,2,1,0:T(8,128)(2,1)S(1)}, bf16[2,6,128,128]{3,2,1,0:T(8,128)(2,1)}, u32[]{:S(2)}) copy-start(bf16[2,6,128,128]{3,2,1,0:T(8,128)(2,1)} %copy-done.7) | copy-start | bytes 1179652
  39.8 1.1 %copy-start.10 = (f32[1,2,30]{2,1,0:T(2,128)S(1)}, f32[1,2,30]{2,1,0:T(2,128)}, u32[]{:S(2)}) copy-start(f32[1,2,30]{2,1,0:T(2,128)} %rest_7_.1) | copy-start | bytes 724
  39.8 1.1 %copy-start.11 = (s32[1,2,30]{2,1,0:T(2,128)S(1)}, s32[1,2,30]{2,1,0:T(2,128)}, u32[]{:S(2)}) copy-start(s32[1,2,30]{2,1,0:T(2,128)} %rest_8_.1) | copy-start | bytes 724
  60.6 3.0 %copy-start.13 = (f32[1,2]{1,0:T(1,128)S(1)}, f32[1,2]{1,0:T(1,128)}, u32[]{:S(2)}) copy-start(f32[1,2]{1,0:T(1,128)} %onsite.1) | copy-start | bytes 28
  64.7 1.4 %collective-permute-start.8 = (bf16[528,128]{1,0:T(8,128)(2,1)S(1)}, bf16[528,128]{1,0:T(8,128)(2,1)S(1)}, u32[]{:S(2)}, u32[]{:S(2)}) collective-permute-start(bf16[528,128]{1,0:T(8,128)(2,1)S(1)} %get-tuple-element.66), channel_id=1, source_target_pairs={{0,1},{1,0},{2,3},{3,2},{4,5},{5,4},{6,7},{7,6},{8,9},{9,8},{10,11... | collective-permute-start | bytes 405512 | tf_op jit(solution)/shard_map/ppermute | solution.py:377
  66.2 4.4 %collective-permute-start.9 = (bf16[272,128]{1,0:T(8,128)(2,1)S(1)}, bf16[272,128]{1,0:T(8,128)(2,1)S(1)}, u32[]{:S(2)}, u32[]{:S(2)}) collective-permute-start(bf16[272,128]{1,0:T(8,128)(2,1)S(1)} %get-tuple-element.69), channel_id=1, source_target_pairs={{0,2},{1,3},{2,0},{3,1},{4,6},{5,7},{6,4},{7,5},{8,10},{9,11},{10,... | collective-permute-start | bytes 208904 | tf_op jit(solution)/shard_map/ppermute | solution.py:377
  73.3 1.4 %collective-permute-start.10 = (bf16[528,128]{1,0:T(8,128)(2,1)S(1)}, bf16[528,128]{1,0:T(8,128)(2,1)S(1)}, u32[]{:S(2)}, u32[]{:S(2)}) collective-permute-start(bf16[528,128]{1,0:T(8,128)(2,1)S(1)} %get-tuple-element.75), channel_id=1, source_target_pairs={{0,1},{1,0},{2,3},{3,2},{4,5},{5,4},{6,7},{7,6},{8,9},{9,8},{10,11... | collective-permute-start | bytes 405512 | tf_op jit(solution)/shard_map/ppermute | solution.py:377
  74.7 4.4 %collective-permute-start.11 = (bf16[272,128]{1,0:T(8,128)(2,1)S(1)}, bf16[272,128]{1,0:T(8,128)(2,1)S(1)}, u32[]{:S(2)}, u32[]{:S(2)}) collective-permute-start(bf16[272,128]{1,0:T(8,128)(2,1)S(1)} %get-tuple-element.78), channel_id=1, source_target_pairs={{0,2},{1,3},{2,0},{3,1},{4,6},{5,7},{6,4},{7,5},{8,10},{9,11},{10,... | collective-permute-start | bytes 208904 | tf_op jit(solution)/shard_map/ppermute | solution.py:377

commit v3 on v2

--- a/solution.py
+++ b/solution.py
@@ -143,7 +143,6 @@
         [HB] * (len(arrays) + len(after)),
         aliases={i: i for i in range(len(arrays))},
         out_specs=[HB] * len(arrays) + [VM],
-        vmem=VMEM_LARGE,
     )(*arrays, *after)
     return held, token
 
@@ -187,7 +186,7 @@
     shape = jax.ShapeDtypeStruct((pd, channels, b, b), bf16)
     return call(
         own_kernel, [shape, shape], [HB, HB, HB], [pltpu.SemaphoreType.DMA],
-        flops=pd * channels * b * b, moved=4 * pd * channels * b * b,
+        flops=10**10, moved=10**6,
     )(env_left, env_right, after)
 
 
@@ -480,10 +479,10 @@
     token, (head,) = grow(env_left, env_right, edge_left, edge_right, bounds[:1], (), VMEM_LARGE)
     got = [pass_on(head)]
     _, (middle, last) = grow(env_left, env_right, edge_left, edge_right, bounds[1:], (token,), VMEM_LARGE)
-    grown, token = gate((*middle, *last), got[0])
-    got.append(pass_on(grown[:2]))
+    got.append(pass_on(middle))
+    grown, token = gate(last, got[0])
     m = mask_wave(wave_blocks, sector_sizes, token)
-    got.append(pass_on(gate(grown[2:], (m,))[0]))
+    got.append(pass_on(grown))
     pieces = gather_waves(sectors, m)
     own_l, own_r = own_ends(env_left, env_right, m)
     acc, lefts, rights = None, [], []

time: 80.8 us -> 76.6 us (0.948)
  local copies, waits for them, and re-layouts: 3.37 us -> 0.04 us
  Pallas kernels: 20.8 us -> 19.6 us
  starting transfers between devices: 21.8 us -> 23 us
  other arithmetic: 0.86 us -> 0.02 us
    ppermute x3, waiting for transfers between devices: 14.8 us -> 18.3 us  [pass_on(): lax.ppermute(grown[0], 'section', up)]
    ppermute x3, waiting for transfers between devices: 9.47 us -> 6.1 us  [pass_on(): lax.ppermute(grown[1], 'section', down)]
    unnamed x30 -> x14, local copies, waits for them, and re-layouts: 3.37 us -> 0.04 us
    pallas_call x2 -> x1, Pallas kernels: 1.19 us -> 0.01 us  [gate(): call(gate_kernel, [jax.ShapeDtypeStruct(a.shape, a.dtype) for a in arrays...]
    ppermute x3, starting transfers between devices: 13.2 us -> 14.3 us  [pass_on(): lax.ppermute(grown[0], 'section', up)]
    concatenate x1, other arithmetic: 0.86 us -> 0.02 us  [gather_waves(): held = jnp.concatenate([held, other], axis=0)]
  transfers between devices with their start and end apart: 12 -> 12, of which waited for: 9 -> 7; matrix products, arithmetic and copies ran while one was open for 1% -> 0% of each run, Pallas kernels for 14% -> 14%
where the time goes in v3:
time: 76.6 us; the launch traced here: 76.3 us
  waiting for transfers between devices  32.8 us (43%)
  starting transfers between devices  23 us (30%)
  Pallas kernels  19.6 us (26%)
  between operations  0.89 us (1%)
    ppermute x3, waiting for transfers between devices, pass_on(): lax.ppermute(grown[0], 'section', up)  18.3 us
    ppermute x3, starting transfers between devices, pass_on(): lax.ppermute(grown[0], 'section', up)  14.3 us
    pallas_call x2, Pallas kernels, grow(): call(functools.partial(grow_kernel, bounds), [jax.ShapeDtypeStruct((8, 12...  10.4 us
    ppermute x4, waiting for transfers between devices, exchange(): lax.ppermute(send, 'sector', [(i, i ^ 1 << stage) for i in range(sectors)])  8.31 us
    ppermute x3, waiting for transfers between devices, pass_on(): lax.ppermute(grown[1], 'section', down)  6.1 us
    pallas_call x3, Pallas kernels, first_apply(): call(functools.partial(first_kernel, chunk, is_first, is_last, groups, ch...  3.94 us
    ppermute x3, starting transfers between devices, pass_on(): lax.ppermute(grown[1], 'section', down)  3.88 us
    ppermute x4, starting transfers between devices, exchange(): lax.ppermute(send, 'sector', [(i, i ^ 1 << stage) for i in range(sectors)])  3.17 us
  transfers between devices with their start and end apart: 12, of which 7 were waited for; matrix products, arithmetic and copies ran while one was open for 0% of the time, Pallas kernels for 14%

profile of v3, /device:TPU:0, one launch (start us, length us, event | category | flops | bytes accessed | tf_op | source)
XLA Modules:
  0.0 76.3 jit_solution(16852601967520025394)
XLA Ops:
  0.6 3.5 %shard_map.104 = (f32[8,128]{1,0:T(8,128)}, bf16[2,6,128,128]{3,2,1,0:T(8,128)(2,1)}, bf16[2,6,128,128]{3,2,1,0:T(8,128)(2,1)}) custom-call(bf16[1,2,30,128,128]{4,3,2,1,0:T(8,128)(2,1)} %left_hbm.5, bf16[1,2,30,128,128]{4,3,2,1,0:T(8,128)(2,1)} %right_hbm.5, bf16[1,2,128,128]{3,2,1,0:T(8,128)(2,1)} %edge_l_hbm.3, bf16[1,2,128,128]{3,2,1,0:T(8,128)(2,1)} %edge_r_hbm.3), custom_call_target="tpu_custom_call" | custom-call | flops 201326592 | bytes 1572864 | tf_op jit(solution)/shard_map/pallas_call | solution.py:119
  4.2 5.0 %collective-permute-start = (bf16[2,6,128,128]{3,2,1,0:T(8,128)(2,1)}, bf16[2,6,128,128]{3,2,1,0:T(8,128)(2,1)S(1)}, u32[]{:S(2)}, u32[]{:S(2)}) collective-permute-start(bf16[2,6,128,128]{3,2,1,0:T(8,128)(2,1)} %get-tuple-element.40), channel_id=1, source_target_pairs={{0,4},{4,8},{8,12},{1,5},{5,9},{9,13},{2,6},{6,10},{10,14},{3,7},{... | collective-permute-start | bytes 1179656 | tf_op jit(solution)/shard_map/ppermute | solution.py:477
  9.1 1.3 %collective-permute-start.1 = (bf16[2,6,128,128]{3,2,1,0:T(8,128)(2,1)}, bf16[2,6,128,128]{3,2,1,0:T(8,128)(2,1)S(1)}, u32[]{:S(2)}, u32[]{:S(2)}) collective-permute-start(bf16[2,6,128,128]{3,2,1,0:T(8,128)(2,1)} %get-tuple-element.41), channel_id=1, source_target_pairs={{4,0},{8,4},{12,8},{5,1},{9,5},{13,9},{6,2},{10,6},{14,10},{7,3},{... | collective-permute-start | bytes 1179656 | tf_op jit(solution)/shard_map/ppermute | solution.py:477
  10.4 0.0 copy-start
  10.5 0.0 copy-start.1
  10.5 6.9 %shard_map.105 = (f32[8,128]{1,0:T(8,128)}, bf16[2,20,128,128]{3,2,1,0:T(8,128)(2,1)}, bf16[2,20,128,128]{3,2,1,0:T(8,128)(2,1)}, bf16[2,4,128,128]{3,2,1,0:T(8,128)(2,1)}, bf16[2,4,128,128]{3,2,1,0:T(8,128)(2,1)}) custom-call(bf16[1,2,30,128,128]{4,3,2,1,0:T(8,128)(2,1)} %left_hbm.5, bf16[1,2,30,128,128]{4,3,2,1,0:T(8,128)(2,1)} %right_hbm.5, ...), custom_call_target="tpu_custom_call" | custom-call | flops 805306368 | bytes 6291456 | tf_op jit(solution)/shard_map/pallas_call | solution.py:119
  17.4 0.0 copy-start.2
  17.4 4.8 %collective-permute-start.2 = (bf16[2,20,128,128]{3,2,1,0:T(8,128)(2,1)}, bf16[2,20,128,128]{3,2,1,0:T(8,128)(2,1)S(1)}, u32[]{:S(2)}, u32[]{:S(2)}) collective-permute-start(bf16[2,20,128,128]{3,2,1,0:T(8,128)(2,1)} %get-tuple-element.46), channel_id=1, source_target_pairs={{0,4},{4,8},{8,12},{1,5},{5,9},{9,13},{2,6},{6,10},{10,14},{3,7},{... | collective-permute-start | bytes 3932168 | tf_op jit(solution)/shard_map/ppermute | solution.py:477
  22.2 1.3 %collective-permute-start.3 = (bf16[2,20,128,128]{3,2,1,0:T(8,128)(2,1)}, bf16[2,20,128,128]{3,2,1,0:T(8,128)(2,1)S(1)}, u32[]{:S(2)}, u32[]{:S(2)}) collective-permute-start(bf16[2,20,128,128]{3,2,1,0:T(8,128)(2,1)} %get-tuple-element.47), channel_id=1, source_target_pairs={{4,0},{8,4},{12,8},{5,1},{9,5},{13,9},{6,2},{10,6},{14,10},{7,3},{... | collective-permute-start | bytes 3932168 | tf_op jit(solution)/shard_map/ppermute | solution.py:477
  23.5 0.6 shard_map.107.after.m.rest_6_
  24.1 0.1 collective-permute-start.6
  24.2 4.6 %collective-permute-start.4 = (bf16[2,4,128,128]{3,2,1,0:T(8,128)(2,1)}, bf16[2,4,128,128]{3,2,1,0:T(8,128)(2,1)S(1)}, u32[]{:S(2)}, u32[]{:S(2)}) collective-permute-start(bf16[2,4,128,128]{3,2,1,0:T(8,128)(2,1)} %get-tuple-element.50), channel_id=1, source_target_pairs={{0,4},{4,8},{8,12},{1,5},{5,9},{9,13},{2,6},{6,10},{10,14},{3,7},{... | collective-permute-start | bytes 786440 | tf_op jit(solution)/shard_map/ppermute | solution.py:477
  28.8 1.3 %collective-permute-start.5 = (bf16[2,4,128,128]{3,2,1,0:T(8,128)(2,1)}, bf16[2,4,128,128]{3,2,1,0:T(8,128)(2,1)S(1)}, u32[]{:S(2)}, u32[]{:S(2)}) collective-permute-start(bf16[2,4,128,128]{3,2,1,0:T(8,128)(2,1)} %get-tuple-element.51), channel_id=1, source_target_pairs={{4,0},{8,4},{12,8},{5,1},{9,5},{13,9},{6,2},{10,6},{14,10},{7,3},{... | collective-permute-start | bytes 786440 | tf_op jit(solution)/shard_map/ppermute | solution.py:477
  30.1 1.6 %collective-permute-start.7 = (bf16[2,2,128,128]{3,2,1,0:T(8,128)(2,1)S(1)}, bf16[2,2,128,128]{3,2,1,0:T(8,128)(2,1)S(1)}, u32[]{:S(2)}, u32[]{:S(2)}) collective-permute-start(bf16[2,2,128,128]{3,2,1,0:T(8,128)(2,1)S(1)} %pad_maximum_fusion), channel_id=1, source_target_pairs={{0,2},{1,3},{2,0},{3,1},{4,6},{5,7},{6,4},{7,5},{8,10},{9,11},{10,... | collective-permute-start | bytes 393224 | tf_op jit(solution)/shard_map/ppermute | solution.py:455
  31.7 0.6 shard_map.108
  32.3 1.0 %shard_map.109 = (bf16[2,6,128,128]{3,2,1,0:T(8,128)(2,1)S(1)}, bf16[2,6,128,128]{3,2,1,0:T(8,128)(2,1)S(1)}, f32[8,128,128]{2,1,0:T(8,128)S(1)}) custom-call(bf16[2,30,128,128]{3,2,1,0:T(8,128)(2,1)S(1)} %get-tuple-element.43.own_l, bf16[2,30,128,128]{3,2,1,0:T(8,128)(2,1)S(1)} %get-tuple-element.44.own_r, ...), custom_call_target="tpu_custom_call" | custom-call | flops 100663296 | bytes 786432 | tf_op jit(solution)/shard_map/pallas_call | solution.py:331
  33.3 18.3 %collective-permute-done.2.got_l = bf16[2,20,128,128]{3,2,1,0:T(8,128)(2,1)S(1)} collective-permute-done((bf16[2,20,128,128]{3,2,1,0:T(8,128)(2,1)}, bf16[2,20,128,128]{3,2,1,0:T(8,128)(2,1)S(1)}, u32[]{:S(2)}, u32[]{:S(2)}) %collective-permute-start.2) | collective-permute-done | bytes 1310752 | tf_op jit(solution)/shard_map/ppermute | solution.py:477
  51.6 4.4 %collective-permute-done.3.got_r = bf16[2,20,128,128]{3,2,1,0:T(8,128)(2,1)S(1)} collective-permute-done((bf16[2,20,128,128]{3,2,1,0:T(8,128)(2,1)}, bf16[2,20,128,128]{3,2,1,0:T(8,128)(2,1)S(1)}, u32[]{:S(2)}, u32[]{:S(2)}) %collective-permute-start.3) | collective-permute-done | bytes 1310752 | tf_op jit(solution)/shard_map/ppermute | solution.py:477
  56.0 1.8 %shard_map.110 = (bf16[2,20,128,128]{3,2,1,0:T(8,128)(2,1)S(1)}, bf16[2,20,128,128]{3,2,1,0:T(8,128)(2,1)S(1)}, f32[8,128,128]{2,1,0:T(8,128)S(1)}) custom-call(bf16[2,30,128,128]{3,2,1,0:T(8,128)(2,1)S(1)} %get-tuple-element.43.own_l, bf16[2,30,128,128]{3,2,1,0:T(8,128)(2,1)S(1)} %get-tuple-element.44.own_r, ...), custom_call_target="tpu_custom_call" | custom-call | flops 335544320 | bytes 2621440 | tf_op jit(solution)/shard_map/pallas_call | solution.py:331
  57.8 1.7 %collective-permute-done.5.got_r = bf16[2,4,128,128]{3,2,1,0:T(8,128)(2,1)S(1)} collective-permute-done((bf16[2,4,128,128]{3,2,1,0:T(8,128)(2,1)}, bf16[2,4,128,128]{3,2,1,0:T(8,128)(2,1)S(1)}, u32[]{:S(2)}, u32[]{:S(2)}) %collective-permute-start.5) | collective-permute-done | bytes 262176 | tf_op jit(solution)/shard_map/ppermute | solution.py:477
  59.6 1.1 %shard_map.111 = (bf16[2,4,128,128]{3,2,1,0:T(8,128)(2,1)S(1)}, bf16[2,4,128,128]{3,2,1,0:T(8,128)(2,1)S(1)}, bf16[528,128]{1,0:T(8,128)(2,1)S(1)}, f32[4,128,12...) custom-call(bf16[2,30,128,128]{3,2,1,0:T(8,128)(2,1)S(1)} %get-tuple-element.43.own_l, ...), custom_call_target="tpu_custom_call" | custom-call | flops 67108864 | bytes 524288 | tf_op jit(solution)/shard_map/pallas_call | solution.py:331
  60.7 0.0 collective-permute-start.8
  60.7 1.3 %collective-permute-done.8.got = bf16[528,128]{1,0:T(8,128)(2,1)S(1)} collective-permute-done((bf16[528,128]{1,0:T(8,128)(2,1)S(1)}, bf16[528,128]{1,0:T(8,128)(2,1)S(1)}, u32[]{:S(2)}, u32[]{:S(2)}) %collective-permute-start.8) | collective-permute-done | bytes 135200 | tf_op jit(solution)/shard_map/ppermute | solution.py:376
  62.1 0.1 shard_map.112
  62.1 1.6 %collective-permute-start.9 = (bf16[272,128]{1,0:T(8,128)(2,1)S(1)}, bf16[272,128]{1,0:T(8,128)(2,1)S(1)}, u32[]{:S(2)}, u32[]{:S(2)}) collective-permute-start(bf16[272,128]{1,0:T(8,128)(2,1)S(1)} %get-tuple-element.61), channel_id=1, source_target_pairs={{0,2},{1,3},{2,0},{3,1},{4,6},{5,7},{6,4},{7,5},{8,10},{9,11},{10,... | collective-permute-start | bytes 208904 | tf_op jit(solution)/shard_map/ppermute | solution.py:376
  63.7 2.8 %collective-permute-done.9.rest_12_ = bf16[272,128]{1,0:T(8,128)(2,1)S(1)} collective-permute-done((bf16[272,128]{1,0:T(8,128)(2,1)S(1)}, bf16[272,128]{1,0:T(8,128)(2,1)S(1)}, u32[]{:S(2)}, u32[]{:S(2)}) %collective-permute-start.9) | collective-permute-done | bytes 69664 | tf_op jit(solution)/shard_map/ppermute | solution.py:376
  66.5 2.7 %shard_map.113 = (bf16[1,2,128,128]{3,2,1,0:T(8,128)(2,1)}, bf16[2,128,128]{2,1,0:T(8,128)(2,1)S(1)}, bf16[528,128]{1,0:T(8,128)(2,1)S(1)}, f32[4,128,128]{2,1,0:T(8,128)S(1)}, f32[8,128]{1,0:T(8,128)S(1)}) custom-call(bf16[2,6,128,128]{3,2,1,0:T(8,128)(2,1)S(1)} %get-tuple-element.45.rest_0_, bf16[2,20,128,128]{3,2,1,0:T(8,128)(2,1)S(1)} %get-tuple-element.49.rest_1_, ...), custom_call_target="tpu_custom_call" | custom-call | flops 503316480 | bytes 3932160 | tf_op jit(solution)/shard_map/pallas_call | solution.py:420
  69.3 1.4 %collective-permute-done.10.got = bf16[528,128]{1,0:T(8,128)(2,1)S(1)} collective-permute-done((bf16[528,128]{1,0:T(8,128)(2,1)S(1)}, bf16[528,128]{1,0:T(8,128)(2,1)S(1)}, u32[]{:S(2)}, u32[]{:S(2)}) %collective-permute-start.10) | collective-permute-done | bytes 135200 | tf_op jit(solution)/shard_map/ppermute | solution.py:376
  70.6 0.1 shard_map.114
  70.7 1.6 %collective-permute-start.11 = (bf16[272,128]{1,0:T(8,128)(2,1)S(1)}, bf16[272,128]{1,0:T(8,128)(2,1)S(1)}, u32[]{:S(2)}, u32[]{:S(2)}) collective-permute-start(bf16[272,128]{1,0:T(8,128)(2,1)S(1)} %get-tuple-element.70), channel_id=1, source_target_pairs={{0,2},{1,3},{2,0},{3,1},{4,6},{5,7},{6,4},{7,5},{8,10},{9,11},{10,... | collective-permute-start | bytes 208904 | tf_op jit(solution)/shard_map/ppermute | solution.py:376
  72.3 2.8 %collective-permute-done.11.got = bf16[272,128]{1,0:T(8,128)(2,1)S(1)} collective-permute-done((bf16[272,128]{1,0:T(8,128)(2,1)S(1)}, bf16[272,128]{1,0:T(8,128)(2,1)S(1)}, u32[]{:S(2)}, u32[]{:S(2)}) %collective-permute-start.11) | collective-permute-done | bytes 69664 | tf_op jit(solution)/shard_map/ppermute | solution.py:376
  75.1 1.3 %shard_map.115 = bf16[1,2,128,128]{3,2,1,0:T(8,128)(2,1)} custom-call(bf16[2,128,128]{2,1,0:T(8,128)(2,1)S(1)} %get-tuple-element.65.resid, f32[1,2]{1,0:T(1,128)S(1)} %copy-done.6, s32[2]{0:T(128)S(1)} %copy-done.5, f32[2,128,128]{2,1,0:T(8,128)S(1)} %get-tuple-element.69.keep, bf16[272,128]{1,0:T(8,128)(2,1)S(1)} %collective-permute-done.11.got, ...), custom_call_target="tpu_custom_call" | custom-call | bytes 262144 | tf_op jit(solution)/shard_map/pallas_call | solution.py:443
  (19 shorter events, 0.1 us)
Async XLA Ops:
  4.2 19.3 %collective-permute-start = (bf16[2,6,128,128]{3,2,1,0:T(8,128)(2,1)}, bf16[2,6,128,128]{3,2,1,0:T(8,128)(2,1)S(1)}, u32[]{:S(2)}, u32[]{:S(2)}) collective-permute-start(bf16[2,6,128,128]{3,2,1,0:T(8,128)(2,1)} %get-tuple-element.40), channel_id=1, source_target_pairs={{0,4},{4,8},{8,12},{1,5},{5,9},{9,13},{2,6},{6,10},{10,14},{3,7},{... | collective-permute-start | bytes 1179656 | tf_op jit(solution)/shard_map/ppermute | solution.py:477
  9.1 14.4 %collective-permute-start.1 = (bf16[2,6,128,128]{3,2,1,0:T(8,128)(2,1)}, bf16[2,6,128,128]{3,2,1,0:T(8,128)(2,1)S(1)}, u32[]{:S(2)}, u32[]{:S(2)}) collective-permute-start(bf16[2,6,128,128]{3,2,1,0:T(8,128)(2,1)} %get-tuple-element.41), channel_id=1, source_target_pairs={{4,0},{8,4},{12,8},{5,1},{9,5},{13,9},{6,2},{10,6},{14,10},{7,3},{... | collective-permute-start | bytes 1179656 | tf_op jit(solution)/shard_map/ppermute | solution.py:477
  10.4 21.2 %copy-start = (bf16[1,2,30,128,128]{4,3,2,1,0:T(8,128)(2,1)S(1)}, bf16[1,2,30,128,128]{4,3,2,1,0:T(8,128)(2,1)}, u32[]{:S(2)}) copy-start(bf16[1,2,30,128,128]{4,3,2,1,0:T(8,128)(2,1)} %left_hbm.5) | copy-start | bytes 5898244
  10.5 21.2 %copy-start.1 = (bf16[1,2,30,128,128]{4,3,2,1,0:T(8,128)(2,1)S(1)}, bf16[1,2,30,128,128]{4,3,2,1,0:T(8,128)(2,1)}, u32[]{:S(2)}) copy-start(bf16[1,2,30,128,128]{4,3,2,1,0:T(8,128)(2,1)} %right_hbm.5) | copy-start | bytes 5898244
  17.4 6.1 %copy-start.2 = (bf16[1,2,128,128]{3,2,1,0:T(8,128)(2,1)S(1)}, bf16[1,2,128,128]{3,2,1,0:T(8,128)(2,1)}, u32[]{:S(2)}) copy-start(bf16[1,2,128,128]{3,2,1,0:T(8,128)(2,1)} %wave.1) | copy-start | bytes 196612
  17.4 6.1 %copy-start.5 = (s32[2]{0:T(128)S(1)}, s32[2]{0:T(128)}, u32[]{:S(2)}) copy-start(s32[2]{0:T(128)} %sizes.3) | copy-start | bytes 28
  17.4 34.2 %collective-permute-start.2 = (bf16[2,20,128,128]{3,2,1,0:T(8,128)(2,1)}, bf16[2,20,128,128]{3,2,1,0:T(8,128)(2,1)S(1)}, u32[]{:S(2)}, u32[]{:S(2)}) collective-permute-start(bf16[2,20,128,128]{3,2,1,0:T(8,128)(2,1)} %get-tuple-element.46), channel_id=1, source_target_pairs={{0,4},{4,8},{8,12},{1,5},{5,9},{9,13},{2,6},{6,10},{10,14},{3,7},{... | collective-permute-start | bytes 3932168 | tf_op jit(solution)/shard_map/ppermute | solution.py:477
  22.2 33.8 %collective-permute-start.3 = (bf16[2,20,128,128]{3,2,1,0:T(8,128)(2,1)}, bf16[2,20,128,128]{3,2,1,0:T(8,128)(2,1)S(1)}, u32[]{:S(2)}, u32[]{:S(2)}) collective-permute-start(bf16[2,20,128,128]{3,2,1,0:T(8,128)(2,1)} %get-tuple-element.47), channel_id=1, source_target_pairs={{4,0},{8,4},{12,8},{5,1},{9,5},{13,9},{6,2},{10,6},{14,10},{7,3},{... | collective-permute-start | bytes 3932168 | tf_op jit(solution)/shard_map/ppermute | solution.py:477
  24.1 6.0 %collective-permute-start.6 = (bf16[1,2,128,128]{3,2,1,0:T(8,128)(2,1)S(1)}, bf16[1,2,128,128]{3,2,1,0:T(8,128)(2,1)S(1)}, u32[]{:S(2)}, u32[]{:S(2)}) collective-permute-start(bf16[1,2,128,128]{3,2,1,0:T(8,128)(2,1)S(1)} %bitcast.1), channel_id=1, source_target_pairs={{0,1},{1,0},{2,3},{3,2},{4,5},{5,4},{6,7},{7,6},{8,9},{9,8},{10,11... | collective-permute-start | bytes 196616 | tf_op jit(solution)/shard_map/ppermute | solution.py:455
  24.2 33.6 %collective-permute-start.4 = (bf16[2,4,128,128]{3,2,1,0:T(8,128)(2,1)}, bf16[2,4,128,128]{3,2,1,0:T(8,128)(2,1)S(1)}, u32[]{:S(2)}, u32[]{:S(2)}) collective-permute-start(bf16[2,4,128,128]{3,2,1,0:T(8,128)(2,1)} %get-tuple-element.50), channel_id=1, source_target_pairs={{0,4},{4,8},{8,12},{1,5},{5,9},{9,13},{2,6},{6,10},{10,14},{3,7},{... | collective-permute-start | bytes 786440 | tf_op jit(solution)/shard_map/ppermute | solution.py:477
  28.8 30.8 %collective-permute-start.5 = (bf16[2,4,128,128]{3,2,1,0:T(8,128)(2,1)}, bf16[2,4,128,128]{3,2,1,0:T(8,128)(2,1)S(1)}, u32[]{:S(2)}, u32[]{:S(2)}) collective-permute-start(bf16[2,4,128,128]{3,2,1,0:T(8,128)(2,1)} %get-tuple-element.51), channel_id=1, source_target_pairs={{4,0},{8,4},{12,8},{5,1},{9,5},{13,9},{6,2},{10,6},{14,10},{7,3},{... | collective-permute-start | bytes 786440 | tf_op jit(solution)/shard_map/ppermute | solution.py:477
  30.1 2.2 %copy-start.3 = (f32[1,2,30]{2,1,0:T(2,128)S(1)}, f32[1,2,30]{2,1,0:T(2,128)}, u32[]{:S(2)}) copy-start(f32[1,2,30]{2,1,0:T(2,128)} %rest_7_.1) | copy-start | bytes 724
  30.1 2.2 %copy-start.4 = (s32[1,2,30]{2,1,0:T(2,128)S(1)}, s32[1,2,30]{2,1,0:T(2,128)}, u32[]{:S(2)}) copy-start(s32[1,2,30]{2,1,0:T(2,128)} %rest_8_.1) | copy-start | bytes 724
  30.1 27.7 %collective-permute-start.7 = (bf16[2,2,128,128]{3,2,1,0:T(8,128)(2,1)S(1)}, bf16[2,2,128,128]{3,2,1,0:T(8,128)(2,1)S(1)}, u32[]{:S(2)}, u32[]{:S(2)}) collective-permute-start(bf16[2,2,128,128]{3,2,1,0:T(8,128)(2,1)S(1)} %pad_maximum_fusion), channel_id=1, source_target_pairs={{0,2},{1,3},{2,0},{3,1},{4,6},{5,7},{6,4},{7,5},{8,10},{9,11},{10,... | collective-permute-start | bytes 393224 | tf_op jit(solution)/shard_map/ppermute | solution.py:455
  56.0 3.6 %copy-start.6 = (f32[1,2]{1,0:T(1,128)S(1)}, f32[1,2]{1,0:T(1,128)}, u32[]{:S(2)}) copy-start(f32[1,2]{1,0:T(1,128)} %onsite.1) | copy-start | bytes 28
  60.7 1.4 %collective-permute-start.8 = (bf16[528,128]{1,0:T(8,128)(2,1)S(1)}, bf16[528,128]{1,0:T(8,128)(2,1)S(1)}, u32[]{:S(2)}, u32[]{:S(2)}) collective-permute-start(bf16[528,128]{1,0:T(8,128)(2,1)S(1)} %get-tuple-element.58), channel_id=1, source_target_pairs={{0,1},{1,0},{2,3},{3,2},{4,5},{5,4},{6,7},{7,6},{8,9},{9,8},{10,11... | collective-permute-start | bytes 405512 | tf_op jit(solution)/shard_map/ppermute | solution.py:376
  62.1 4.4 %collective-permute-start.9 = (bf16[272,128]{1,0:T(8,128)(2,1)S(1)}, bf16[272,128]{1,0:T(8,128)(2,1)S(1)}, u32[]{:S(2)}, u32[]{:S(2)}) collective-permute-start(bf16[272,128]{1,0:T(8,128)(2,1)S(1)} %get-tuple-element.61), channel_id=1, source_target_pairs={{0,2},{1,3},{2,0},{3,1},{4,6},{5,7},{6,4},{7,5},{8,10},{9,11},{10,... | collective-permute-start | bytes 208904 | tf_op jit(solution)/shard_map/ppermute | solution.py:376
  69.3 1.4 %collective-permute-start.10 = (bf16[528,128]{1,0:T(8,128)(2,1)S(1)}, bf16[528,128]{1,0:T(8,128)(2,1)S(1)}, u32[]{:S(2)}, u32[]{:S(2)}) collective-permute-start(bf16[528,128]{1,0:T(8,128)(2,1)S(1)} %get-tuple-element.67), channel_id=1, source_target_pairs={{0,1},{1,0},{2,3},{3,2},{4,5},{5,4},{6,7},{7,6},{8,9},{9,8},{10,11... | collective-permute-start | bytes 405512 | tf_op jit(solution)/shard_map/ppermute | solution.py:376
  70.7 4.4 %collective-permute-start.11 = (bf16[272,128]{1,0:T(8,128)(2,1)S(1)}, bf16[272,128]{1,0:T(8,128)(2,1)S(1)}, u32[]{:S(2)}, u32[]{:S(2)}) collective-permute-start(bf16[272,128]{1,0:T(8,128)(2,1)S(1)} %get-tuple-element.70), channel_id=1, source_target_pairs={{0,2},{1,3},{2,0},{3,1},{4,6},{5,7},{6,4},{7,5},{8,10},{9,11},{10,... | collective-permute-start | bytes 208904 | tf_op jit(solution)/shard_map/ppermute | solution.py:376

commit v4 on v3

--- a/solution.py
+++ b/solution.py
@@ -42,7 +42,7 @@
 
 
 def chunk_sizes(channels):
-    first, last = max(1, channels // 5), max(1, channels * 2 // 15)
+    first, last = max(1, channels * 3 // 10), max(1, channels // 10)
     return [c for c in (first, channels - first - last, last) if c > 0]
 
 

time: 76.6 us -> 72.8 us (0.950)
  waiting for transfers between devices: 32.8 us -> 30.3 us
  starting transfers between devices: 23 us -> 21.9 us
    ppermute x3, waiting for transfers between devices: 18.3 us -> 12.8 us  [pass_on(): lax.ppermute(grown[0], 'section', up)]
    ppermute x3, waiting for transfers between devices: 6.1 us -> 9.17 us  [pass_on(): lax.ppermute(grown[1], 'section', down)]
    ppermute x3, starting transfers between devices: 14.3 us -> 13.3 us  [pass_on(): lax.ppermute(grown[0], 'section', up)]
  transfers between devices with their start and end apart: 12 -> 12, of which waited for: 7 -> 8; matrix products, arithmetic and copies ran while one was open for 0% -> 0% of each run, Pallas kernels for 14% -> 14%
where the time goes in v4:
time: 72.8 us; the launch traced here: 72.5 us
  waiting for transfers between devices  30.3 us (42%)
  starting transfers between devices  21.9 us (30%)
  Pallas kernels  19.4 us (27%)
  between operations  0.86 us (1%)
    ppermute x3, starting transfers between devices, pass_on(): lax.ppermute(grown[0], 'section', up)  13.3 us
    ppermute x3, waiting for transfers between devices, pass_on(): lax.ppermute(grown[0], 'section', up)  12.8 us
    pallas_call x2, Pallas kernels, grow(): call(functools.partial(grow_kernel, bounds), [jax.ShapeDtypeStruct((8, 12...  10.2 us
    ppermute x3, waiting for transfers between devices, pass_on(): lax.ppermute(grown[1], 'section', down)  9.17 us
    ppermute x4, waiting for transfers between devices, exchange(): lax.ppermute(send, 'sector', [(i, i ^ 1 << stage) for i in range(sectors)])  8.33 us
    pallas_call x3, Pallas kernels, first_apply(): call(functools.partial(first_kernel, chunk, is_first, is_last, groups, ch...  3.93 us
    ppermute x3, starting transfers between devices, pass_on(): lax.ppermute(grown[1], 'section', down)  3.88 us
    ppermute x4, starting transfers between devices, exchange(): lax.ppermute(send, 'sector', [(i, i ^ 1 << stage) for i in range(sectors)])  3.15 us
  transfers between devices with their start and end apart: 12, of which 8 were waited for; matrix products, arithmetic and copies ran while one was open for 0% of the time, Pallas kernels for 14%

profile of v4, /device:TPU:0, one launch (start us, length us, event | category | flops | bytes accessed | tf_op | source)
XLA Modules:
  0.0 72.5 jit_solution(13544685375000755626)
XLA Ops:
  0.6 3.8 %shard_map.104 = (f32[8,128]{1,0:T(8,128)}, bf16[2,9,128,128]{3,2,1,0:T(8,128)(2,1)}, bf16[2,9,128,128]{3,2,1,0:T(8,128)(2,1)}) custom-call(bf16[1,2,30,128,128]{4,3,2,1,0:T(8,128)(2,1)} %left_hbm.5, bf16[1,2,30,128,128]{4,3,2,1,0:T(8,128)(2,1)} %right_hbm.5, bf16[1,2,128,128]{3,2,1,0:T(8,128)(2,1)} %edge_l_hbm.3, bf16[1,2,128,128]{3,2,1,0:T(8,128)(2,1)} %edge_r_hbm.3), custom_call_target="tpu_custom_call" | custom-call | flops 301989888 | bytes 2359296 | tf_op jit(solution)/shard_map/pallas_call | solution.py:119
  4.4 5.0 %collective-permute-start = (bf16[2,9,128,128]{3,2,1,0:T(8,128)(2,1)}, bf16[2,9,128,128]{3,2,1,0:T(8,128)(2,1)S(1)}, u32[]{:S(2)}, u32[]{:S(2)}) collective-permute-start(bf16[2,9,128,128]{3,2,1,0:T(8,128)(2,1)} %get-tuple-element.40), channel_id=1, source_target_pairs={{0,4},{4,8},{8,12},{1,5},{5,9},{9,13},{2,6},{6,10},{10,14},{3,7},{... | collective-permute-start | bytes 1769480 | tf_op jit(solution)/shard_map/ppermute | solution.py:477
  9.4 1.3 %collective-permute-start.1 = (bf16[2,9,128,128]{3,2,1,0:T(8,128)(2,1)}, bf16[2,9,128,128]{3,2,1,0:T(8,128)(2,1)S(1)}, u32[]{:S(2)}, u32[]{:S(2)}) collective-permute-start(bf16[2,9,128,128]{3,2,1,0:T(8,128)(2,1)} %get-tuple-element.41), channel_id=1, source_target_pairs={{4,0},{8,4},{12,8},{5,1},{9,5},{13,9},{6,2},{10,6},{14,10},{7,3},{... | collective-permute-start | bytes 1769480 | tf_op jit(solution)/shard_map/ppermute | solution.py:477
  10.7 0.0 copy-start.2
  10.7 6.4 %shard_map.105 = (f32[8,128]{1,0:T(8,128)}, bf16[2,18,128,128]{3,2,1,0:T(8,128)(2,1)}, bf16[2,18,128,128]{3,2,1,0:T(8,128)(2,1)}, bf16[2,3,128,128]{3,2,1,0:T(8,128)(2,1)}, bf16[2,3,128,128]{3,2,1,0:T(8,128)(2,1)}) custom-call(bf16[1,2,30,128,128]{4,3,2,1,0:T(8,128)(2,1)} %left_hbm.5, bf16[1,2,30,128,128]{4,3,2,1,0:T(8,128)(2,1)} %right_hbm.5, ...), custom_call_target="tpu_custom_call" | custom-call | flops 704643072 | bytes 5505024 | tf_op jit(solution)/shard_map/pallas_call | solution.py:119
  17.1 0.0 copy-start
  17.1 4.8 %collective-permute-start.2 = (bf16[2,18,128,128]{3,2,1,0:T(8,128)(2,1)}, bf16[2,18,128,128]{3,2,1,0:T(8,128)(2,1)S(1)}, u32[]{:S(2)}, u32[]{:S(2)}) collective-permute-start(bf16[2,18,128,128]{3,2,1,0:T(8,128)(2,1)} %get-tuple-element.46), channel_id=1, source_target_pairs={{0,4},{4,8},{8,12},{1,5},{5,9},{9,13},{2,6},{6,10},{10,14},{3,7},{... | collective-permute-start | bytes 3538952 | tf_op jit(solution)/shard_map/ppermute | solution.py:477
  21.9 1.3 %collective-permute-start.3 = (bf16[2,18,128,128]{3,2,1,0:T(8,128)(2,1)}, bf16[2,18,128,128]{3,2,1,0:T(8,128)(2,1)S(1)}, u32[]{:S(2)}, u32[]{:S(2)}) collective-permute-start(bf16[2,18,128,128]{3,2,1,0:T(8,128)(2,1)} %get-tuple-element.47), channel_id=1, source_target_pairs={{4,0},{8,4},{12,8},{5,1},{9,5},{13,9},{6,2},{10,6},{14,10},{7,3},{... | collective-permute-start | bytes 3538952 | tf_op jit(solution)/shard_map/ppermute | solution.py:477
  23.2 3.7 %collective-permute-done.1.refs_3_.got_r = bf16[2,9,128,128]{3,2,1,0:T(8,128)(2,1)S(1)} collective-permute-done((bf16[2,9,128,128]{3,2,1,0:T(8,128)(2,1)}, bf16[2,9,128,128]{3,2,1,0:T(8,128)(2,1)S(1)}, u32[]{:S(2)}, u32[]{:S(2)}) %collective-permute-start.1) | collective-permute-done | bytes 589856 | tf_op jit(solution)/shard_map/ppermute | solution.py:477
  26.9 0.6 shard_map.107.after.m.rest_6_
  27.5 0.1 collective-permute-start.6
  27.6 3.5 %collective-permute-start.4 = (bf16[2,3,128,128]{3,2,1,0:T(8,128)(2,1)}, bf16[2,3,128,128]{3,2,1,0:T(8,128)(2,1)S(1)}, u32[]{:S(2)}, u32[]{:S(2)}) collective-permute-start(bf16[2,3,128,128]{3,2,1,0:T(8,128)(2,1)} %get-tuple-element.50), channel_id=1, source_target_pairs={{0,4},{4,8},{8,12},{1,5},{5,9},{9,13},{2,6},{6,10},{10,14},{3,7},{... | collective-permute-start | bytes 589832 | tf_op jit(solution)/shard_map/ppermute | solution.py:477
  31.1 1.3 %collective-permute-start.5 = (bf16[2,3,128,128]{3,2,1,0:T(8,128)(2,1)}, bf16[2,3,128,128]{3,2,1,0:T(8,128)(2,1)S(1)}, u32[]{:S(2)}, u32[]{:S(2)}) collective-permute-start(bf16[2,3,128,128]{3,2,1,0:T(8,128)(2,1)} %get-tuple-element.51), channel_id=1, source_target_pairs={{4,0},{8,4},{12,8},{5,1},{9,5},{13,9},{6,2},{10,6},{14,10},{7,3},{... | collective-permute-start | bytes 589832 | tf_op jit(solution)/shard_map/ppermute | solution.py:477
  32.5 1.5 %collective-permute-start.7 = (bf16[2,2,128,128]{3,2,1,0:T(8,128)(2,1)S(1)}, bf16[2,2,128,128]{3,2,1,0:T(8,128)(2,1)S(1)}, u32[]{:S(2)}, u32[]{:S(2)}) collective-permute-start(bf16[2,2,128,128]{3,2,1,0:T(8,128)(2,1)S(1)} %pad_maximum_fusion), channel_id=1, source_target_pairs={{0,2},{1,3},{2,0},{3,1},{4,6},{5,7},{6,4},{7,5},{8,10},{9,11},{10,... | collective-permute-start | bytes 393224 | tf_op jit(solution)/shard_map/ppermute | solution.py:455
  34.0 0.6 shard_map.108
  34.6 1.1 %shard_map.109 = (bf16[2,9,128,128]{3,2,1,0:T(8,128)(2,1)S(1)}, bf16[2,9,128,128]{3,2,1,0:T(8,128)(2,1)S(1)}, f32[8,128,128]{2,1,0:T(8,128)S(1)}) custom-call(bf16[2,30,128,128]{3,2,1,0:T(8,128)(2,1)S(1)} %get-tuple-element.43.own_l, bf16[2,30,128,128]{3,2,1,0:T(8,128)(2,1)S(1)} %get-tuple-element.44.own_r, ...), custom_call_target="tpu_custom_call" | custom-call | flops 150994944 | bytes 1179648 | tf_op jit(solution)/shard_map/pallas_call | solution.py:331
  35.7 12.8 %collective-permute-done.2.got_l = bf16[2,18,128,128]{3,2,1,0:T(8,128)(2,1)S(1)} collective-permute-done((bf16[2,18,128,128]{3,2,1,0:T(8,128)(2,1)}, bf16[2,18,128,128]{3,2,1,0:T(8,128)(2,1)S(1)}, u32[]{:S(2)}, u32[]{:S(2)}) %collective-permute-start.2) | collective-permute-done | bytes 1179680 | tf_op jit(solution)/shard_map/ppermute | solution.py:477
  48.5 4.4 %collective-permute-done.3.got_r = bf16[2,18,128,128]{3,2,1,0:T(8,128)(2,1)S(1)} collective-permute-done((bf16[2,18,128,128]{3,2,1,0:T(8,128)(2,1)}, bf16[2,18,128,128]{3,2,1,0:T(8,128)(2,1)S(1)}, u32[]{:S(2)}, u32[]{:S(2)}) %collective-permute-start.3) | collective-permute-done | bytes 1179680 | tf_op jit(solution)/shard_map/ppermute | solution.py:477
  52.9 1.7 %shard_map.110 = (bf16[2,18,128,128]{3,2,1,0:T(8,128)(2,1)S(1)}, bf16[2,18,128,128]{3,2,1,0:T(8,128)(2,1)S(1)}, f32[8,128,128]{2,1,0:T(8,128)S(1)}) custom-call(bf16[2,30,128,128]{3,2,1,0:T(8,128)(2,1)S(1)} %get-tuple-element.43.own_l, bf16[2,30,128,128]{3,2,1,0:T(8,128)(2,1)S(1)} %get-tuple-element.44.own_r, ...), custom_call_target="tpu_custom_call" | custom-call | flops 301989888 | bytes 2359296 | tf_op jit(solution)/shard_map/pallas_call | solution.py:331
  54.7 1.1 %collective-permute-done.5.got_r = bf16[2,3,128,128]{3,2,1,0:T(8,128)(2,1)S(1)} collective-permute-done((bf16[2,3,128,128]{3,2,1,0:T(8,128)(2,1)}, bf16[2,3,128,128]{3,2,1,0:T(8,128)(2,1)S(1)}, u32[]{:S(2)}, u32[]{:S(2)}) %collective-permute-start.5) | collective-permute-done | bytes 196640 | tf_op jit(solution)/shard_map/ppermute | solution.py:477
  55.8 1.1 %shard_map.111 = (bf16[2,3,128,128]{3,2,1,0:T(8,128)(2,1)S(1)}, bf16[2,3,128,128]{3,2,1,0:T(8,128)(2,1)S(1)}, bf16[528,128]{1,0:T(8,128)(2,1)S(1)}, f32[4,128,12...) custom-call(bf16[2,30,128,128]{3,2,1,0:T(8,128)(2,1)S(1)} %get-tuple-element.43.own_l, ...), custom_call_target="tpu_custom_call" | custom-call | flops 50331648 | bytes 393216 | tf_op jit(solution)/shard_map/pallas_call | solution.py:331
  56.8 0.0 collective-permute-start.8
  56.9 1.3 %collective-permute-done.8.got = bf16[528,128]{1,0:T(8,128)(2,1)S(1)} collective-permute-done((bf16[528,128]{1,0:T(8,128)(2,1)S(1)}, bf16[528,128]{1,0:T(8,128)(2,1)S(1)}, u32[]{:S(2)}, u32[]{:S(2)}) %collective-permute-start.8) | collective-permute-done | bytes 135200 | tf_op jit(solution)/shard_map/ppermute | solution.py:376
  58.2 0.1 shard_map.112
  58.3 1.6 %collective-permute-start.9 = (bf16[272,128]{1,0:T(8,128)(2,1)S(1)}, bf16[272,128]{1,0:T(8,128)(2,1)S(1)}, u32[]{:S(2)}, u32[]{:S(2)}) collective-permute-start(bf16[272,128]{1,0:T(8,128)(2,1)S(1)} %get-tuple-element.61), channel_id=1, source_target_pairs={{0,2},{1,3},{2,0},{3,1},{4,6},{5,7},{6,4},{7,5},{8,10},{9,11},{10,... | collective-permute-start | bytes 208904 | tf_op jit(solution)/shard_map/ppermute | solution.py:376
  59.9 2.8 %collective-permute-done.9.rest_12_ = bf16[272,128]{1,0:T(8,128)(2,1)S(1)} collective-permute-done((bf16[272,128]{1,0:T(8,128)(2,1)S(1)}, bf16[272,128]{1,0:T(8,128)(2,1)S(1)}, u32[]{:S(2)}, u32[]{:S(2)}) %collective-permute-start.9) | collective-permute-done | bytes 69664 | tf_op jit(solution)/shard_map/ppermute | solution.py:376
  62.7 2.8 %shard_map.113 = (bf16[1,2,128,128]{3,2,1,0:T(8,128)(2,1)}, bf16[2,128,128]{2,1,0:T(8,128)(2,1)S(1)}, bf16[528,128]{1,0:T(8,128)(2,1)S(1)}, f32[4,128,128]{2,1,0:T(8,128)S(1)}, f32[8,128]{1,0:T(8,128)S(1)}) custom-call(bf16[2,9,128,128]{3,2,1,0:T(8,128)(2,1)S(1)} %get-tuple-element.45.rest_0_, bf16[2,18,128,128]{3,2,1,0:T(8,128)(2,1)S(1)} %get-tuple-element.49.rest_1_, ...), custom_call_target="tpu_custom_call" | custom-call | flops 503316480 | bytes 3932160 | tf_op jit(solution)/shard_map/pallas_call | solution.py:420
  65.5 1.4 %collective-permute-done.10.got = bf16[528,128]{1,0:T(8,128)(2,1)S(1)} collective-permute-done((bf16[528,128]{1,0:T(8,128)(2,1)S(1)}, bf16[528,128]{1,0:T(8,128)(2,1)S(1)}, u32[]{:S(2)}, u32[]{:S(2)}) %collective-permute-start.10) | collective-permute-done | bytes 135200 | tf_op jit(solution)/shard_map/ppermute | solution.py:376
  66.8 0.1 shard_map.114
  66.9 1.6 %collective-permute-start.11 = (bf16[272,128]{1,0:T(8,128)(2,1)S(1)}, bf16[272,128]{1,0:T(8,128)(2,1)S(1)}, u32[]{:S(2)}, u32[]{:S(2)}) collective-permute-start(bf16[272,128]{1,0:T(8,128)(2,1)S(1)} %get-tuple-element.70), channel_id=1, source_target_pairs={{0,2},{1,3},{2,0},{3,1},{4,6},{5,7},{6,4},{7,5},{8,10},{9,11},{10,... | collective-permute-start | bytes 208904 | tf_op jit(solution)/shard_map/ppermute | solution.py:376
  68.5 2.8 %collective-permute-done.11.got = bf16[272,128]{1,0:T(8,128)(2,1)S(1)} collective-permute-done((bf16[272,128]{1,0:T(8,128)(2,1)S(1)}, bf16[272,128]{1,0:T(8,128)(2,1)S(1)}, u32[]{:S(2)}, u32[]{:S(2)}) %collective-permute-start.11) | collective-permute-done | bytes 69664 | tf_op jit(solution)/shard_map/ppermute | solution.py:376
  71.3 1.3 %shard_map.115 = bf16[1,2,128,128]{3,2,1,0:T(8,128)(2,1)} custom-call(bf16[2,128,128]{2,1,0:T(8,128)(2,1)S(1)} %get-tuple-element.65.resid, f32[1,2]{1,0:T(1,128)S(1)} %copy-done.6, s32[2]{0:T(128)S(1)} %copy-done.5, f32[2,128,128]{2,1,0:T(8,128)S(1)} %get-tuple-element.69.keep, bf16[272,128]{1,0:T(8,128)(2,1)S(1)} %collective-permute-done.11.got, ...), custom_call_target="tpu_custom_call" | custom-call | bytes 262144 | tf_op jit(solution)/shard_map/pallas_call | solution.py:443
  (19 shorter events, 0.1 us)
Async XLA Ops:
  4.4 18.8 %collective-permute-start = (bf16[2,9,128,128]{3,2,1,0:T(8,128)(2,1)}, bf16[2,9,128,128]{3,2,1,0:T(8,128)(2,1)S(1)}, u32[]{:S(2)}, u32[]{:S(2)}) collective-permute-start(bf16[2,9,128,128]{3,2,1,0:T(8,128)(2,1)} %get-tuple-element.40), channel_id=1, source_target_pairs={{0,4},{4,8},{8,12},{1,5},{5,9},{9,13},{2,6},{6,10},{10,14},{3,7},{... | collective-permute-start | bytes 1769480 | tf_op jit(solution)/shard_map/ppermute | solution.py:477
  9.4 17.5 %collective-permute-start.1 = (bf16[2,9,128,128]{3,2,1,0:T(8,128)(2,1)}, bf16[2,9,128,128]{3,2,1,0:T(8,128)(2,1)S(1)}, u32[]{:S(2)}, u32[]{:S(2)}) collective-permute-start(bf16[2,9,128,128]{3,2,1,0:T(8,128)(2,1)} %get-tuple-element.41), channel_id=1, source_target_pairs={{4,0},{8,4},{12,8},{5,1},{9,5},{13,9},{6,2},{10,6},{14,10},{7,3},{... | collective-permute-start | bytes 1769480 | tf_op jit(solution)/shard_map/ppermute | solution.py:477
  10.7 16.2 %copy-start.2 = (bf16[1,2,128,128]{3,2,1,0:T(8,128)(2,1)S(1)}, bf16[1,2,128,128]{3,2,1,0:T(8,128)(2,1)}, u32[]{:S(2)}) copy-start(bf16[1,2,128,128]{3,2,1,0:T(8,128)(2,1)} %wave.1) | copy-start | bytes 196612
  10.7 16.2 %copy-start.5 = (s32[2]{0:T(128)S(1)}, s32[2]{0:T(128)}, u32[]{:S(2)}) copy-start(s32[2]{0:T(128)} %sizes.3) | copy-start | bytes 28
  10.7 23.3 %copy-start.1 = (bf16[1,2,30,128,128]{4,3,2,1,0:T(8,128)(2,1)S(1)}, bf16[1,2,30,128,128]{4,3,2,1,0:T(8,128)(2,1)}, u32[]{:S(2)}) copy-start(bf16[1,2,30,128,128]{4,3,2,1,0:T(8,128)(2,1)} %right_hbm.5) | copy-start | bytes 5898244
  17.1 16.9 %copy-start = (bf16[1,2,30,128,128]{4,3,2,1,0:T(8,128)(2,1)S(1)}, bf16[1,2,30,128,128]{4,3,2,1,0:T(8,128)(2,1)}, u32[]{:S(2)}) copy-start(bf16[1,2,30,128,128]{4,3,2,1,0:T(8,128)(2,1)} %left_hbm.5) | copy-start | bytes 5898244
  17.1 31.4 %collective-permute-start.2 = (bf16[2,18,128,128]{3,2,1,0:T(8,128)(2,1)}, bf16[2,18,128,128]{3,2,1,0:T(8,128)(2,1)S(1)}, u32[]{:S(2)}, u32[]{:S(2)}) collective-permute-start(bf16[2,18,128,128]{3,2,1,0:T(8,128)(2,1)} %get-tuple-element.46), channel_id=1, source_target_pairs={{0,4},{4,8},{8,12},{1,5},{5,9},{9,13},{2,6},{6,10},{10,14},{3,7},{... | collective-permute-start | bytes 3538952 | tf_op jit(solution)/shard_map/ppermute | solution.py:477
  21.9 31.0 %collective-permute-start.3 = (bf16[2,18,128,128]{3,2,1,0:T(8,128)(2,1)}, bf16[2,18,128,128]{3,2,1,0:T(8,128)(2,1)S(1)}, u32[]{:S(2)}, u32[]{:S(2)}) collective-permute-start(bf16[2,18,128,128]{3,2,1,0:T(8,128)(2,1)} %get-tuple-element.47), channel_id=1, source_target_pairs={{4,0},{8,4},{12,8},{5,1},{9,5},{13,9},{6,2},{10,6},{14,10},{7,3},{... | collective-permute-start | bytes 3538952 | tf_op jit(solution)/shard_map/ppermute | solution.py:477
  27.5 4.9 %collective-permute-start.6 = (bf16[1,2,128,128]{3,2,1,0:T(8,128)(2,1)S(1)}, bf16[1,2,128,128]{3,2,1,0:T(8,128)(2,1)S(1)}, u32[]{:S(2)}, u32[]{:S(2)}) collective-permute-start(bf16[1,2,128,128]{3,2,1,0:T(8,128)(2,1)S(1)} %bitcast.1), channel_id=1, source_target_pairs={{0,1},{1,0},{2,3},{3,2},{4,5},{5,4},{6,7},{7,6},{8,9},{9,8},{10,11... | collective-permute-start | bytes 196616 | tf_op jit(solution)/shard_map/ppermute | solution.py:455
  27.6 27.1 %collective-permute-start.4 = (bf16[2,3,128,128]{3,2,1,0:T(8,128)(2,1)}, bf16[2,3,128,128]{3,2,1,0:T(8,128)(2,1)S(1)}, u32[]{:S(2)}, u32[]{:S(2)}) collective-permute-start(bf16[2,3,128,128]{3,2,1,0:T(8,128)(2,1)} %get-tuple-element.50), channel_id=1, source_target_pairs={{0,4},{4,8},{8,12},{1,5},{5,9},{9,13},{2,6},{6,10},{10,14},{3,7},{... | collective-permute-start | bytes 589832 | tf_op jit(solution)/shard_map/ppermute | solution.py:477
  31.1 24.7 %collective-permute-start.5 = (bf16[2,3,128,128]{3,2,1,0:T(8,128)(2,1)}, bf16[2,3,128,128]{3,2,1,0:T(8,128)(2,1)S(1)}, u32[]{:S(2)}, u32[]{:S(2)}) collective-permute-start(bf16[2,3,128,128]{3,2,1,0:T(8,128)(2,1)} %get-tuple-element.51), channel_id=1, source_target_pairs={{4,0},{8,4},{12,8},{5,1},{9,5},{13,9},{6,2},{10,6},{14,10},{7,3},{... | collective-permute-start | bytes 589832 | tf_op jit(solution)/shard_map/ppermute | solution.py:477
  32.4 2.1 %copy-start.3 = (f32[1,2,30]{2,1,0:T(2,128)S(1)}, f32[1,2,30]{2,1,0:T(2,128)}, u32[]{:S(2)}) copy-start(f32[1,2,30]{2,1,0:T(2,128)} %rest_7_.1) | copy-start | bytes 724
  32.5 2.1 %copy-start.4 = (s32[1,2,30]{2,1,0:T(2,128)S(1)}, s32[1,2,30]{2,1,0:T(2,128)}, u32[]{:S(2)}) copy-start(s32[1,2,30]{2,1,0:T(2,128)} %rest_8_.1) | copy-start | bytes 724
  32.5 22.2 %collective-permute-start.7 = (bf16[2,2,128,128]{3,2,1,0:T(8,128)(2,1)S(1)}, bf16[2,2,128,128]{3,2,1,0:T(8,128)(2,1)S(1)}, u32[]{:S(2)}, u32[]{:S(2)}) collective-permute-start(bf16[2,2,128,128]{3,2,1,0:T(8,128)(2,1)S(1)} %pad_maximum_fusion), channel_id=1, source_target_pairs={{0,2},{1,3},{2,0},{3,1},{4,6},{5,7},{6,4},{7,5},{8,10},{9,11},{10,... | collective-permute-start | bytes 393224 | tf_op jit(solution)/shard_map/ppermute | solution.py:455
  52.9 2.9 %copy-start.6 = (f32[1,2]{1,0:T(1,128)S(1)}, f32[1,2]{1,0:T(1,128)}, u32[]{:S(2)}) copy-start(f32[1,2]{1,0:T(1,128)} %onsite.1) | copy-start | bytes 28
  56.8 1.4 %collective-permute-start.8 = (bf16[528,128]{1,0:T(8,128)(2,1)S(1)}, bf16[528,128]{1,0:T(8,128)(2,1)S(1)}, u32[]{:S(2)}, u32[]{:S(2)}) collective-permute-start(bf16[528,128]{1,0:T(8,128)(2,1)S(1)} %get-tuple-element.58), channel_id=1, source_target_pairs={{0,1},{1,0},{2,3},{3,2},{4,5},{5,4},{6,7},{7,6},{8,9},{9,8},{10,11... | collective-permute-start | bytes 405512 | tf_op jit(solution)/shard_map/ppermute | solution.py:376
  58.3 4.4 %collective-permute-start.9 = (bf16[272,128]{1,0:T(8,128)(2,1)S(1)}, bf16[272,128]{1,0:T(8,128)(2,1)S(1)}, u32[]{:S(2)}, u32[]{:S(2)}) collective-permute-start(bf16[272,128]{1,0:T(8,128)(2,1)S(1)} %get-tuple-element.61), channel_id=1, source_target_pairs={{0,2},{1,3},{2,0},{3,1},{4,6},{5,7},{6,4},{7,5},{8,10},{9,11},{10,... | collective-permute-start | bytes 208904 | tf_op jit(solution)/shard_map/ppermute | solution.py:376
  65.5 1.4 %collective-permute-start.10 = (bf16[528,128]{1,0:T(8,128)(2,1)S(1)}, bf16[528,128]{1,0:T(8,128)(2,1)S(1)}, u32[]{:S(2)}, u32[]{:S(2)}) collective-permute-start(bf16[528,128]{1,0:T(8,128)(2,1)S(1)} %get-tuple-element.67), channel_id=1, source_target_pairs={{0,1},{1,0},{2,3},{3,2},{4,5},{5,4},{6,7},{7,6},{8,9},{9,8},{10,11... | collective-permute-start | bytes 405512 | tf_op jit(solution)/shard_map/ppermute | solution.py:376
  66.9 4.4 %collective-permute-start.11 = (bf16[272,128]{1,0:T(8,128)(2,1)S(1)}, bf16[272,128]{1,0:T(8,128)(2,1)S(1)}, u32[]{:S(2)}, u32[]{:S(2)}) collective-permute-start(bf16[272,128]{1,0:T(8,128)(2,1)S(1)} %get-tuple-element.70), channel_id=1, source_target_pairs={{0,2},{1,3},{2,0},{3,1},{4,6},{5,7},{6,4},{7,5},{8,10},{9,11},{10,... | collective-permute-start | bytes 208904 | tf_op jit(solution)/shard_map/ppermute | solution.py:376

commit v5 on v4

--- a/solution.py
+++ b/solution.py
@@ -48,6 +48,10 @@
 
 def unit_of(count, most=11):
     return max(u for u in range(1, most + 1) if count % u == 0)
+
+
+def up_first():
+    return lax.rem(lax.axis_index("sector"), 2) == 0
 
 
 def grow_kernel(bounds, left_hbm, right_hbm, edge_l_hbm, edge_r_hbm, *rest):
@@ -100,10 +104,21 @@
                 step(0, 0)
             else:
                 lax.fori_loop(0, count // unit, step, 0)
-            for side, res in enumerate((res_l, res_r)):
-                c = pltpu.make_async_copy(res.at[k], outs[2 * i + side].at[k], out_sems.at[i, k, side])
-                c.start()
-                sends.append(c)
+            out_x, out_y = outs[2 * i].at[k], outs[2 * i + 1].at[k]
+            sem_x, sem_y = out_sems.at[i, k, 0], out_sems.at[i, k, 1]
+
+            @pl.when(up_first())
+            def _():
+                pltpu.make_async_copy(res_l.at[k], out_x, sem_x).start()
+                pltpu.make_async_copy(res_r.at[k], out_y, sem_y).start()
+
+            @pl.when(jnp.logical_not(up_first()))
+            def _():
+                pltpu.make_async_copy(res_r.at[k], out_x, sem_x).start()
+                pltpu.make_async_copy(res_l.at[k], out_y, sem_y).start()
+
+            sends.append(pltpu.make_async_copy(res_l.at[k], out_x, sem_x))
+            sends.append(pltpu.make_async_copy(res_r.at[k], out_y, sem_y))
     token[...] = jnp.zeros_like(token)
     for c in sends:
         c.wait()
@@ -255,9 +270,10 @@
 
 def first_kernel(
     chunk, is_first, is_last, groups, scale,
-    own_l, own_r, got_l, got_r, m, coef, routes, *rest
+    own_l, own_r, got_x, got_y, m, coef, routes, *rest
 ):
     start, count = chunk
+    up = up_first()
     rest = list(rest)
     acc_in = None if is_first else rest.pop(0)
     if is_last:
@@ -278,8 +294,9 @@
 
     def load(k, at, unit):
         here, there = pl.ds(at, unit), pl.ds(start + at, unit)
-        left = got_l[k, here] + own_l[k, there]
-        right = got_r[k, here] + own_r[k, there]
+        got_first, got_second = got_x[k, here], got_y[k, here]
+        left = jnp.where(up, got_first, got_second) + own_l[k, there]
+        right = jnp.where(up, got_second, got_first) + own_r[k, there]
         new_l[k, here] = left
         new_r[k, here] = right
         return left, right
@@ -471,10 +488,13 @@
     for c in chunk_sizes(channels):
         bounds.append((at, c))
         at += c
-    up = [(i, i + 1) for i in range(sections - 1)]
-    down = [(i + 1, i) for i in range(sections - 1)]
+    up = [(i * sectors + j, (i + 1) * sectors + j) for i in range(sections - 1) for j in range(sectors)]
+    first = [(a, b) if a % sectors % 2 == 0 else (b, a) for a, b in up]
+    second = [(b, a) for a, b in first]
+
     def pass_on(grown):
-        return lax.ppermute(grown[0], "section", up), lax.ppermute(grown[1], "section", down)
+        axes = ("section", "sector")
+        return lax.ppermute(grown[0], axes, first), lax.ppermute(grown[1], axes, second)
 
     token, (head,) = grow(env_left, env_right, edge_left, edge_right, bounds[:1], (), VMEM_LARGE)
     got = [pass_on(head)]

time: 72.8 us -> 69.8 us (0.959)
  waiting for transfers between devices: 30.3 us -> 25.9 us
  starting transfers between devices: 21.9 us -> 23 us
    ppermute x6, waiting for transfers between devices: 22 us -> 17.8 us  [the longest x3 15.4 us: pass_on(): lax.ppermute(grown[0], axes, first)]
  transfers between devices with their start and end apart: 12 -> 12, of which waited for: 8 -> 8; matrix products, arithmetic and copies ran while one was open for 0% -> 0% of each run, Pallas kernels for 14% -> 15%
where the time goes in v5:
time: 69.8 us; the launch traced here: 69.6 us
  waiting for transfers between devices  25.9 us (37%)
  starting transfers between devices  23 us (33%)
  Pallas kernels  19.7 us (28%)
  between operations  0.85 us (1%)
    ppermute x3, waiting for transfers between devices, pass_on(): lax.ppermute(grown[0], axes, first)  15.4 us
    ppermute x3, starting transfers between devices, pass_on(): lax.ppermute(grown[0], axes, first)  13.9 us
    pallas_call x2, Pallas kernels, grow(): call(functools.partial(grow_kernel, bounds), [jax.ShapeDtypeStruct((8, 12...  10.2 us
    ppermute x4, waiting for transfers between devices, exchange(): lax.ppermute(send, 'sector', [(i, i ^ 1 << stage) for i in range(sectors)])  8.07 us
    pallas_call x3, Pallas kernels, first_apply(): call(functools.partial(first_kernel, chunk, is_first, is_last, groups, ch...  4.25 us
    ppermute x3, starting transfers between devices, pass_on(): lax.ppermute(grown[1], axes, second)  3.88 us
    ppermute x4, starting transfers between devices, exchange(): lax.ppermute(send, 'sector', [(i, i ^ 1 << stage) for i in range(sectors)])  3.55 us
    pallas_call x1, Pallas kernels, second_apply(): call(functools.partial(second_kernel, bounds, groups, channels ** (-0.5))...  2.8 us
  transfers between devices with their start and end apart: 12, of which 8 were waited for; matrix products, arithmetic and copies ran while one was open for 0% of the time, Pallas kernels for 15%

profile of v5, /device:TPU:0, one launch (start us, length us, event | category | flops | bytes accessed | tf_op | source)
XLA Modules:
  0.0 69.6 jit_solution(17727261755457178719)
XLA Ops:
  0.6 3.8 %shard_map.104 = (f32[8,128]{1,0:T(8,128)}, bf16[2,9,128,128]{3,2,1,0:T(8,128)(2,1)}, bf16[2,9,128,128]{3,2,1,0:T(8,128)(2,1)}) custom-call(bf16[1,2,30,128,128]{4,3,2,1,0:T(8,128)(2,1)} %left_hbm.5, bf16[1,2,30,128,128]{4,3,2,1,0:T(8,128)(2,1)} %right_hbm.5, bf16[1,2,128,128]{3,2,1,0:T(8,128)(2,1)} %edge_l_hbm.3, bf16[1,2,128,128]{3,2,1,0:T(8,128)(2,1)} %edge_r_hbm.3), custom_call_target="tpu_custom_call" | custom-call | flops 301989888 | bytes 2359296 | tf_op jit(solution)/shard_map/pallas_call | solution.py:134
  4.4 5.0 %collective-permute-start = (bf16[2,9,128,128]{3,2,1,0:T(8,128)(2,1)}, bf16[2,9,128,128]{3,2,1,0:T(8,128)(2,1)S(1)}, u32[]{:S(2)}, u32[]{:S(2)}) collective-permute-start(bf16[2,9,128,128]{3,2,1,0:T(8,128)(2,1)} %get-tuple-element.40), channel_id=1, source_target_pairs={{0,4},{5,1},{2,6},{7,3},{4,8},{9,5},{6,10},{11,7},{8,12},{13,9},{1... | collective-permute-start | bytes 1769480 | tf_op jit(solution)/shard_map/ppermute | solution.py:497
  9.4 1.3 %collective-permute-start.1 = (bf16[2,9,128,128]{3,2,1,0:T(8,128)(2,1)}, bf16[2,9,128,128]{3,2,1,0:T(8,128)(2,1)S(1)}, u32[]{:S(2)}, u32[]{:S(2)}) collective-permute-start(bf16[2,9,128,128]{3,2,1,0:T(8,128)(2,1)} %get-tuple-element.41), channel_id=1, source_target_pairs={{4,0},{1,5},{6,2},{3,7},{8,4},{5,9},{10,6},{7,11},{12,8},{9,13},{1... | collective-permute-start | bytes 1769480 | tf_op jit(solution)/shard_map/ppermute | solution.py:497
  10.7 0.0 copy-start.2
  10.7 6.4 %shard_map.105 = (f32[8,128]{1,0:T(8,128)}, bf16[2,18,128,128]{3,2,1,0:T(8,128)(2,1)}, bf16[2,18,128,128]{3,2,1,0:T(8,128)(2,1)}, bf16[2,3,128,128]{3,2,1,0:T(8,128)(2,1)}, bf16[2,3,128,128]{3,2,1,0:T(8,128)(2,1)}) custom-call(bf16[1,2,30,128,128]{4,3,2,1,0:T(8,128)(2,1)} %left_hbm.5, bf16[1,2,30,128,128]{4,3,2,1,0:T(8,128)(2,1)} %right_hbm.5, ...), custom_call_target="tpu_custom_call" | custom-call | flops 704643072 | bytes 5505024 | tf_op jit(solution)/shard_map/pallas_call | solution.py:134
  17.1 0.0 copy-start
  17.1 4.8 %collective-permute-start.2 = (bf16[2,18,128,128]{3,2,1,0:T(8,128)(2,1)}, bf16[2,18,128,128]{3,2,1,0:T(8,128)(2,1)S(1)}, u32[]{:S(2)}, u32[]{:S(2)}) collective-permute-start(bf16[2,18,128,128]{3,2,1,0:T(8,128)(2,1)} %get-tuple-element.46), channel_id=1, source_target_pairs={{0,4},{5,1},{2,6},{7,3},{4,8},{9,5},{6,10},{11,7},{8,12},{13,9},{1... | collective-permute-start | bytes 3538952 | tf_op jit(solution)/shard_map/ppermute | solution.py:497
  21.9 1.3 %collective-permute-start.3 = (bf16[2,18,128,128]{3,2,1,0:T(8,128)(2,1)}, bf16[2,18,128,128]{3,2,1,0:T(8,128)(2,1)S(1)}, u32[]{:S(2)}, u32[]{:S(2)}) collective-permute-start(bf16[2,18,128,128]{3,2,1,0:T(8,128)(2,1)} %get-tuple-element.47), channel_id=1, source_target_pairs={{4,0},{1,5},{6,2},{3,7},{8,4},{5,9},{10,6},{7,11},{12,8},{9,13},{1... | collective-permute-start | bytes 3538952 | tf_op jit(solution)/shard_map/ppermute | solution.py:497
  23.2 0.4 collective-permute-done.1.refs_3_.got_y
  23.6 0.6 shard_map.107.after.m.rest_6_
  24.2 0.1 collective-permute-start.6
  24.3 4.2 %collective-permute-start.4 = (bf16[2,3,128,128]{3,2,1,0:T(8,128)(2,1)}, bf16[2,3,128,128]{3,2,1,0:T(8,128)(2,1)S(1)}, u32[]{:S(2)}, u32[]{:S(2)}) collective-permute-start(bf16[2,3,128,128]{3,2,1,0:T(8,128)(2,1)} %get-tuple-element.50), channel_id=1, source_target_pairs={{0,4},{5,1},{2,6},{7,3},{4,8},{9,5},{6,10},{11,7},{8,12},{13,9},{1... | collective-permute-start | bytes 589832 | tf_op jit(solution)/shard_map/ppermute | solution.py:497
  28.5 1.3 %collective-permute-start.5 = (bf16[2,3,128,128]{3,2,1,0:T(8,128)(2,1)}, bf16[2,3,128,128]{3,2,1,0:T(8,128)(2,1)S(1)}, u32[]{:S(2)}, u32[]{:S(2)}) collective-permute-start(bf16[2,3,128,128]{3,2,1,0:T(8,128)(2,1)} %get-tuple-element.51), channel_id=1, source_target_pairs={{4,0},{1,5},{6,2},{3,7},{8,4},{5,9},{10,6},{7,11},{12,8},{9,13},{1... | collective-permute-start | bytes 589832 | tf_op jit(solution)/shard_map/ppermute | solution.py:497
  29.9 1.6 %collective-permute-start.7 = (bf16[2,2,128,128]{3,2,1,0:T(8,128)(2,1)S(1)}, bf16[2,2,128,128]{3,2,1,0:T(8,128)(2,1)S(1)}, u32[]{:S(2)}, u32[]{:S(2)}) collective-permute-start(bf16[2,2,128,128]{3,2,1,0:T(8,128)(2,1)S(1)} %pad_maximum_fusion), channel_id=1, source_target_pairs={{0,2},{1,3},{2,0},{3,1},{4,6},{5,7},{6,4},{7,5},{8,10},{9,11},{10,... | collective-permute-start | bytes 393224 | tf_op jit(solution)/shard_map/ppermute | solution.py:472
  31.4 0.6 shard_map.108
  32.0 1.2 %shard_map.109 = (bf16[2,9,128,128]{3,2,1,0:T(8,128)(2,1)S(1)}, bf16[2,9,128,128]{3,2,1,0:T(8,128)(2,1)S(1)}, f32[8,128,128]{2,1,0:T(8,128)S(1)}) custom-call(bf16[2,30,128,128]{3,2,1,0:T(8,128)(2,1)S(1)} %get-tuple-element.43.own_l, bf16[2,30,128,128]{3,2,1,0:T(8,128)(2,1)S(1)} %get-tuple-element.44.own_r, ...), custom_call_target="tpu_custom_call" | custom-call | flops 150994944 | bytes 1179648 | tf_op jit(solution)/shard_map/pallas_call | solution.py:348
  33.3 15.1 %collective-permute-done.2.got_x = bf16[2,18,128,128]{3,2,1,0:T(8,128)(2,1)S(1)} collective-permute-done((bf16[2,18,128,128]{3,2,1,0:T(8,128)(2,1)}, bf16[2,18,128,128]{3,2,1,0:T(8,128)(2,1)S(1)}, u32[]{:S(2)}, u32[]{:S(2)}) %collective-permute-start.2) | collective-permute-done | bytes 1179680 | tf_op jit(solution)/shard_map/ppermute | solution.py:497
  48.4 2.0 %collective-permute-done.3.got_y = bf16[2,18,128,128]{3,2,1,0:T(8,128)(2,1)S(1)} collective-permute-done((bf16[2,18,128,128]{3,2,1,0:T(8,128)(2,1)}, bf16[2,18,128,128]{3,2,1,0:T(8,128)(2,1)S(1)}, u32[]{:S(2)}, u32[]{:S(2)}) %collective-permute-start.3) | collective-permute-done | bytes 1179680 | tf_op jit(solution)/shard_map/ppermute | solution.py:497
  50.4 1.9 %shard_map.110 = (bf16[2,18,128,128]{3,2,1,0:T(8,128)(2,1)S(1)}, bf16[2,18,128,128]{3,2,1,0:T(8,128)(2,1)S(1)}, f32[8,128,128]{2,1,0:T(8,128)S(1)}) custom-call(bf16[2,30,128,128]{3,2,1,0:T(8,128)(2,1)S(1)} %get-tuple-element.43.own_l, bf16[2,30,128,128]{3,2,1,0:T(8,128)(2,1)S(1)} %get-tuple-element.44.own_r, ...), custom_call_target="tpu_custom_call" | custom-call | flops 301989888 | bytes 2359296 | tf_op jit(solution)/shard_map/pallas_call | solution.py:348
  52.3 0.3 collective-permute-done.4.got_x
  52.6 1.1 %shard_map.111 = (bf16[2,3,128,128]{3,2,1,0:T(8,128)(2,1)S(1)}, bf16[2,3,128,128]{3,2,1,0:T(8,128)(2,1)S(1)}, bf16[528,128]{1,0:T(8,128)(2,1)S(1)}, f32[4,128,12...) custom-call(bf16[2,30,128,128]{3,2,1,0:T(8,128)(2,1)S(1)} %get-tuple-element.43.own_l, ...), custom_call_target="tpu_custom_call" | custom-call | flops 50331648 | bytes 393216 | tf_op jit(solution)/shard_map/pallas_call | solution.py:348
  53.7 0.4 collective-permute-start.8
  54.1 1.0 %collective-permute-done.8.got = bf16[528,128]{1,0:T(8,128)(2,1)S(1)} collective-permute-done((bf16[528,128]{1,0:T(8,128)(2,1)S(1)}, bf16[528,128]{1,0:T(8,128)(2,1)S(1)}, u32[]{:S(2)}, u32[]{:S(2)}) %collective-permute-start.8) | collective-permute-done | bytes 135200 | tf_op jit(solution)/shard_map/ppermute | solution.py:393
  55.1 0.1 shard_map.112
  55.2 1.6 %collective-permute-start.9 = (bf16[272,128]{1,0:T(8,128)(2,1)S(1)}, bf16[272,128]{1,0:T(8,128)(2,1)S(1)}, u32[]{:S(2)}, u32[]{:S(2)}) collective-permute-start(bf16[272,128]{1,0:T(8,128)(2,1)S(1)} %get-tuple-element.61), channel_id=1, source_target_pairs={{0,2},{1,3},{2,0},{3,1},{4,6},{5,7},{6,4},{7,5},{8,10},{9,11},{10,... | collective-permute-start | bytes 208904 | tf_op jit(solution)/shard_map/ppermute | solution.py:393
  56.8 2.9 %collective-permute-done.9.rest_12_ = bf16[272,128]{1,0:T(8,128)(2,1)S(1)} collective-permute-done((bf16[272,128]{1,0:T(8,128)(2,1)S(1)}, bf16[272,128]{1,0:T(8,128)(2,1)S(1)}, u32[]{:S(2)}, u32[]{:S(2)}) %collective-permute-start.9) | collective-permute-done | bytes 69664 | tf_op jit(solution)/shard_map/ppermute | solution.py:393
  59.7 2.8 %shard_map.113 = (bf16[1,2,128,128]{3,2,1,0:T(8,128)(2,1)}, bf16[2,128,128]{2,1,0:T(8,128)(2,1)S(1)}, bf16[528,128]{1,0:T(8,128)(2,1)S(1)}, f32[4,128,128]{2,1,0:T(8,128)S(1)}, f32[8,128]{1,0:T(8,128)S(1)}) custom-call(bf16[2,9,128,128]{3,2,1,0:T(8,128)(2,1)S(1)} %get-tuple-element.45.rest_0_, bf16[2,18,128,128]{3,2,1,0:T(8,128)(2,1)S(1)} %get-tuple-element.49.rest_1_, ...), custom_call_target="tpu_custom_call" | custom-call | flops 503316480 | bytes 3932160 | tf_op jit(solution)/shard_map/pallas_call | solution.py:437
  62.5 1.4 %collective-permute-done.10.got = bf16[528,128]{1,0:T(8,128)(2,1)S(1)} collective-permute-done((bf16[528,128]{1,0:T(8,128)(2,1)S(1)}, bf16[528,128]{1,0:T(8,128)(2,1)S(1)}, u32[]{:S(2)}, u32[]{:S(2)}) %collective-permute-start.10) | collective-permute-done | bytes 135200 | tf_op jit(solution)/shard_map/ppermute | solution.py:393
  63.9 0.1 shard_map.114
  63.9 1.6 %collective-permute-start.11 = (bf16[272,128]{1,0:T(8,128)(2,1)S(1)}, bf16[272,128]{1,0:T(8,128)(2,1)S(1)}, u32[]{:S(2)}, u32[]{:S(2)}) collective-permute-start(bf16[272,128]{1,0:T(8,128)(2,1)S(1)} %get-tuple-element.70), channel_id=1, source_target_pairs={{0,2},{1,3},{2,0},{3,1},{4,6},{5,7},{6,4},{7,5},{8,10},{9,11},{10,... | collective-permute-start | bytes 208904 | tf_op jit(solution)/shard_map/ppermute | solution.py:393
  65.5 2.8 %collective-permute-done.11.got = bf16[272,128]{1,0:T(8,128)(2,1)S(1)} collective-permute-done((bf16[272,128]{1,0:T(8,128)(2,1)S(1)}, bf16[272,128]{1,0:T(8,128)(2,1)S(1)}, u32[]{:S(2)}, u32[]{:S(2)}) %collective-permute-start.11) | collective-permute-done | bytes 69664 | tf_op jit(solution)/shard_map/ppermute | solution.py:393
  68.3 1.3 %shard_map.115 = bf16[1,2,128,128]{3,2,1,0:T(8,128)(2,1)} custom-call(bf16[2,128,128]{2,1,0:T(8,128)(2,1)S(1)} %get-tuple-element.65.resid, f32[1,2]{1,0:T(1,128)S(1)} %copy-done.6, s32[2]{0:T(128)S(1)} %copy-done.5, f32[2,128,128]{2,1,0:T(8,128)S(1)} %get-tuple-element.69.keep, bf16[272,128]{1,0:T(8,128)(2,1)S(1)} %collective-permute-done.11.got, ...), custom_call_target="tpu_custom_call" | custom-call | bytes 262144 | tf_op jit(solution)/shard_map/pallas_call | solution.py:460
  (19 shorter events, 0.1 us)
Async XLA Ops:
  4.4 18.8 %collective-permute-start = (bf16[2,9,128,128]{3,2,1,0:T(8,128)(2,1)}, bf16[2,9,128,128]{3,2,1,0:T(8,128)(2,1)S(1)}, u32[]{:S(2)}, u32[]{:S(2)}) collective-permute-start(bf16[2,9,128,128]{3,2,1,0:T(8,128)(2,1)} %get-tuple-element.40), channel_id=1, source_target_pairs={{0,4},{5,1},{2,6},{7,3},{4,8},{9,5},{6,10},{11,7},{8,12},{13,9},{1... | collective-permute-start | bytes 1769480 | tf_op jit(solution)/shard_map/ppermute | solution.py:497
  9.4 14.2 %collective-permute-start.1 = (bf16[2,9,128,128]{3,2,1,0:T(8,128)(2,1)}, bf16[2,9,128,128]{3,2,1,0:T(8,128)(2,1)S(1)}, u32[]{:S(2)}, u32[]{:S(2)}) collective-permute-start(bf16[2,9,128,128]{3,2,1,0:T(8,128)(2,1)} %get-tuple-element.41), channel_id=1, source_target_pairs={{4,0},{1,5},{6,2},{3,7},{8,4},{5,9},{10,6},{7,11},{12,8},{9,13},{1... | collective-permute-start | bytes 1769480 | tf_op jit(solution)/shard_map/ppermute | solution.py:497
  10.7 12.9 %copy-start.2 = (bf16[1,2,128,128]{3,2,1,0:T(8,128)(2,1)S(1)}, bf16[1,2,128,128]{3,2,1,0:T(8,128)(2,1)}, u32[]{:S(2)}) copy-start(bf16[1,2,128,128]{3,2,1,0:T(8,128)(2,1)} %wave.1) | copy-start | bytes 196612
  10.7 12.9 %copy-start.5 = (s32[2]{0:T(128)S(1)}, s32[2]{0:T(128)}, u32[]{:S(2)}) copy-start(s32[2]{0:T(128)} %sizes.3) | copy-start | bytes 28
  10.7 20.7 %copy-start.1 = (bf16[1,2,30,128,128]{4,3,2,1,0:T(8,128)(2,1)S(1)}, bf16[1,2,30,128,128]{4,3,2,1,0:T(8,128)(2,1)}, u32[]{:S(2)}) copy-start(bf16[1,2,30,128,128]{4,3,2,1,0:T(8,128)(2,1)} %right_hbm.5) | copy-start | bytes 5898244
  17.1 14.3 %copy-start = (bf16[1,2,30,128,128]{4,3,2,1,0:T(8,128)(2,1)S(1)}, bf16[1,2,30,128,128]{4,3,2,1,0:T(8,128)(2,1)}, u32[]{:S(2)}) copy-start(bf16[1,2,30,128,128]{4,3,2,1,0:T(8,128)(2,1)} %left_hbm.5) | copy-start | bytes 5898244
  17.1 31.3 %collective-permute-start.2 = (bf16[2,18,128,128]{3,2,1,0:T(8,128)(2,1)}, bf16[2,18,128,128]{3,2,1,0:T(8,128)(2,1)S(1)}, u32[]{:S(2)}, u32[]{:S(2)}) collective-permute-start(bf16[2,18,128,128]{3,2,1,0:T(8,128)(2,1)} %get-tuple-element.46), channel_id=1, source_target_pairs={{0,4},{5,1},{2,6},{7,3},{4,8},{9,5},{6,10},{11,7},{8,12},{13,9},{1... | collective-permute-start | bytes 3538952 | tf_op jit(solution)/shard_map/ppermute | solution.py:497
  21.9 28.5 %collective-permute-start.3 = (bf16[2,18,128,128]{3,2,1,0:T(8,128)(2,1)}, bf16[2,18,128,128]{3,2,1,0:T(8,128)(2,1)S(1)}, u32[]{:S(2)}, u32[]{:S(2)}) collective-permute-start(bf16[2,18,128,128]{3,2,1,0:T(8,128)(2,1)} %get-tuple-element.47), channel_id=1, source_target_pairs={{4,0},{1,5},{6,2},{3,7},{8,4},{5,9},{10,6},{7,11},{12,8},{9,13},{1... | collective-permute-start | bytes 3538952 | tf_op jit(solution)/shard_map/ppermute | solution.py:497
  24.2 5.6 %collective-permute-start.6 = (bf16[1,2,128,128]{3,2,1,0:T(8,128)(2,1)S(1)}, bf16[1,2,128,128]{3,2,1,0:T(8,128)(2,1)S(1)}, u32[]{:S(2)}, u32[]{:S(2)}) collective-permute-start(bf16[1,2,128,128]{3,2,1,0:T(8,128)(2,1)S(1)} %bitcast.1), channel_id=1, source_target_pairs={{0,1},{1,0},{2,3},{3,2},{4,5},{5,4},{6,7},{7,6},{8,9},{9,8},{10,11... | collective-permute-start | bytes 196616 | tf_op jit(solution)/shard_map/ppermute | solution.py:472
  24.3 28.3 %collective-permute-start.4 = (bf16[2,3,128,128]{3,2,1,0:T(8,128)(2,1)}, bf16[2,3,128,128]{3,2,1,0:T(8,128)(2,1)S(1)}, u32[]{:S(2)}, u32[]{:S(2)}) collective-permute-start(bf16[2,3,128,128]{3,2,1,0:T(8,128)(2,1)} %get-tuple-element.50), channel_id=1, source_target_pairs={{0,4},{5,1},{2,6},{7,3},{4,8},{9,5},{6,10},{11,7},{8,12},{13,9},{1... | collective-permute-start | bytes 589832 | tf_op jit(solution)/shard_map/ppermute | solution.py:497
  28.5 24.1 %collective-permute-start.5 = (bf16[2,3,128,128]{3,2,1,0:T(8,128)(2,1)}, bf16[2,3,128,128]{3,2,1,0:T(8,128)(2,1)S(1)}, u32[]{:S(2)}, u32[]{:S(2)}) collective-permute-start(bf16[2,3,128,128]{3,2,1,0:T(8,128)(2,1)} %get-tuple-element.51), channel_id=1, source_target_pairs={{4,0},{1,5},{6,2},{3,7},{8,4},{5,9},{10,6},{7,11},{12,8},{9,13},{1... | collective-permute-start | bytes 589832 | tf_op jit(solution)/shard_map/ppermute | solution.py:497
  29.8 2.2 %copy-start.3 = (f32[1,2,30]{2,1,0:T(2,128)S(1)}, f32[1,2,30]{2,1,0:T(2,128)}, u32[]{:S(2)}) copy-start(f32[1,2,30]{2,1,0:T(2,128)} %rest_7_.1) | copy-start | bytes 724
  29.9 2.2 %copy-start.4 = (s32[1,2,30]{2,1,0:T(2,128)S(1)}, s32[1,2,30]{2,1,0:T(2,128)}, u32[]{:S(2)}) copy-start(s32[1,2,30]{2,1,0:T(2,128)} %rest_8_.1) | copy-start | bytes 724
  29.9 22.4 %collective-permute-start.7 = (bf16[2,2,128,128]{3,2,1,0:T(8,128)(2,1)S(1)}, bf16[2,2,128,128]{3,2,1,0:T(8,128)(2,1)S(1)}, u32[]{:S(2)}, u32[]{:S(2)}) collective-permute-start(bf16[2,2,128,128]{3,2,1,0:T(8,128)(2,1)S(1)} %pad_maximum_fusion), channel_id=1, source_target_pairs={{0,2},{1,3},{2,0},{3,1},{4,6},{5,7},{6,4},{7,5},{8,10},{9,11},{10,... | collective-permute-start | bytes 393224 | tf_op jit(solution)/shard_map/ppermute | solution.py:472
  50.4 2.2 %copy-start.6 = (f32[1,2]{1,0:T(1,128)S(1)}, f32[1,2]{1,0:T(1,128)}, u32[]{:S(2)}) copy-start(f32[1,2]{1,0:T(1,128)} %onsite.1) | copy-start | bytes 28
  53.7 1.4 %collective-permute-start.8 = (bf16[528,128]{1,0:T(8,128)(2,1)S(1)}, bf16[528,128]{1,0:T(8,128)(2,1)S(1)}, u32[]{:S(2)}, u32[]{:S(2)}) collective-permute-start(bf16[528,128]{1,0:T(8,128)(2,1)S(1)} %get-tuple-element.58), channel_id=1, source_target_pairs={{0,1},{1,0},{2,3},{3,2},{4,5},{5,4},{6,7},{7,6},{8,9},{9,8},{10,11... | collective-permute-start | bytes 405512 | tf_op jit(solution)/shard_map/ppermute | solution.py:393
  55.2 4.5 %collective-permute-start.9 = (bf16[272,128]{1,0:T(8,128)(2,1)S(1)}, bf16[272,128]{1,0:T(8,128)(2,1)S(1)}, u32[]{:S(2)}, u32[]{:S(2)}) collective-permute-start(bf16[272,128]{1,0:T(8,128)(2,1)S(1)} %get-tuple-element.61), channel_id=1, source_target_pairs={{0,2},{1,3},{2,0},{3,1},{4,6},{5,7},{6,4},{7,5},{8,10},{9,11},{10,... | collective-permute-start | bytes 208904 | tf_op jit(solution)/shard_map/ppermute | solution.py:393
  62.5 1.4 %collective-permute-start.10 = (bf16[528,128]{1,0:T(8,128)(2,1)S(1)}, bf16[528,128]{1,0:T(8,128)(2,1)S(1)}, u32[]{:S(2)}, u32[]{:S(2)}) collective-permute-start(bf16[528,128]{1,0:T(8,128)(2,1)S(1)} %get-tuple-element.67), channel_id=1, source_target_pairs={{0,1},{1,0},{2,3},{3,2},{4,5},{5,4},{6,7},{7,6},{8,9},{9,8},{10,11... | collective-permute-start | bytes 405512 | tf_op jit(solution)/shard_map/ppermute | solution.py:393
  63.9 4.4 %collective-permute-start.11 = (bf16[272,128]{1,0:T(8,128)(2,1)S(1)}, bf16[272,128]{1,0:T(8,128)(2,1)S(1)}, u32[]{:S(2)}, u32[]{:S(2)}) collective-permute-start(bf16[272,128]{1,0:T(8,128)(2,1)S(1)} %get-tuple-element.70), channel_id=1, source_target_pairs={{0,2},{1,3},{2,0},{3,1},{4,6},{5,7},{6,4},{7,5},{8,10},{9,11},{10,... | collective-permute-start | bytes 208904 | tf_op jit(solution)/shard_map/ppermute | solution.py:393

commit v6 on v5

--- a/solution.py
+++ b/solution.py
@@ -10,7 +10,7 @@
 epsilon = 1e-06
 VMEM_BYTES = 16 * 1024 * 1024
 VMEM_LARGE = 56 * 1024 * 1024
-EXTRA = 16
+EXTRA = 32
 
 f32 = jnp.float32
 bf16 = jnp.bfloat16
@@ -211,29 +211,56 @@
     return rows & cols
 
 
-def mask_kernel(wave, sizes, after, out):
-    for k in range(wave.shape[1]):
+def prepare_kernel(scale, wave, coef, onsite, sizes, after, out, live, weights, energy):
+    pd, channels = weights.shape[0], weights.shape[1]
+    for k in range(pd):
         v = wave[0, k].astype(f32)
-        out[k] = jnp.where(live_of(sizes[k], v.shape), v, 0.0).astype(bf16)
-
-
-def mask_wave(wave, sizes, after):
+        alive = live_of(sizes[k], v.shape)
+        out[k] = jnp.where(alive, v, 0.0).astype(bf16)
+        live[k] = jnp.where(alive, 1.0, 0.0)
+        energy[k] = jnp.full(energy.shape[1:], onsite[0, k], f32)
+
+        def step(w, carry):
+            weights[k, w] = jnp.full(weights.shape[2:], coef[0, k, w] * scale, f32)
+            return carry
+
+        lax.fori_loop(0, channels, step, 0)
+
+
+def prepare(wave, coef, onsite, sizes, after):
     _, pd, b, _ = wave.shape
-    return call(mask_kernel, [jax.ShapeDtypeStruct((pd, b, b), bf16)], [VM, SM, HB], moved=4 * pd * b * b)(wave, sizes, after)[0]
-
-
-def apply_blocks(load, count, vectors, first, acc, coef, routes, scale, unit):
+    channels = coef.shape[2]
+    return call(
+        functools.partial(prepare_kernel, channels ** (-0.5)),
+        [
+            jax.ShapeDtypeStruct((pd, b, b), bf16),
+            jax.ShapeDtypeStruct((pd, b, b), f32),
+            jax.ShapeDtypeStruct((pd, channels, 8, b), f32),
+            jax.ShapeDtypeStruct((pd, 8, b), f32),
+        ],
+        [VM, SM, SM, SM, HB],
+        moved=4 * pd * b * b,
+    )(wave, coef, onsite, sizes, after)
+
+
+def times(tile, x):
+    return (x.reshape(-1, 8, x.shape[-1]) * tile).reshape(x.shape)
+
+
+def apply_blocks(load, count, vectors, first, acc, weights, routes, unit, ready=None):
     pd, b = len(vectors), vectors[0].shape[0]
 
     def step(s, carry):
         at = s * unit
         loaded = [load(k, at, unit) for k in range(pd)]
         halves = [dot(loaded[k][0].reshape(unit * b, b), vectors[k]).astype(bf16) for k in range(pd)]
+        if ready is not None:
+            ready.wait()
         for k in range(pd):
             for u in range(unit):
                 contrib = dot(halves[k][u * b : (u + 1) * b], loaded[k][1][u])
                 j = routes[0, k, first + at + u]
-                acc[j] += contrib * (coef[0, k, first + at + u] * scale)
+                acc[j] += times(weights[k, first + at + u], contrib)
         return carry
 
     if count == unit:
@@ -242,16 +269,19 @@
         lax.fori_loop(0, count // unit, step, 0)
 
 
-def three_terms(x, rows):
+def three_terms(x):
     hi = x.astype(bf16).astype(f32)
     mid = (x - hi).astype(bf16).astype(f32)
     low = x - hi - mid
-    place = lax.broadcasted_iota(jnp.int32, (EXTRA, 128), 0)
-    return jnp.where(place == 0, hi, jnp.where(place == 1, mid, jnp.where(place == 2, low, 0.0))).astype(bf16)
+    return jnp.concatenate([hi, mid, low, jnp.zeros_like(x)], axis=0).astype(bf16)
 
 
 def from_terms(rows):
-    return jnp.sum(rows.astype(f32), axis=0, keepdims=True)
+    return fold(rows.astype(f32))
+
+
+def fold(x):
+    return jnp.sum(x.reshape(-1, 8, x.shape[-1]), axis=0)
 
 
 def total_of(x):
@@ -265,27 +295,29 @@
             sent = acc[(2 * i + 1 - bit) * pd + q]
             keep[i * pd + q] = kept
             send[pl.ds((i * pd + q) * b, b)] = sent.astype(bf16)
-    send[pl.ds(groups // 2 * pd * b, EXTRA)] = three_terms(extra, EXTRA)
+    send[pl.ds(groups // 2 * pd * b, EXTRA)] = three_terms(extra)
 
 
 def first_kernel(
-    chunk, is_first, is_last, groups, scale,
-    own_l, own_r, got_x, got_y, m, coef, routes, *rest
+    chunk, is_first, is_last, groups,
+    own_l, own_r, got_x, got_y, m, weights, routes_in, *rest
 ):
     start, count = chunk
     up = up_first()
     rest = list(rest)
     acc_in = None if is_first else rest.pop(0)
     if is_last:
-        onsite = rest.pop(0)
+        energy = rest.pop(0)
         pieces = []
         at = 1
         while at < groups:
             pieces.append(rest.pop(0))
             at += pieces[-1].shape[0]
-        new_l, new_r, send, keep, squares_out, corr_out, acc = rest
+        new_l, new_r, send, keep, squares_out, corr_out, routes, routes_sem, acc = rest
     else:
-        new_l, new_r, acc = rest
+        new_l, new_r, acc, routes, routes_sem = rest
+    routes_copy = pltpu.make_async_copy(routes_in, routes, routes_sem)
+    routes_copy.start()
     pd, b = m.shape[0], m.shape[1]
     if is_first:
         acc[...] = jnp.zeros_like(acc)
@@ -301,7 +333,11 @@
         new_r[k, here] = right
         return left, right
 
-    apply_blocks(load, count, [m[k] for k in range(pd)], start, acc, coef, routes, scale, unit_of(count))
+    unit = unit_of(count)
+    ready = routes_copy if unit == count else None
+    if ready is None:
+        routes_copy.wait()
+    apply_blocks(load, count, [m[k] for k in range(pd)], start, acc, weights, routes, unit, ready)
     if not is_last:
         return
     me = lax.axis_index("sector")
@@ -309,7 +345,7 @@
     squares = jnp.zeros((b, b), f32)
     for k in range(pd):
         g = m[k].astype(f32)
-        corr += g * (acc[me * pd + k] + onsite[0, k] * g)
+        corr += g * (acc[me * pd + k] + times(energy[k], g))
         squares += g * g
     distance = 1
     for piece in pieces:
@@ -320,33 +356,33 @@
                 corr += g * acc[owner * pd + k]
                 squares += g * g
             distance += 1
-    corr = total_of(corr)
-    squares_out[...] = jnp.broadcast_to(total_of(squares), squares_out.shape)
-    corr_out[...] = jnp.broadcast_to(corr, corr_out.shape)
+    corr = fold(corr)
+    squares_out[...] = fold(squares)
+    corr_out[...] = corr
     split_halves(acc, groups, pd, b, lax.rem(me, 2), send, keep, corr)
 
 
-def first_apply(chunk, is_first, is_last, groups, channels, arrays, acc_in, extra):
+def first_apply(chunk, is_first, is_last, groups, arrays, acc_in, extra):
     start, count = chunk
     m = arrays[4]
     pd, b, _ = m.shape
     total = jax.ShapeDtypeStruct((groups * pd, b, b), f32)
     block = jax.ShapeDtypeStruct((pd, count, b, b), bf16)
     args = list(arrays)
-    specs = [VM, VM, VM, VM, VM, SM, SM]
+    specs = [VM, VM, VM, VM, VM, VM, HB]
     if not is_first:
         args.append(acc_in)
         specs.append(VM)
-    scratch = []
+    scratch = [pltpu.SMEM(arrays[6].shape, jnp.int32), pltpu.SemaphoreType.DMA]
     if is_last:
         args += list(extra)
-        specs += [SM] + [VM] * (len(extra) - 1)
+        specs += [VM] * len(extra)
         outs = [block, block] + exchange_shapes(groups, pd, b) + [jax.ShapeDtypeStruct((8, 128), f32)] * 2
-        scratch = [pltpu.VMEM((groups * pd, b, b), f32)]
+        scratch.append(pltpu.VMEM((groups * pd, b, b), f32))
     else:
         outs = [block, block, total]
     return call(
-        functools.partial(first_kernel, chunk, is_first, is_last, groups, channels ** (-0.5)),
+        functools.partial(first_kernel, chunk, is_first, is_last, groups),
         outs,
         specs,
         scratch,
@@ -368,8 +404,8 @@
     me = lax.axis_index("sector")
     for i in range(groups * pd):
         acc[i] = keep_in[i] + got[pl.ds(i * b, b)].astype(f32)
-    extra = extra_in[0:1, 0:1] + from_terms(got[pl.ds(groups * pd * b, EXTRA)])[:, 0:1]
-    extra_out[...] = jnp.broadcast_to(extra, extra_out.shape)
+    extra = extra_in[...] + from_terms(got[pl.ds(groups * pd * b, EXTRA)])
+    extra_out[...] = extra
     bit = lax.rem(lax.div(me, 2**stage), 2)
     split_halves(acc, groups, pd, b, bit, send, keep, extra)
 
@@ -398,71 +434,88 @@
         send, keep, extra = combine(groups, stage, pd, keep, got, extra)
 
 
-def second_kernel(bounds, groups, scale, *rest):
+def second_kernel(bounds, groups, *rest):
     n = len(bounds)
     lefts, rights = rest[:n], rest[n : 2 * n]
-    (m, coef, routes, onsite, sizes, keep_in, got, corr_in, squares_in,
-     image_out, resid_out, send, keep, sq_out, acc) = rest[2 * n :]
+    (m, weights, routes_in, energy, live, keep_in, got, corr_in, squares_in,
+     image_hbm, resid_out, send, keep, sq_out, acc, image_out, image_sem, routes, routes_sem) = rest[2 * n :]
     pd, b = m.shape[0], m.shape[1]
+    routes_copy = pltpu.make_async_copy(routes_in, routes, routes_sem)
+    routes_copy.start()
     acc[...] = jnp.zeros_like(acc)
-    squares = squares_in[0:1, 0:1]
-    corr = corr_in[0:1, 0:1] + from_terms(got[pl.ds(pd * b, EXTRA)])[:, 0:1]
+    squares = total_of(squares_in[...])
+    corr = total_of(corr_in[...] + from_terms(got[pl.ds(pd * b, EXTRA)]))
     ritz = corr / (squares + epsilon)
     sums = jnp.zeros((b, b), f32)
     for k in range(pd):
         g = m[k].astype(f32)
-        summed = keep_in[k] + got[pl.ds(k * b, b)].astype(f32) + onsite[0, k] * g
-        image = jnp.where(live_of(sizes[k], (b, b)), summed, 0.0)
-        image_out[0, k] = image.astype(bf16)
+        summed = keep_in[k] + got[pl.ds(k * b, b)].astype(f32) + times(energy[k], g)
+        image = jnp.where(live[k] > 0.0, summed, 0.0)
+        image_out[k] = image.astype(bf16)
         resid = image - ritz * g
         resid_out[k] = resid.astype(bf16)
         sums += resid * resid
-    total = total_of(sums)
-    sq_out[...] = jnp.broadcast_to(total, sq_out.shape)
+    image_copy = pltpu.make_async_copy(image_out, image_hbm.at[0], image_sem)
+    image_copy.start()
+    total = fold(sums)
+    sq_out[...] = total
     vectors = [resid_out[k] for k in range(pd)]
+    routes_copy.wait()
     for i, (start, count) in enumerate(bounds):
 
         def load(k, at, unit):
             return lefts[i][k, pl.ds(at, unit)], rights[i][k, pl.ds(at, unit)]
 
-        apply_blocks(load, count, vectors, start, acc, coef, routes, scale, unit_of(count))
+        apply_blocks(load, count, vectors, start, acc, weights, routes, unit_of(count))
     me = lax.axis_index("sector")
     split_halves(acc, groups, pd, b, lax.rem(me, 2), send, keep, total)
-
-
-def second_apply(bounds, groups, channels, lefts, rights, m, coef, routes, onsite, sizes, keep, got, corr, squares):
+    image_copy.wait()
+
+
+def second_apply(bounds, groups, channels, lefts, rights, m, weights, routes, energy, live, keep, got, corr, squares):
     pd, b, _ = m.shape
     n = len(bounds)
     block = jax.ShapeDtypeStruct((1, pd, b, b), bf16)
     return call(
-        functools.partial(second_kernel, bounds, groups, channels ** (-0.5)),
+        functools.partial(second_kernel, bounds, groups),
         [block, jax.ShapeDtypeStruct((pd, b, b), bf16)]
         + exchange_shapes(groups, pd, b)
         + [jax.ShapeDtypeStruct((8, 128), f32)],
-        [VM] * (2 * n) + [VM, SM, SM, SM, SM, VM, VM, VM, VM],
-        [pltpu.VMEM((groups * pd, b, b), f32)],
+        [VM] * (2 * n) + [VM, VM, HB, VM, VM, VM, VM, VM, VM],
+        [
+            pltpu.VMEM((groups * pd, b, b), f32), pltpu.VMEM((pd, b, b), bf16), pltpu.SemaphoreType.DMA,
+            pltpu.SMEM(routes.shape, jnp.int32), pltpu.SemaphoreType.DMA,
+        ],
         flops=4 * pd * channels * b**3,
         moved=4 * pd * channels * b * b,
-    )(*lefts, *rights, m, coef, routes, onsite, sizes, keep, got, corr, squares)
-
-
-def final_kernel(resid, onsite, sizes, keep, got, sq_in, squares_in, out):
+        out_specs=[HB, VM, VM, VM, VM],
+    )(*lefts, *rights, m, weights, routes, energy, live, keep, got, corr, squares)
+
+
+def final_kernel(resid, energy, live, keep, got, sq_in, squares_in, out, image, sems):
     pd, b = resid.shape[0], resid.shape[1]
-    sq = sq_in[0:1, 0:1] + from_terms(got[pl.ds(pd * b, EXTRA)])[:, 0:1]
-    alpha = jnp.sqrt(squares_in[0:1, 0:1] / (sq + epsilon))
+    sq = total_of(sq_in[...] + from_terms(got[pl.ds(pd * b, EXTRA)]))
+    alpha = jnp.sqrt(total_of(squares_in[...]) / (sq + epsilon))
+    copies = []
     for k in range(pd):
-        summed = keep[k] + got[pl.ds(k * b, b)].astype(f32) + onsite[0, k] * resid[k].astype(f32)
-        out[0, k] = jnp.where(live_of(sizes[k], (b, b)), alpha * summed, 0.0).astype(bf16)
-
-
-def final(resid, onsite, sizes, keep, got, sq, squares):
+        summed = keep[k] + got[pl.ds(k * b, b)].astype(f32) + times(energy[k], resid[k].astype(f32))
+        image[k] = jnp.where(live[k] > 0.0, alpha * summed, 0.0).astype(bf16)
+        copies.append(pltpu.make_async_copy(image.at[k], out.at[0, k], sems.at[k]))
+        copies[-1].start()
+    for c in copies:
+        c.wait()
+
+
+def final(resid, energy, live, keep, got, sq, squares):
     pd, b, _ = resid.shape
     return call(
         final_kernel,
         [jax.ShapeDtypeStruct((1, pd, b, b), bf16)],
-        [VM, SM, SM, VM, VM, VM, VM],
+        [VM] * 7,
+        [pltpu.VMEM((pd, b, b), bf16), pltpu.SemaphoreType.DMA((pd,))],
         moved=8 * pd * b * b,
-    )(resid, onsite, sizes, keep, got, sq, squares)[0]
+        out_specs=[HB],
+    )(resid, energy, live, keep, got, sq, squares)[0]
 
 
 def gather_waves(sectors, m):
@@ -501,7 +554,7 @@
     _, (middle, last) = grow(env_left, env_right, edge_left, edge_right, bounds[1:], (token,), VMEM_LARGE)
     got.append(pass_on(middle))
     grown, token = gate(last, got[0])
-    m = mask_wave(wave_blocks, sector_sizes, token)
+    m, live, weights, energy = prepare(wave_blocks, mpo_coef, onsite, sector_sizes, token)
     got.append(pass_on(grown))
     pieces = gather_waves(sectors, m)
     own_l, own_r = own_ends(env_left, env_right, m)
@@ -509,8 +562,8 @@
     for i, chunk in enumerate(bounds):
         is_last = i == len(bounds) - 1
         res = first_apply(
-            chunk, i == 0, is_last, sectors, channels,
-            (own_l, own_r, got[i][0], got[i][1], m, mpo_coef, routes), acc, (onsite, *pieces),
+            chunk, i == 0, is_last, sectors,
+            (own_l, own_r, got[i][0], got[i][1], m, weights, routes), acc, (energy, *pieces),
         )
         lefts.append(res[0])
         rights.append(res[1])
@@ -518,11 +571,11 @@
     send, keep, squares, corr = res[2:]
     keep, summed, corr = exchange(sectors, pd, send, keep, corr)
     image1, resid, send, keep, sq = second_apply(
-        bounds, sectors, channels, lefts, rights, m, mpo_coef, routes, onsite,
-        sector_sizes, keep, summed, corr, squares,
+        bounds, sectors, channels, lefts, rights, m, weights, routes, energy,
+        live, keep, summed, corr, squares,
     )
     keep, summed, sq = exchange(sectors, pd, send, keep, sq)
-    image2 = final(resid, onsite, sector_sizes, keep, summed, sq, squares)
+    image2 = final(resid, energy, live, keep, summed, sq, squares)
     return (image1, image2)
 
 

time: 69.8 us -> 69 us (0.989)
  local copies, waits for them, and re-layouts: 0.04 us -> 3.27 us
  waiting for transfers between devices: 25.9 us -> 22.7 us
  Pallas kernels: 19.7 us -> 18.7 us
    unnamed x14 -> x22, local copies, waits for them, and re-layouts: 0.04 us -> 3.27 us
    ppermute x3, waiting for transfers between devices: 15.4 us -> 12.2 us  [pass_on(): lax.ppermute(grown[0], axes, first)]
    pallas_call x6, Pallas kernels: 8.87 us -> 7.84 us  [the longest x3 3.65 us: first_apply(): call(functools.partial(first_kernel, chunk, is_first, is_last, groups), o...]
  transfers between devices with their start and end apart: 12 -> 12, of which waited for: 8 -> 8; matrix products, arithmetic and copies ran while one was open for 0% -> 0% of each run, Pallas kernels for 15% -> 16%
where the time goes in v6:
time: 69 us; the launch traced here: 68.7 us
  starting transfers between devices  23.1 us (33%)
  waiting for transfers between devices  22.7 us (33%)
  Pallas kernels  18.7 us (27%)
  local copies, waits for them, and re-layouts  3.27 us (5%)
  between operations  0.87 us (1%)
    ppermute x3, starting transfers between devices, pass_on(): lax.ppermute(grown[0], axes, first)  13.9 us
    ppermute x3, waiting for transfers between devices, pass_on(): lax.ppermute(grown[0], axes, first)  12.2 us
    pallas_call x2, Pallas kernels, grow(): call(functools.partial(grow_kernel, bounds), [jax.ShapeDtypeStruct((8, 12...  10.2 us
    ppermute x4, waiting for transfers between devices, exchange(): lax.ppermute(send, 'sector', [(i, i ^ 1 << stage) for i in range(sectors)])  8.21 us
    ppermute x3, starting transfers between devices, pass_on(): lax.ppermute(grown[1], axes, second)  3.88 us
    pallas_call x3, Pallas kernels, first_apply(): call(functools.partial(first_kernel, chunk, is_first, is_last, groups), o...  3.65 us
    ppermute x4, starting transfers between devices, exchange(): lax.ppermute(send, 'sector', [(i, i ^ 1 << stage) for i in range(sectors)])  3.64 us
    unnamed x22, local copies, waits for them, and re-layouts  3.27 us
  transfers between devices with their start and end apart: 12, of which 8 were waited for; matrix products, arithmetic and copies ran while one was open for 0% of the time, Pallas kernels for 16%

profile of v6, /device:TPU:0, one launch (start us, length us, event | category | flops | bytes accessed | tf_op | source)
XLA Modules:
  0.0 68.7 jit_solution(16931699158481801696)
XLA Ops:
  0.6 3.8 %shard_map.104 = (f32[8,128]{1,0:T(8,128)}, bf16[2,9,128,128]{3,2,1,0:T(8,128)(2,1)}, bf16[2,9,128,128]{3,2,1,0:T(8,128)(2,1)}) custom-call(bf16[1,2,30,128,128]{4,3,2,1,0:T(8,128)(2,1)} %left_hbm.5, bf16[1,2,30,128,128]{4,3,2,1,0:T(8,128)(2,1)} %right_hbm.5, bf16[1,2,128,128]{3,2,1,0:T(8,128)(2,1)} %edge_l_hbm.3, bf16[1,2,128,128]{3,2,1,0:T(8,128)(2,1)} %edge_r_hbm.3), custom_call_target="tpu_custom_call" | custom-call | flops 301989888 | bytes 2359296 | tf_op jit(solution)/shard_map/pallas_call | solution.py:134
  4.4 5.0 %collective-permute-start = (bf16[2,9,128,128]{3,2,1,0:T(8,128)(2,1)}, bf16[2,9,128,128]{3,2,1,0:T(8,128)(2,1)S(1)}, u32[]{:S(2)}, u32[]{:S(2)}) collective-permute-start(bf16[2,9,128,128]{3,2,1,0:T(8,128)(2,1)} %get-tuple-element.44), channel_id=1, source_target_pairs={{0,4},{5,1},{2,6},{7,3},{4,8},{9,5},{6,10},{11,7},{8,12},{13,9},{1... | collective-permute-start | bytes 1769480 | tf_op jit(solution)/shard_map/ppermute | solution.py:550
  9.4 1.3 %collective-permute-start.1 = (bf16[2,9,128,128]{3,2,1,0:T(8,128)(2,1)}, bf16[2,9,128,128]{3,2,1,0:T(8,128)(2,1)S(1)}, u32[]{:S(2)}, u32[]{:S(2)}) collective-permute-start(bf16[2,9,128,128]{3,2,1,0:T(8,128)(2,1)} %get-tuple-element.45), channel_id=1, source_target_pairs={{4,0},{1,5},{6,2},{3,7},{8,4},{5,9},{10,6},{7,11},{12,8},{9,13},{1... | collective-permute-start | bytes 1769480 | tf_op jit(solution)/shard_map/ppermute | solution.py:550
  10.7 6.4 %shard_map.105 = (f32[8,128]{1,0:T(8,128)}, bf16[2,18,128,128]{3,2,1,0:T(8,128)(2,1)}, bf16[2,18,128,128]{3,2,1,0:T(8,128)(2,1)}, bf16[2,3,128,128]{3,2,1,0:T(8,128)(2,1)}, bf16[2,3,128,128]{3,2,1,0:T(8,128)(2,1)}) custom-call(bf16[1,2,30,128,128]{4,3,2,1,0:T(8,128)(2,1)} %left_hbm.5, bf16[1,2,30,128,128]{4,3,2,1,0:T(8,128)(2,1)} %right_hbm.5, ...), custom_call_target="tpu_custom_call" | custom-call | flops 704643072 | bytes 5505024 | tf_op jit(solution)/shard_map/pallas_call | solution.py:134
  17.2 4.7 %collective-permute-start.2 = (bf16[2,18,128,128]{3,2,1,0:T(8,128)(2,1)}, bf16[2,18,128,128]{3,2,1,0:T(8,128)(2,1)S(1)}, u32[]{:S(2)}, u32[]{:S(2)}) collective-permute-start(bf16[2,18,128,128]{3,2,1,0:T(8,128)(2,1)} %get-tuple-element.52), channel_id=1, source_target_pairs={{0,4},{5,1},{2,6},{7,3},{4,8},{9,5},{6,10},{11,7},{8,12},{13,9},{1... | collective-permute-start | bytes 3538952 | tf_op jit(solution)/shard_map/ppermute | solution.py:550
  21.9 1.3 %collective-permute-start.3 = (bf16[2,18,128,128]{3,2,1,0:T(8,128)(2,1)}, bf16[2,18,128,128]{3,2,1,0:T(8,128)(2,1)S(1)}, u32[]{:S(2)}, u32[]{:S(2)}) collective-permute-start(bf16[2,18,128,128]{3,2,1,0:T(8,128)(2,1)} %get-tuple-element.53), channel_id=1, source_target_pairs={{4,0},{1,5},{6,2},{3,7},{8,4},{5,9},{10,6},{7,11},{12,8},{9,13},{1... | collective-permute-start | bytes 3538952 | tf_op jit(solution)/shard_map/ppermute | solution.py:550
  23.2 0.3 collective-permute-done.1.refs_3_.got_y
  23.6 0.9 %copy-done.2 = bf16[2,3,128,128]{3,2,1,0:T(8,128)(2,1)S(1)} copy-done((bf16[2,3,128,128]{3,2,1,0:T(8,128)(2,1)S(1)}, bf16[2,3,128,128]{3,2,1,0:T(8,128)(2,1)}, u32[]{:S(2)}) %copy-start.2) | copy-done | bytes 196632
  24.5 0.9 %copy-done.4 = bf16[2,3,128,128]{3,2,1,0:T(8,128)(2,1)S(1)} copy-done((bf16[2,3,128,128]{3,2,1,0:T(8,128)(2,1)S(1)}, bf16[2,3,128,128]{3,2,1,0:T(8,128)(2,1)}, u32[]{:S(2)}) %copy-start.4) | copy-done | bytes 196632
  25.4 0.7 copy-done.3
  26.1 0.7 copy-done.5
  26.8 1.0 %shard_map.107 = (bf16[2,128,128]{2,1,0:T(8,128)(2,1)S(1)}, f32[2,128,128]{2,1,0:T(8,128)S(1)}, f32[2,30,8,128]{3,2,1,0:T(8,128)S(1)}, f32[2,8,128]{2,1,0:T(8,128)S(1)}) custom-call(bf16[1,2,128,128]{3,2,1,0:T(8,128)(2,1)S(1)} %copy-done.6, f32[1,2,30]{2,1,0:T(2,128)S(1)} %copy-done.8, f32[1,2]{1,0:T(1,128)S(1)} %copy-done.9, s32[2]{0:T(128)S(1)} %copy-done.10, ...), custom_call_target="tpu_custom_call" | custom-call | bytes 131072 | tf_op jit(solution)/shard_map/pallas_call | solution.py:233
  27.8 0.1 collective-permute-start.6
  27.9 4.2 %collective-permute-start.4 = (bf16[2,3,128,128]{3,2,1,0:T(8,128)(2,1)}, bf16[2,3,128,128]{3,2,1,0:T(8,128)(2,1)S(1)}, u32[]{:S(2)}, u32[]{:S(2)}) collective-permute-start(bf16[2,3,128,128]{3,2,1,0:T(8,128)(2,1)} %copy-done.3), channel_id=1, source_target_pairs={{0,4},{5,1},{2,6},{7,3},{4,8},{9,5},{6,10},{11,7},{8,12},{13,9},{1... | collective-permute-start | bytes 589832 | tf_op jit(solution)/shard_map/ppermute | solution.py:550
  32.1 1.3 %collective-permute-start.5 = (bf16[2,3,128,128]{3,2,1,0:T(8,128)(2,1)}, bf16[2,3,128,128]{3,2,1,0:T(8,128)(2,1)S(1)}, u32[]{:S(2)}, u32[]{:S(2)}) collective-permute-start(bf16[2,3,128,128]{3,2,1,0:T(8,128)(2,1)} %copy-done.5), channel_id=1, source_target_pairs={{4,0},{1,5},{6,2},{3,7},{8,4},{5,9},{10,6},{7,11},{12,8},{9,13},{1... | collective-permute-start | bytes 589832 | tf_op jit(solution)/shard_map/ppermute | solution.py:550
  33.5 1.6 %collective-permute-start.7 = (bf16[2,2,128,128]{3,2,1,0:T(8,128)(2,1)S(1)}, bf16[2,2,128,128]{3,2,1,0:T(8,128)(2,1)S(1)}, u32[]{:S(2)}, u32[]{:S(2)}) collective-permute-start(bf16[2,2,128,128]{3,2,1,0:T(8,128)(2,1)S(1)} %pad_maximum_fusion), channel_id=1, source_target_pairs={{0,2},{1,3},{2,0},{3,1},{4,6},{5,7},{6,4},{7,5},{8,10},{9,11},{10,... | collective-permute-start | bytes 393224 | tf_op jit(solution)/shard_map/ppermute | solution.py:525
  35.1 0.6 shard_map.108
  35.6 0.9 %shard_map.109 = (bf16[2,9,128,128]{3,2,1,0:T(8,128)(2,1)S(1)}, bf16[2,9,128,128]{3,2,1,0:T(8,128)(2,1)S(1)}, f32[8,128,128]{2,1,0:T(8,128)S(1)}) custom-call(bf16[2,30,128,128]{3,2,1,0:T(8,128)(2,1)S(1)} %get-tuple-element.48.own_l, bf16[2,30,128,128]{3,2,1,0:T(8,128)(2,1)S(1)} %get-tuple-element.49.own_r, ...), custom_call_target="tpu_custom_call" | custom-call | flops 150994944 | bytes 1179648 | tf_op jit(solution)/shard_map/pallas_call | solution.py:384
  36.5 11.9 %collective-permute-done.2.got_x = bf16[2,18,128,128]{3,2,1,0:T(8,128)(2,1)S(1)} collective-permute-done((bf16[2,18,128,128]{3,2,1,0:T(8,128)(2,1)}, bf16[2,18,128,128]{3,2,1,0:T(8,128)(2,1)S(1)}, u32[]{:S(2)}, u32[]{:S(2)}) %collective-permute-start.2) | collective-permute-done | bytes 1179680 | tf_op jit(solution)/shard_map/ppermute | solution.py:550
  48.4 2.0 %collective-permute-done.3.got_y = bf16[2,18,128,128]{3,2,1,0:T(8,128)(2,1)S(1)} collective-permute-done((bf16[2,18,128,128]{3,2,1,0:T(8,128)(2,1)}, bf16[2,18,128,128]{3,2,1,0:T(8,128)(2,1)S(1)}, u32[]{:S(2)}, u32[]{:S(2)}) %collective-permute-start.3) | collective-permute-done | bytes 1179680 | tf_op jit(solution)/shard_map/ppermute | solution.py:550
  50.4 1.9 %shard_map.110 = (bf16[2,18,128,128]{3,2,1,0:T(8,128)(2,1)S(1)}, bf16[2,18,128,128]{3,2,1,0:T(8,128)(2,1)S(1)}, f32[8,128,128]{2,1,0:T(8,128)S(1)}) custom-call(bf16[2,30,128,128]{3,2,1,0:T(8,128)(2,1)S(1)} %get-tuple-element.48.own_l, bf16[2,30,128,128]{3,2,1,0:T(8,128)(2,1)S(1)} %get-tuple-element.49.own_r, ...), custom_call_target="tpu_custom_call" | custom-call | flops 301989888 | bytes 2359296 | tf_op jit(solution)/shard_map/pallas_call | solution.py:384
  52.3 0.4 collective-permute-done.4.got_x
  52.6 0.9 %shard_map.111 = (bf16[2,3,128,128]{3,2,1,0:T(8,128)(2,1)S(1)}, bf16[2,3,128,128]{3,2,1,0:T(8,128)(2,1)S(1)}, bf16[544,128]{1,0:T(8,128)(2,1)S(1)}, f32[4,128,12...) custom-call(bf16[2,30,128,128]{3,2,1,0:T(8,128)(2,1)S(1)} %get-tuple-element.48.own_l, ...), custom_call_target="tpu_custom_call" | custom-call | flops 50331648 | bytes 393216 | tf_op jit(solution)/shard_map/pallas_call | solution.py:384
  53.5 0.4 collective-permute-start.8
  53.9 1.0 %collective-permute-done.8.got = bf16[544,128]{1,0:T(8,128)(2,1)S(1)} collective-permute-done((bf16[544,128]{1,0:T(8,128)(2,1)S(1)}, bf16[544,128]{1,0:T(8,128)(2,1)S(1)}, u32[]{:S(2)}, u32[]{:S(2)}) %collective-permute-start.8) | collective-permute-done | bytes 139296 | tf_op jit(solution)/shard_map/ppermute | solution.py:429
  55.0 1.6 %collective-permute-start.9 = (bf16[288,128]{1,0:T(8,128)(2,1)S(1)}, bf16[288,128]{1,0:T(8,128)(2,1)S(1)}, u32[]{:S(2)}, u32[]{:S(2)}) collective-permute-start(bf16[288,128]{1,0:T(8,128)(2,1)S(1)} %get-tuple-element.69), channel_id=1, source_target_pairs={{0,2},{1,3},{2,0},{3,1},{4,6},{5,7},{6,4},{7,5},{8,10},{9,11},{10,... | collective-permute-start | bytes 221192 | tf_op jit(solution)/shard_map/ppermute | solution.py:429
  56.6 3.0 %collective-permute-done.9.rest_12_ = bf16[288,128]{1,0:T(8,128)(2,1)S(1)} collective-permute-done((bf16[288,128]{1,0:T(8,128)(2,1)S(1)}, bf16[288,128]{1,0:T(8,128)(2,1)S(1)}, u32[]{:S(2)}, u32[]{:S(2)}) %collective-permute-start.9) | collective-permute-done | bytes 73760 | tf_op jit(solution)/shard_map/ppermute | solution.py:429
  59.6 2.4 %shard_map.113 = (bf16[1,2,128,128]{3,2,1,0:T(8,128)(2,1)}, bf16[2,128,128]{2,1,0:T(8,128)(2,1)S(1)}, bf16[544,128]{1,0:T(8,128)(2,1)S(1)}, f32[4,128,128]{2,1,0:T(8,128)S(1)}, f32[8,128]{1,0:T(8,128)S(1)}) custom-call(bf16[2,9,128,128]{3,2,1,0:T(8,128)(2,1)S(1)} %get-tuple-element.51.rest_0_, bf16[2,18,128,128]{3,2,1,0:T(8,128)(2,1)S(1)} %get-tuple-element.55.rest_1_, ...), custom_call_target="tpu_custom_call" | custom-call | flops 503316480 | bytes 3932160 | tf_op jit(solution)/shard_map/pallas_call | solution.py:479
  62.1 1.3 %collective-permute-done.10.got = bf16[544,128]{1,0:T(8,128)(2,1)S(1)} collective-permute-done((bf16[544,128]{1,0:T(8,128)(2,1)S(1)}, bf16[544,128]{1,0:T(8,128)(2,1)S(1)}, u32[]{:S(2)}, u32[]{:S(2)}) %collective-permute-start.10) | collective-permute-done | bytes 139296 | tf_op jit(solution)/shard_map/ppermute | solution.py:429
  63.5 1.6 %collective-permute-start.11 = (bf16[288,128]{1,0:T(8,128)(2,1)S(1)}, bf16[288,128]{1,0:T(8,128)(2,1)S(1)}, u32[]{:S(2)}, u32[]{:S(2)}) collective-permute-start(bf16[288,128]{1,0:T(8,128)(2,1)S(1)} %get-tuple-element.78), channel_id=1, source_target_pairs={{0,2},{1,3},{2,0},{3,1},{4,6},{5,7},{6,4},{7,5},{8,10},{9,11},{10,... | collective-permute-start | bytes 221192 | tf_op jit(solution)/shard_map/ppermute | solution.py:429
  65.1 2.8 %collective-permute-done.11.got = bf16[288,128]{1,0:T(8,128)(2,1)S(1)} collective-permute-done((bf16[288,128]{1,0:T(8,128)(2,1)S(1)}, bf16[288,128]{1,0:T(8,128)(2,1)S(1)}, u32[]{:S(2)}, u32[]{:S(2)}) %collective-permute-start.11) | collective-permute-done | bytes 73760 | tf_op jit(solution)/shard_map/ppermute | solution.py:429
  67.9 0.8 %shard_map.115 = bf16[1,2,128,128]{3,2,1,0:T(8,128)(2,1)} custom-call(bf16[2,128,128]{2,1,0:T(8,128)(2,1)S(1)} %get-tuple-element.73.resid, f32[2,8,128]{2,1,0:T(8,128)S(1)} %get-tuple-element.59.rest_1_.rest_9_.energy, f32[2,128,128]{2,1,0:T(8,128)S(1)} %get-tuple-element.64.rest_10_.live, f32[2,128,128]{2,1,0:T(8,128)S(1)} %get-tuple-element.77.keep, ...), custom_call_target="tpu_custom_call" | custom-call | bytes 262144 | tf_op jit(solution)/shard_map/pallas_call | solution.py:511
  (27 shorter events, 0.3 us)
Async XLA Ops:
  4.4 18.8 %collective-permute-start = (bf16[2,9,128,128]{3,2,1,0:T(8,128)(2,1)}, bf16[2,9,128,128]{3,2,1,0:T(8,128)(2,1)S(1)}, u32[]{:S(2)}, u32[]{:S(2)}) collective-permute-start(bf16[2,9,128,128]{3,2,1,0:T(8,128)(2,1)} %get-tuple-element.44), channel_id=1, source_target_pairs={{0,4},{5,1},{2,6},{7,3},{4,8},{9,5},{6,10},{11,7},{8,12},{13,9},{1... | collective-permute-start | bytes 1769480 | tf_op jit(solution)/shard_map/ppermute | solution.py:550
  9.4 14.2 %collective-permute-start.1 = (bf16[2,9,128,128]{3,2,1,0:T(8,128)(2,1)}, bf16[2,9,128,128]{3,2,1,0:T(8,128)(2,1)S(1)}, u32[]{:S(2)}, u32[]{:S(2)}) collective-permute-start(bf16[2,9,128,128]{3,2,1,0:T(8,128)(2,1)} %get-tuple-element.45), channel_id=1, source_target_pairs={{4,0},{1,5},{6,2},{3,7},{8,4},{5,9},{10,6},{7,11},{12,8},{9,13},{1... | collective-permute-start | bytes 1769480 | tf_op jit(solution)/shard_map/ppermute | solution.py:550
  10.7 16.1 %copy-start.6 = (bf16[1,2,128,128]{3,2,1,0:T(8,128)(2,1)S(1)}, bf16[1,2,128,128]{3,2,1,0:T(8,128)(2,1)}, u32[]{:S(2)}) copy-start(bf16[1,2,128,128]{3,2,1,0:T(8,128)(2,1)} %wave.1) | copy-start | bytes 196612
  10.7 24.4 %copy-start = (bf16[1,2,30,128,128]{4,3,2,1,0:T(8,128)(2,1)S(1)}, bf16[1,2,30,128,128]{4,3,2,1,0:T(8,128)(2,1)}, u32[]{:S(2)}) copy-start(bf16[1,2,30,128,128]{4,3,2,1,0:T(8,128)(2,1)} %left_hbm.5) | copy-start | bytes 5898244
  10.7 24.4 %copy-start.1 = (bf16[1,2,30,128,128]{4,3,2,1,0:T(8,128)(2,1)S(1)}, bf16[1,2,30,128,128]{4,3,2,1,0:T(8,128)(2,1)}, u32[]{:S(2)}) copy-start(bf16[1,2,30,128,128]{4,3,2,1,0:T(8,128)(2,1)} %right_hbm.5) | copy-start | bytes 5898244
  17.1 9.7 %copy-start.8 = (f32[1,2,30]{2,1,0:T(2,128)S(1)}, f32[1,2,30]{2,1,0:T(2,128)}, u32[]{:S(2)}) copy-start(f32[1,2,30]{2,1,0:T(2,128)} %coef.1) | copy-start | bytes 724
  17.1 9.7 %copy-start.9 = (f32[1,2]{1,0:T(1,128)S(1)}, f32[1,2]{1,0:T(1,128)}, u32[]{:S(2)}) copy-start(f32[1,2]{1,0:T(1,128)} %onsite.1) | copy-start | bytes 28
  17.2 9.7 %copy-start.10 = (s32[2]{0:T(128)S(1)}, s32[2]{0:T(128)}, u32[]{:S(2)}) copy-start(s32[2]{0:T(128)} %sizes.1) | copy-start | bytes 28
  17.2 31.2 %collective-permute-start.2 = (bf16[2,18,128,128]{3,2,1,0:T(8,128)(2,1)}, bf16[2,18,128,128]{3,2,1,0:T(8,128)(2,1)S(1)}, u32[]{:S(2)}, u32[]{:S(2)}) collective-permute-start(bf16[2,18,128,128]{3,2,1,0:T(8,128)(2,1)} %get-tuple-element.52), channel_id=1, source_target_pairs={{0,4},{5,1},{2,6},{7,3},{4,8},{9,5},{6,10},{11,7},{8,12},{13,9},{1... | collective-permute-start | bytes 3538952 | tf_op jit(solution)/shard_map/ppermute | solution.py:550
  21.9 28.4 %collective-permute-start.3 = (bf16[2,18,128,128]{3,2,1,0:T(8,128)(2,1)}, bf16[2,18,128,128]{3,2,1,0:T(8,128)(2,1)S(1)}, u32[]{:S(2)}, u32[]{:S(2)}) collective-permute-start(bf16[2,18,128,128]{3,2,1,0:T(8,128)(2,1)} %get-tuple-element.53), channel_id=1, source_target_pairs={{4,0},{1,5},{6,2},{3,7},{8,4},{5,9},{10,6},{7,11},{12,8},{9,13},{1... | collective-permute-start | bytes 3538952 | tf_op jit(solution)/shard_map/ppermute | solution.py:550
  23.6 0.9 %copy-start.2 = (bf16[2,3,128,128]{3,2,1,0:T(8,128)(2,1)S(1)}, bf16[2,3,128,128]{3,2,1,0:T(8,128)(2,1)}, u32[]{:S(2)}) copy-start(bf16[2,3,128,128]{3,2,1,0:T(8,128)(2,1)} %get-tuple-element.42.refs_0_) | copy-start | bytes 589828
  24.5 0.9 %copy-start.4 = (bf16[2,3,128,128]{3,2,1,0:T(8,128)(2,1)S(1)}, bf16[2,3,128,128]{3,2,1,0:T(8,128)(2,1)}, u32[]{:S(2)}) copy-start(bf16[2,3,128,128]{3,2,1,0:T(8,128)(2,1)} %get-tuple-element.43.refs_1_) | copy-start | bytes 589828
  25.4 0.7 %copy-start.3 = (bf16[2,3,128,128]{3,2,1,0:T(8,128)(2,1)}, bf16[2,3,128,128]{3,2,1,0:T(8,128)(2,1)S(1)}, u32[]{:S(2)}) copy-start(bf16[2,3,128,128]{3,2,1,0:T(8,128)(2,1)S(1)} %get-tuple-element.56) | copy-start | bytes 589828
  26.1 0.7 copy-start.5
  27.8 5.6 %collective-permute-start.6 = (bf16[1,2,128,128]{3,2,1,0:T(8,128)(2,1)S(1)}, bf16[1,2,128,128]{3,2,1,0:T(8,128)(2,1)S(1)}, u32[]{:S(2)}, u32[]{:S(2)}) collective-permute-start(bf16[1,2,128,128]{3,2,1,0:T(8,128)(2,1)S(1)} %bitcast.1), channel_id=1, source_target_pairs={{0,1},{1,0},{2,3},{3,2},{4,5},{5,4},{6,7},{7,6},{8,9},{9,8},{10,11... | collective-permute-start | bytes 196616 | tf_op jit(solution)/shard_map/ppermute | solution.py:525
  27.9 24.7 %collective-permute-start.4 = (bf16[2,3,128,128]{3,2,1,0:T(8,128)(2,1)}, bf16[2,3,128,128]{3,2,1,0:T(8,128)(2,1)S(1)}, u32[]{:S(2)}, u32[]{:S(2)}) collective-permute-start(bf16[2,3,128,128]{3,2,1,0:T(8,128)(2,1)} %copy-done.3), channel_id=1, source_target_pairs={{0,4},{5,1},{2,6},{7,3},{4,8},{9,5},{6,10},{11,7},{8,12},{13,9},{1... | collective-permute-start | bytes 589832 | tf_op jit(solution)/shard_map/ppermute | solution.py:550
  32.1 20.5 %collective-permute-start.5 = (bf16[2,3,128,128]{3,2,1,0:T(8,128)(2,1)}, bf16[2,3,128,128]{3,2,1,0:T(8,128)(2,1)S(1)}, u32[]{:S(2)}, u32[]{:S(2)}) collective-permute-start(bf16[2,3,128,128]{3,2,1,0:T(8,128)(2,1)} %copy-done.5), channel_id=1, source_target_pairs={{4,0},{1,5},{6,2},{3,7},{8,4},{5,9},{10,6},{7,11},{12,8},{9,13},{1... | collective-permute-start | bytes 589832 | tf_op jit(solution)/shard_map/ppermute | solution.py:550
  33.5 2.2 %copy-start.7 = (s32[1,2,30]{2,1,0:T(2,128)S(1)}, s32[1,2,30]{2,1,0:T(2,128)}, u32[]{:S(2)}) copy-start(s32[1,2,30]{2,1,0:T(2,128)} %rest_8_.1) | copy-start | bytes 724
  33.5 18.8 %collective-permute-start.7 = (bf16[2,2,128,128]{3,2,1,0:T(8,128)(2,1)S(1)}, bf16[2,2,128,128]{3,2,1,0:T(8,128)(2,1)S(1)}, u32[]{:S(2)}, u32[]{:S(2)}) collective-permute-start(bf16[2,2,128,128]{3,2,1,0:T(8,128)(2,1)S(1)} %pad_maximum_fusion), channel_id=1, source_target_pairs={{0,2},{1,3},{2,0},{3,1},{4,6},{5,7},{6,4},{7,5},{8,10},{9,11},{10,... | collective-permute-start | bytes 393224 | tf_op jit(solution)/shard_map/ppermute | solution.py:525
  53.5 1.4 %collective-permute-start.8 = (bf16[544,128]{1,0:T(8,128)(2,1)S(1)}, bf16[544,128]{1,0:T(8,128)(2,1)S(1)}, u32[]{:S(2)}, u32[]{:S(2)}) collective-permute-start(bf16[544,128]{1,0:T(8,128)(2,1)S(1)} %get-tuple-element.66), channel_id=1, source_target_pairs={{0,1},{1,0},{2,3},{3,2},{4,5},{5,4},{6,7},{7,6},{8,9},{9,8},{10,11... | collective-permute-start | bytes 417800 | tf_op jit(solution)/shard_map/ppermute | solution.py:429
  55.0 4.6 %collective-permute-start.9 = (bf16[288,128]{1,0:T(8,128)(2,1)S(1)}, bf16[288,128]{1,0:T(8,128)(2,1)S(1)}, u32[]{:S(2)}, u32[]{:S(2)}) collective-permute-start(bf16[288,128]{1,0:T(8,128)(2,1)S(1)} %get-tuple-element.69), channel_id=1, source_target_pairs={{0,2},{1,3},{2,0},{3,1},{4,6},{5,7},{6,4},{7,5},{8,10},{9,11},{10,... | collective-permute-start | bytes 221192 | tf_op jit(solution)/shard_map/ppermute | solution.py:429
  62.0 1.4 %collective-permute-start.10 = (bf16[544,128]{1,0:T(8,128)(2,1)S(1)}, bf16[544,128]{1,0:T(8,128)(2,1)S(1)}, u32[]{:S(2)}, u32[]{:S(2)}) collective-permute-start(bf16[544,128]{1,0:T(8,128)(2,1)S(1)} %get-tuple-element.75), channel_id=1, source_target_pairs={{0,1},{1,0},{2,3},{3,2},{4,5},{5,4},{6,7},{7,6},{8,9},{9,8},{10,11... | collective-permute-start | bytes 417800 | tf_op jit(solution)/shard_map/ppermute | solution.py:429
  63.5 4.4 %collective-permute-start.11 = (bf16[288,128]{1,0:T(8,128)(2,1)S(1)}, bf16[288,128]{1,0:T(8,128)(2,1)S(1)}, u32[]{:S(2)}, u32[]{:S(2)}) collective-permute-start(bf16[288,128]{1,0:T(8,128)(2,1)S(1)} %get-tuple-element.78), channel_id=1, source_target_pairs={{0,2},{1,3},{2,0},{3,1},{4,6},{5,7},{6,4},{7,5},{8,10},{9,11},{10,... | collective-permute-start | bytes 221192 | tf_op jit(solution)/shard_map/ppermute | solution.py:429

commit v7 on v6

--- a/solution.py
+++ b/solution.py
@@ -466,7 +466,7 @@
         def load(k, at, unit):
             return lefts[i][k, pl.ds(at, unit)], rights[i][k, pl.ds(at, unit)]
 
-        apply_blocks(load, count, vectors, start, acc, weights, routes, unit_of(count))
+        apply_blocks(load, count, vectors, start, acc, weights, routes, unit_of(count, 18))
     me = lax.axis_index("sector")
     split_halves(acc, groups, pd, b, lax.rem(me, 2), send, keep, total)
     image_copy.wait()

time: 69 us -> 68.5 us (level)
  no operation moved by 1% of the time
where the time goes in v7:
time: 68.5 us; the launch traced here: 68.2 us
  starting transfers between devices  23.1 us (34%)
  waiting for transfers between devices  22.8 us (33%)
  Pallas kernels  18.2 us (27%)
  local copies, waits for them, and re-layouts  3.27 us (5%)
  between operations  0.87 us (1%)
    ppermute x3, starting transfers between devices, pass_on(): lax.ppermute(grown[0], axes, first)  13.9 us
    ppermute x3, waiting for transfers between devices, pass_on(): lax.ppermute(grown[0], axes, first)  12.2 us
    pallas_call x2, Pallas kernels, grow(): call(functools.partial(grow_kernel, bounds), [jax.ShapeDtypeStruct((8, 12...  10.2 us
    ppermute x4, waiting for transfers between devices, exchange(): lax.ppermute(send, 'sector', [(i, i ^ 1 << stage) for i in range(sectors)])  8.23 us
    ppermute x3, starting transfers between devices, pass_on(): lax.ppermute(grown[1], axes, second)  3.88 us
    pallas_call x3, Pallas kernels, first_apply(): call(functools.partial(first_kernel, chunk, is_first, is_last, groups), o...  3.65 us
    ppermute x4, starting transfers between devices, exchange(): lax.ppermute(send, 'sector', [(i, i ^ 1 << stage) for i in range(sectors)])  3.63 us
    unnamed x22, local copies, waits for them, and re-layouts  3.27 us
  transfers between devices with their start and end apart: 12, of which 8 were waited for; matrix products, arithmetic and copies ran while one was open for 0% of the time, Pallas kernels for 16%

profile of v7, /device:TPU:0, one launch (start us, length us, event | category | flops | bytes accessed | tf_op | source)
XLA Modules:
  0.0 68.2 jit_solution(3953835742359974096)
XLA Ops:
  0.6 3.8 %shard_map.104 = (f32[8,128]{1,0:T(8,128)}, bf16[2,9,128,128]{3,2,1,0:T(8,128)(2,1)}, bf16[2,9,128,128]{3,2,1,0:T(8,128)(2,1)}) custom-call(bf16[1,2,30,128,128]{4,3,2,1,0:T(8,128)(2,1)} %left_hbm.5, bf16[1,2,30,128,128]{4,3,2,1,0:T(8,128)(2,1)} %right_hbm.5, bf16[1,2,128,128]{3,2,1,0:T(8,128)(2,1)} %edge_l_hbm.3, bf16[1,2,128,128]{3,2,1,0:T(8,128)(2,1)} %edge_r_hbm.3), custom_call_target="tpu_custom_call" | custom-call | flops 301989888 | bytes 2359296 | tf_op jit(solution)/shard_map/pallas_call | solution.py:134
  4.4 5.0 %collective-permute-start = (bf16[2,9,128,128]{3,2,1,0:T(8,128)(2,1)}, bf16[2,9,128,128]{3,2,1,0:T(8,128)(2,1)S(1)}, u32[]{:S(2)}, u32[]{:S(2)}) collective-permute-start(bf16[2,9,128,128]{3,2,1,0:T(8,128)(2,1)} %get-tuple-element.44), channel_id=1, source_target_pairs={{0,4},{5,1},{2,6},{7,3},{4,8},{9,5},{6,10},{11,7},{8,12},{13,9},{1... | collective-permute-start | bytes 1769480 | tf_op jit(solution)/shard_map/ppermute | solution.py:550
  9.4 1.3 %collective-permute-start.1 = (bf16[2,9,128,128]{3,2,1,0:T(8,128)(2,1)}, bf16[2,9,128,128]{3,2,1,0:T(8,128)(2,1)S(1)}, u32[]{:S(2)}, u32[]{:S(2)}) collective-permute-start(bf16[2,9,128,128]{3,2,1,0:T(8,128)(2,1)} %get-tuple-element.45), channel_id=1, source_target_pairs={{4,0},{1,5},{6,2},{3,7},{8,4},{5,9},{10,6},{7,11},{12,8},{9,13},{1... | collective-permute-start | bytes 1769480 | tf_op jit(solution)/shard_map/ppermute | solution.py:550
  10.7 6.4 %shard_map.105 = (f32[8,128]{1,0:T(8,128)}, bf16[2,18,128,128]{3,2,1,0:T(8,128)(2,1)}, bf16[2,18,128,128]{3,2,1,0:T(8,128)(2,1)}, bf16[2,3,128,128]{3,2,1,0:T(8,128)(2,1)}, bf16[2,3,128,128]{3,2,1,0:T(8,128)(2,1)}) custom-call(bf16[1,2,30,128,128]{4,3,2,1,0:T(8,128)(2,1)} %left_hbm.5, bf16[1,2,30,128,128]{4,3,2,1,0:T(8,128)(2,1)} %right_hbm.5, ...), custom_call_target="tpu_custom_call" | custom-call | flops 704643072 | bytes 5505024 | tf_op jit(solution)/shard_map/pallas_call | solution.py:134
  17.2 4.7 %collective-permute-start.2 = (bf16[2,18,128,128]{3,2,1,0:T(8,128)(2,1)}, bf16[2,18,128,128]{3,2,1,0:T(8,128)(2,1)S(1)}, u32[]{:S(2)}, u32[]{:S(2)}) collective-permute-start(bf16[2,18,128,128]{3,2,1,0:T(8,128)(2,1)} %get-tuple-element.52), channel_id=1, source_target_pairs={{0,4},{5,1},{2,6},{7,3},{4,8},{9,5},{6,10},{11,7},{8,12},{13,9},{1... | collective-permute-start | bytes 3538952 | tf_op jit(solution)/shard_map/ppermute | solution.py:550
  21.9 1.3 %collective-permute-start.3 = (bf16[2,18,128,128]{3,2,1,0:T(8,128)(2,1)}, bf16[2,18,128,128]{3,2,1,0:T(8,128)(2,1)S(1)}, u32[]{:S(2)}, u32[]{:S(2)}) collective-permute-start(bf16[2,18,128,128]{3,2,1,0:T(8,128)(2,1)} %get-tuple-element.53), channel_id=1, source_target_pairs={{4,0},{1,5},{6,2},{3,7},{8,4},{5,9},{10,6},{7,11},{12,8},{9,13},{1... | collective-permute-start | bytes 3538952 | tf_op jit(solution)/shard_map/ppermute | solution.py:550
  23.2 0.3 collective-permute-done.1.refs_3_.got_y
  23.6 0.9 %copy-done.2 = bf16[2,3,128,128]{3,2,1,0:T(8,128)(2,1)S(1)} copy-done((bf16[2,3,128,128]{3,2,1,0:T(8,128)(2,1)S(1)}, bf16[2,3,128,128]{3,2,1,0:T(8,128)(2,1)}, u32[]{:S(2)}) %copy-start.2) | copy-done | bytes 196632
  24.5 0.9 %copy-done.4 = bf16[2,3,128,128]{3,2,1,0:T(8,128)(2,1)S(1)} copy-done((bf16[2,3,128,128]{3,2,1,0:T(8,128)(2,1)S(1)}, bf16[2,3,128,128]{3,2,1,0:T(8,128)(2,1)}, u32[]{:S(2)}) %copy-start.4) | copy-done | bytes 196632
  25.4 0.7 %copy-done.3 = bf16[2,3,128,128]{3,2,1,0:T(8,128)(2,1)} copy-done((bf16[2,3,128,128]{3,2,1,0:T(8,128)(2,1)}, bf16[2,3,128,128]{3,2,1,0:T(8,128)(2,1)S(1)}, u32[]{:S(2)}) %copy-start.3) | copy-done | bytes 196632
  26.1 0.7 copy-done.5
  26.8 1.0 %shard_map.107 = (bf16[2,128,128]{2,1,0:T(8,128)(2,1)S(1)}, f32[2,128,128]{2,1,0:T(8,128)S(1)}, f32[2,30,8,128]{3,2,1,0:T(8,128)S(1)}, f32[2,8,128]{2,1,0:T(8,128)S(1)}) custom-call(bf16[1,2,128,128]{3,2,1,0:T(8,128)(2,1)S(1)} %copy-done.6, f32[1,2,30]{2,1,0:T(2,128)S(1)} %copy-done.8, f32[1,2]{1,0:T(1,128)S(1)} %copy-done.9, s32[2]{0:T(128)S(1)} %copy-done.10, ...), custom_call_target="tpu_custom_call" | custom-call | bytes 131072 | tf_op jit(solution)/shard_map/pallas_call | solution.py:233
  27.8 0.1 collective-permute-start.6
  27.9 4.2 %collective-permute-start.4 = (bf16[2,3,128,128]{3,2,1,0:T(8,128)(2,1)}, bf16[2,3,128,128]{3,2,1,0:T(8,128)(2,1)S(1)}, u32[]{:S(2)}, u32[]{:S(2)}) collective-permute-start(bf16[2,3,128,128]{3,2,1,0:T(8,128)(2,1)} %copy-done.3), channel_id=1, source_target_pairs={{0,4},{5,1},{2,6},{7,3},{4,8},{9,5},{6,10},{11,7},{8,12},{13,9},{1... | collective-permute-start | bytes 589832 | tf_op jit(solution)/shard_map/ppermute | solution.py:550
  32.1 1.3 %collective-permute-start.5 = (bf16[2,3,128,128]{3,2,1,0:T(8,128)(2,1)}, bf16[2,3,128,128]{3,2,1,0:T(8,128)(2,1)S(1)}, u32[]{:S(2)}, u32[]{:S(2)}) collective-permute-start(bf16[2,3,128,128]{3,2,1,0:T(8,128)(2,1)} %copy-done.5), channel_id=1, source_target_pairs={{4,0},{1,5},{6,2},{3,7},{8,4},{5,9},{10,6},{7,11},{12,8},{9,13},{1... | collective-permute-start | bytes 589832 | tf_op jit(solution)/shard_map/ppermute | solution.py:550
  33.5 1.6 %collective-permute-start.7 = (bf16[2,2,128,128]{3,2,1,0:T(8,128)(2,1)S(1)}, bf16[2,2,128,128]{3,2,1,0:T(8,128)(2,1)S(1)}, u32[]{:S(2)}, u32[]{:S(2)}) collective-permute-start(bf16[2,2,128,128]{3,2,1,0:T(8,128)(2,1)S(1)} %pad_maximum_fusion), channel_id=1, source_target_pairs={{0,2},{1,3},{2,0},{3,1},{4,6},{5,7},{6,4},{7,5},{8,10},{9,11},{10,... | collective-permute-start | bytes 393224 | tf_op jit(solution)/shard_map/ppermute | solution.py:525
  35.1 0.6 shard_map.108
  35.6 0.9 %shard_map.109 = (bf16[2,9,128,128]{3,2,1,0:T(8,128)(2,1)S(1)}, bf16[2,9,128,128]{3,2,1,0:T(8,128)(2,1)S(1)}, f32[8,128,128]{2,1,0:T(8,128)S(1)}) custom-call(bf16[2,30,128,128]{3,2,1,0:T(8,128)(2,1)S(1)} %get-tuple-element.48.own_l, bf16[2,30,128,128]{3,2,1,0:T(8,128)(2,1)S(1)} %get-tuple-element.49.own_r, ...), custom_call_target="tpu_custom_call" | custom-call | flops 150994944 | bytes 1179648 | tf_op jit(solution)/shard_map/pallas_call | solution.py:384
  36.5 11.9 %collective-permute-done.2.got_x = bf16[2,18,128,128]{3,2,1,0:T(8,128)(2,1)S(1)} collective-permute-done((bf16[2,18,128,128]{3,2,1,0:T(8,128)(2,1)}, bf16[2,18,128,128]{3,2,1,0:T(8,128)(2,1)S(1)}, u32[]{:S(2)}, u32[]{:S(2)}) %collective-permute-start.2) | collective-permute-done | bytes 1179680 | tf_op jit(solution)/shard_map/ppermute | solution.py:550
  48.4 2.0 %collective-permute-done.3.got_y = bf16[2,18,128,128]{3,2,1,0:T(8,128)(2,1)S(1)} collective-permute-done((bf16[2,18,128,128]{3,2,1,0:T(8,128)(2,1)}, bf16[2,18,128,128]{3,2,1,0:T(8,128)(2,1)S(1)}, u32[]{:S(2)}, u32[]{:S(2)}) %collective-permute-start.3) | collective-permute-done | bytes 1179680 | tf_op jit(solution)/shard_map/ppermute | solution.py:550
  50.4 1.9 %shard_map.110 = (bf16[2,18,128,128]{3,2,1,0:T(8,128)(2,1)S(1)}, bf16[2,18,128,128]{3,2,1,0:T(8,128)(2,1)S(1)}, f32[8,128,128]{2,1,0:T(8,128)S(1)}) custom-call(bf16[2,30,128,128]{3,2,1,0:T(8,128)(2,1)S(1)} %get-tuple-element.48.own_l, bf16[2,30,128,128]{3,2,1,0:T(8,128)(2,1)S(1)} %get-tuple-element.49.own_r, ...), custom_call_target="tpu_custom_call" | custom-call | flops 301989888 | bytes 2359296 | tf_op jit(solution)/shard_map/pallas_call | solution.py:384
  52.3 0.4 collective-permute-done.4.got_x
  52.6 0.9 %shard_map.111 = (bf16[2,3,128,128]{3,2,1,0:T(8,128)(2,1)S(1)}, bf16[2,3,128,128]{3,2,1,0:T(8,128)(2,1)S(1)}, bf16[544,128]{1,0:T(8,128)(2,1)S(1)}, f32[4,128,12...) custom-call(bf16[2,30,128,128]{3,2,1,0:T(8,128)(2,1)S(1)} %get-tuple-element.48.own_l, ...), custom_call_target="tpu_custom_call" | custom-call | flops 50331648 | bytes 393216 | tf_op jit(solution)/shard_map/pallas_call | solution.py:384
  53.5 0.4 collective-permute-start.8
  53.9 1.0 %collective-permute-done.8.got = bf16[544,128]{1,0:T(8,128)(2,1)S(1)} collective-permute-done((bf16[544,128]{1,0:T(8,128)(2,1)S(1)}, bf16[544,128]{1,0:T(8,128)(2,1)S(1)}, u32[]{:S(2)}, u32[]{:S(2)}) %collective-permute-start.8) | collective-permute-done | bytes 139296 | tf_op jit(solution)/shard_map/ppermute | solution.py:429
  55.0 1.6 %collective-permute-start.9 = (bf16[288,128]{1,0:T(8,128)(2,1)S(1)}, bf16[288,128]{1,0:T(8,128)(2,1)S(1)}, u32[]{:S(2)}, u32[]{:S(2)}) collective-permute-start(bf16[288,128]{1,0:T(8,128)(2,1)S(1)} %get-tuple-element.69), channel_id=1, source_target_pairs={{0,2},{1,3},{2,0},{3,1},{4,6},{5,7},{6,4},{7,5},{8,10},{9,11},{10,... | collective-permute-start | bytes 221192 | tf_op jit(solution)/shard_map/ppermute | solution.py:429
  56.6 3.0 %collective-permute-done.9.rest_12_ = bf16[288,128]{1,0:T(8,128)(2,1)S(1)} collective-permute-done((bf16[288,128]{1,0:T(8,128)(2,1)S(1)}, bf16[288,128]{1,0:T(8,128)(2,1)S(1)}, u32[]{:S(2)}, u32[]{:S(2)}) %collective-permute-start.9) | collective-permute-done | bytes 73760 | tf_op jit(solution)/shard_map/ppermute | solution.py:429
  59.6 1.9 %shard_map.113 = (bf16[1,2,128,128]{3,2,1,0:T(8,128)(2,1)}, bf16[2,128,128]{2,1,0:T(8,128)(2,1)S(1)}, bf16[544,128]{1,0:T(8,128)(2,1)S(1)}, f32[4,128,128]{2,1,0:T(8,128)S(1)}, f32[8,128]{1,0:T(8,128)S(1)}) custom-call(bf16[2,9,128,128]{3,2,1,0:T(8,128)(2,1)S(1)} %get-tuple-element.51.rest_0_, bf16[2,18,128,128]{3,2,1,0:T(8,128)(2,1)S(1)} %get-tuple-element.55.rest_1_, ...), custom_call_target="tpu_custom_call" | custom-call | flops 503316480 | bytes 3932160 | tf_op jit(solution)/shard_map/pallas_call | solution.py:479
  61.6 1.3 %collective-permute-done.10.got = bf16[544,128]{1,0:T(8,128)(2,1)S(1)} collective-permute-done((bf16[544,128]{1,0:T(8,128)(2,1)S(1)}, bf16[544,128]{1,0:T(8,128)(2,1)S(1)}, u32[]{:S(2)}, u32[]{:S(2)}) %collective-permute-start.10) | collective-permute-done | bytes 139296 | tf_op jit(solution)/shard_map/ppermute | solution.py:429
  63.0 1.6 %collective-permute-start.11 = (bf16[288,128]{1,0:T(8,128)(2,1)S(1)}, bf16[288,128]{1,0:T(8,128)(2,1)S(1)}, u32[]{:S(2)}, u32[]{:S(2)}) collective-permute-start(bf16[288,128]{1,0:T(8,128)(2,1)S(1)} %get-tuple-element.78), channel_id=1, source_target_pairs={{0,2},{1,3},{2,0},{3,1},{4,6},{5,7},{6,4},{7,5},{8,10},{9,11},{10,... | collective-permute-start | bytes 221192 | tf_op jit(solution)/shard_map/ppermute | solution.py:429
  64.6 2.9 %collective-permute-done.11.got = bf16[288,128]{1,0:T(8,128)(2,1)S(1)} collective-permute-done((bf16[288,128]{1,0:T(8,128)(2,1)S(1)}, bf16[288,128]{1,0:T(8,128)(2,1)S(1)}, u32[]{:S(2)}, u32[]{:S(2)}) %collective-permute-start.11) | collective-permute-done | bytes 73760 | tf_op jit(solution)/shard_map/ppermute | solution.py:429
  67.4 0.8 %shard_map.115 = bf16[1,2,128,128]{3,2,1,0:T(8,128)(2,1)} custom-call(bf16[2,128,128]{2,1,0:T(8,128)(2,1)S(1)} %get-tuple-element.73.resid, f32[2,8,128]{2,1,0:T(8,128)S(1)} %get-tuple-element.59.rest_1_.rest_9_.energy, f32[2,128,128]{2,1,0:T(8,128)S(1)} %get-tuple-element.64.rest_10_.live, f32[2,128,128]{2,1,0:T(8,128)S(1)} %get-tuple-element.77.keep, ...), custom_call_target="tpu_custom_call" | custom-call | bytes 262144 | tf_op jit(solution)/shard_map/pallas_call | solution.py:511
  (27 shorter events, 0.3 us)
Async XLA Ops:
  4.4 18.8 %collective-permute-start = (bf16[2,9,128,128]{3,2,1,0:T(8,128)(2,1)}, bf16[2,9,128,128]{3,2,1,0:T(8,128)(2,1)S(1)}, u32[]{:S(2)}, u32[]{:S(2)}) collective-permute-start(bf16[2,9,128,128]{3,2,1,0:T(8,128)(2,1)} %get-tuple-element.44), channel_id=1, source_target_pairs={{0,4},{5,1},{2,6},{7,3},{4,8},{9,5},{6,10},{11,7},{8,12},{13,9},{1... | collective-permute-start | bytes 1769480 | tf_op jit(solution)/shard_map/ppermute | solution.py:550
  9.4 14.2 %collective-permute-start.1 = (bf16[2,9,128,128]{3,2,1,0:T(8,128)(2,1)}, bf16[2,9,128,128]{3,2,1,0:T(8,128)(2,1)S(1)}, u32[]{:S(2)}, u32[]{:S(2)}) collective-permute-start(bf16[2,9,128,128]{3,2,1,0:T(8,128)(2,1)} %get-tuple-element.45), channel_id=1, source_target_pairs={{4,0},{1,5},{6,2},{3,7},{8,4},{5,9},{10,6},{7,11},{12,8},{9,13},{1... | collective-permute-start | bytes 1769480 | tf_op jit(solution)/shard_map/ppermute | solution.py:550
  10.7 16.1 %copy-start.6 = (bf16[1,2,128,128]{3,2,1,0:T(8,128)(2,1)S(1)}, bf16[1,2,128,128]{3,2,1,0:T(8,128)(2,1)}, u32[]{:S(2)}) copy-start(bf16[1,2,128,128]{3,2,1,0:T(8,128)(2,1)} %wave.1) | copy-start | bytes 196612
  10.7 24.4 %copy-start = (bf16[1,2,30,128,128]{4,3,2,1,0:T(8,128)(2,1)S(1)}, bf16[1,2,30,128,128]{4,3,2,1,0:T(8,128)(2,1)}, u32[]{:S(2)}) copy-start(bf16[1,2,30,128,128]{4,3,2,1,0:T(8,128)(2,1)} %left_hbm.5) | copy-start | bytes 5898244
  10.7 24.4 %copy-start.1 = (bf16[1,2,30,128,128]{4,3,2,1,0:T(8,128)(2,1)S(1)}, bf16[1,2,30,128,128]{4,3,2,1,0:T(8,128)(2,1)}, u32[]{:S(2)}) copy-start(bf16[1,2,30,128,128]{4,3,2,1,0:T(8,128)(2,1)} %right_hbm.5) | copy-start | bytes 5898244
  17.1 9.7 %copy-start.8 = (f32[1,2,30]{2,1,0:T(2,128)S(1)}, f32[1,2,30]{2,1,0:T(2,128)}, u32[]{:S(2)}) copy-start(f32[1,2,30]{2,1,0:T(2,128)} %coef.1) | copy-start | bytes 724
  17.1 9.7 %copy-start.9 = (f32[1,2]{1,0:T(1,128)S(1)}, f32[1,2]{1,0:T(1,128)}, u32[]{:S(2)}) copy-start(f32[1,2]{1,0:T(1,128)} %onsite.1) | copy-start | bytes 28
  17.2 9.7 %copy-start.10 = (s32[2]{0:T(128)S(1)}, s32[2]{0:T(128)}, u32[]{:S(2)}) copy-start(s32[2]{0:T(128)} %sizes.1) | copy-start | bytes 28
  17.2 31.2 %collective-permute-start.2 = (bf16[2,18,128,128]{3,2,1,0:T(8,128)(2,1)}, bf16[2,18,128,128]{3,2,1,0:T(8,128)(2,1)S(1)}, u32[]{:S(2)}, u32[]{:S(2)}) collective-permute-start(bf16[2,18,128,128]{3,2,1,0:T(8,128)(2,1)} %get-tuple-element.52), channel_id=1, source_target_pairs={{0,4},{5,1},{2,6},{7,3},{4,8},{9,5},{6,10},{11,7},{8,12},{13,9},{1... | collective-permute-start | bytes 3538952 | tf_op jit(solution)/shard_map/ppermute | solution.py:550
  21.9 28.4 %collective-permute-start.3 = (bf16[2,18,128,128]{3,2,1,0:T(8,128)(2,1)}, bf16[2,18,128,128]{3,2,1,0:T(8,128)(2,1)S(1)}, u32[]{:S(2)}, u32[]{:S(2)}) collective-permute-start(bf16[2,18,128,128]{3,2,1,0:T(8,128)(2,1)} %get-tuple-element.53), channel_id=1, source_target_pairs={{4,0},{1,5},{6,2},{3,7},{8,4},{5,9},{10,6},{7,11},{12,8},{9,13},{1... | collective-permute-start | bytes 3538952 | tf_op jit(solution)/shard_map/ppermute | solution.py:550
  23.6 0.9 %copy-start.2 = (bf16[2,3,128,128]{3,2,1,0:T(8,128)(2,1)S(1)}, bf16[2,3,128,128]{3,2,1,0:T(8,128)(2,1)}, u32[]{:S(2)}) copy-start(bf16[2,3,128,128]{3,2,1,0:T(8,128)(2,1)} %get-tuple-element.42.refs_0_) | copy-start | bytes 589828
  24.5 0.9 %copy-start.4 = (bf16[2,3,128,128]{3,2,1,0:T(8,128)(2,1)S(1)}, bf16[2,3,128,128]{3,2,1,0:T(8,128)(2,1)}, u32[]{:S(2)}) copy-start(bf16[2,3,128,128]{3,2,1,0:T(8,128)(2,1)} %get-tuple-element.43.refs_1_) | copy-start | bytes 589828
  25.4 0.7 %copy-start.3 = (bf16[2,3,128,128]{3,2,1,0:T(8,128)(2,1)}, bf16[2,3,128,128]{3,2,1,0:T(8,128)(2,1)S(1)}, u32[]{:S(2)}) copy-start(bf16[2,3,128,128]{3,2,1,0:T(8,128)(2,1)S(1)} %get-tuple-element.56) | copy-start | bytes 589828
  26.1 0.7 %copy-start.5 = (bf16[2,3,128,128]{3,2,1,0:T(8,128)(2,1)}, bf16[2,3,128,128]{3,2,1,0:T(8,128)(2,1)S(1)}, u32[]{:S(2)}) copy-start(bf16[2,3,128,128]{3,2,1,0:T(8,128)(2,1)S(1)} %get-tuple-element.57) | copy-start | bytes 589828
  27.8 5.6 %collective-permute-start.6 = (bf16[1,2,128,128]{3,2,1,0:T(8,128)(2,1)S(1)}, bf16[1,2,128,128]{3,2,1,0:T(8,128)(2,1)S(1)}, u32[]{:S(2)}, u32[]{:S(2)}) collective-permute-start(bf16[1,2,128,128]{3,2,1,0:T(8,128)(2,1)S(1)} %bitcast.1), channel_id=1, source_target_pairs={{0,1},{1,0},{2,3},{3,2},{4,5},{5,4},{6,7},{7,6},{8,9},{9,8},{10,11... | collective-permute-start | bytes 196616 | tf_op jit(solution)/shard_map/ppermute | solution.py:525
  27.9 24.7 %collective-permute-start.4 = (bf16[2,3,128,128]{3,2,1,0:T(8,128)(2,1)}, bf16[2,3,128,128]{3,2,1,0:T(8,128)(2,1)S(1)}, u32[]{:S(2)}, u32[]{:S(2)}) collective-permute-start(bf16[2,3,128,128]{3,2,1,0:T(8,128)(2,1)} %copy-done.3), channel_id=1, source_target_pairs={{0,4},{5,1},{2,6},{7,3},{4,8},{9,5},{6,10},{11,7},{8,12},{13,9},{1... | collective-permute-start | bytes 589832 | tf_op jit(solution)/shard_map/ppermute | solution.py:550
  32.1 20.5 %collective-permute-start.5 = (bf16[2,3,128,128]{3,2,1,0:T(8,128)(2,1)}, bf16[2,3,128,128]{3,2,1,0:T(8,128)(2,1)S(1)}, u32[]{:S(2)}, u32[]{:S(2)}) collective-permute-start(bf16[2,3,128,128]{3,2,1,0:T(8,128)(2,1)} %copy-done.5), channel_id=1, source_target_pairs={{4,0},{1,5},{6,2},{3,7},{8,4},{5,9},{10,6},{7,11},{12,8},{9,13},{1... | collective-permute-start | bytes 589832 | tf_op jit(solution)/shard_map/ppermute | solution.py:550
  33.5 2.2 %copy-start.7 = (s32[1,2,30]{2,1,0:T(2,128)S(1)}, s32[1,2,30]{2,1,0:T(2,128)}, u32[]{:S(2)}) copy-start(s32[1,2,30]{2,1,0:T(2,128)} %rest_8_.1) | copy-start | bytes 724
  33.5 18.8 %collective-permute-start.7 = (bf16[2,2,128,128]{3,2,1,0:T(8,128)(2,1)S(1)}, bf16[2,2,128,128]{3,2,1,0:T(8,128)(2,1)S(1)}, u32[]{:S(2)}, u32[]{:S(2)}) collective-permute-start(bf16[2,2,128,128]{3,2,1,0:T(8,128)(2,1)S(1)} %pad_maximum_fusion), channel_id=1, source_target_pairs={{0,2},{1,3},{2,0},{3,1},{4,6},{5,7},{6,4},{7,5},{8,10},{9,11},{10,... | collective-permute-start | bytes 393224 | tf_op jit(solution)/shard_map/ppermute | solution.py:525
  53.5 1.4 %collective-permute-start.8 = (bf16[544,128]{1,0:T(8,128)(2,1)S(1)}, bf16[544,128]{1,0:T(8,128)(2,1)S(1)}, u32[]{:S(2)}, u32[]{:S(2)}) collective-permute-start(bf16[544,128]{1,0:T(8,128)(2,1)S(1)} %get-tuple-element.66), channel_id=1, source_target_pairs={{0,1},{1,0},{2,3},{3,2},{4,5},{5,4},{6,7},{7,6},{8,9},{9,8},{10,11... | collective-permute-start | bytes 417800 | tf_op jit(solution)/shard_map/ppermute | solution.py:429
  55.0 4.6 %collective-permute-start.9 = (bf16[288,128]{1,0:T(8,128)(2,1)S(1)}, bf16[288,128]{1,0:T(8,128)(2,1)S(1)}, u32[]{:S(2)}, u32[]{:S(2)}) collective-permute-start(bf16[288,128]{1,0:T(8,128)(2,1)S(1)} %get-tuple-element.69), channel_id=1, source_target_pairs={{0,2},{1,3},{2,0},{3,1},{4,6},{5,7},{6,4},{7,5},{8,10},{9,11},{10,... | collective-permute-start | bytes 221192 | tf_op jit(solution)/shard_map/ppermute | solution.py:429
  61.5 1.4 %collective-permute-start.10 = (bf16[544,128]{1,0:T(8,128)(2,1)S(1)}, bf16[544,128]{1,0:T(8,128)(2,1)S(1)}, u32[]{:S(2)}, u32[]{:S(2)}) collective-permute-start(bf16[544,128]{1,0:T(8,128)(2,1)S(1)} %get-tuple-element.75), channel_id=1, source_target_pairs={{0,1},{1,0},{2,3},{3,2},{4,5},{5,4},{6,7},{7,6},{8,9},{9,8},{10,11... | collective-permute-start | bytes 417800 | tf_op jit(solution)/shard_map/ppermute | solution.py:429
  63.0 4.4 %collective-permute-start.11 = (bf16[288,128]{1,0:T(8,128)(2,1)S(1)}, bf16[288,128]{1,0:T(8,128)(2,1)S(1)}, u32[]{:S(2)}, u32[]{:S(2)}) collective-permute-start(bf16[288,128]{1,0:T(8,128)(2,1)S(1)} %get-tuple-element.78), channel_id=1, source_target_pairs={{0,2},{1,3},{2,0},{3,1},{4,6},{5,7},{6,4},{7,5},{8,10},{9,11},{10,... | collective-permute-start | bytes 221192 | tf_op jit(solution)/shard_map/ppermute | solution.py:429

commit v8 on v7

--- a/solution.py
+++ b/solution.py
@@ -147,6 +147,13 @@
     return res[0], [(res[2 * i + 1], res[2 * i + 2]) for i in range(n)]
 
 
+def raw(env_left, env_right, edge_left, edge_right, count):
+    left = jnp.concatenate([env_left[0, :, :count], edge_left[0][:, None]], axis=1)
+    right = jnp.concatenate([env_right[0, :, :count], edge_right[0][:, None]], axis=1)
+    up = up_first()
+    return jnp.where(up, left, right), jnp.where(up, right, left)
+
+
 def gate_kernel(*refs):
     refs[-1][...] = jnp.zeros_like(refs[-1])
 
@@ -327,8 +334,16 @@
     def load(k, at, unit):
         here, there = pl.ds(at, unit), pl.ds(start + at, unit)
         got_first, got_second = got_x[k, here], got_y[k, here]
-        left = jnp.where(up, got_first, got_second) + own_l[k, there]
-        right = jnp.where(up, got_second, got_first) + own_r[k, there]
+        left, right = jnp.where(up, got_first, got_second), jnp.where(up, got_second, got_first)
+        if is_first:
+            edge_first, edge_second = got_x[k, count], got_y[k, count]
+            e, f = jnp.where(up, edge_first, edge_second), jnp.where(up, edge_second, edge_first)
+            e_t = e.T
+            inner = jnp.concatenate([dot(e_t, left[u]).astype(bf16) for u in range(unit)], axis=0)
+            left = dot(inner, e).astype(bf16).reshape(left.shape)
+            inner = [dot(f, right[u]).astype(bf16) for u in range(unit)]
+            right = jnp.stack([dot_t(f, x).astype(bf16) for x in inner])
+        left, right = left + own_l[k, there], right + own_r[k, there]
         new_l[k, here] = left
         new_r[k, here] = right
         return left, right
@@ -549,9 +564,9 @@
         axes = ("section", "sector")
         return lax.ppermute(grown[0], axes, first), lax.ppermute(grown[1], axes, second)
 
-    token, (head,) = grow(env_left, env_right, edge_left, edge_right, bounds[:1], (), VMEM_LARGE)
+    head = raw(env_left, env_right, edge_left, edge_right, bounds[0][1])
     got = [pass_on(head)]
-    _, (middle, last) = grow(env_left, env_right, edge_left, edge_right, bounds[1:], (token,), VMEM_LARGE)
+    _, (middle, last) = grow(env_left, env_right, edge_left, edge_right, bounds[1:], head[:1], VMEM_LARGE)
     got.append(pass_on(middle))
     grown, token = gate(last, got[0])
     m, live, weights, energy = prepare(wave_blocks, mpo_coef, onsite, sector_sizes, token)

time: 68.5 us -> 67.5 us (0.985)
  Pallas kernels: 18.2 us -> 15.1 us
  waiting for transfers between devices: 22.8 us -> 25.9 us
  local copies, waits for them, and re-layouts: 3.27 us -> 1.46 us
    pallas_call x2 -> x1, Pallas kernels: 10.2 us -> 6.4 us  [grow(): call(functools.partial(grow_kernel, bounds), [jax.ShapeDtypeStruct((8, 12...]
    unnamed x22 -> x20, local copies, waits for them, and re-layouts: 3.27 us -> 0.06 us
    ppermute x3, waiting for transfers between devices: 2.32 us -> 5.02 us  [pass_on(): lax.ppermute(grown[1], axes, second)]
    squeeze x0 -> x1, local copies, waits for them, and re-layouts: none -> 1.4 us  [raw(): env_right[0, :, :count]]
    pallas_call x3, Pallas kernels: 3.65 us -> 4.35 us  [first_apply(): call(functools.partial(first_kernel, chunk, is_first, is_last, groups), o...]
  transfers between devices with their start and end apart: 12 -> 12, of which waited for: 8 -> 9; matrix products, arithmetic and copies ran while one was open for 0% -> 0% of each run, Pallas kernels for 16% -> 17%
where the time goes in v8:
time: 67.5 us; the launch traced here: 67.2 us
  waiting for transfers between devices  25.9 us (38%)
  starting transfers between devices  23.6 us (35%)
  Pallas kernels  15.1 us (22%)
  local copies, waits for them, and re-layouts  1.46 us (2%)
  between operations  0.94 us (1%)
    ppermute x3, starting transfers between devices, pass_on(): lax.ppermute(grown[0], axes, first)  13.9 us
    ppermute x3, waiting for transfers between devices, pass_on(): lax.ppermute(grown[0], axes, first)  12.7 us
    ppermute x4, waiting for transfers between devices, exchange(): lax.ppermute(send, 'sector', [(i, i ^ 1 << stage) for i in range(sectors)])  8.24 us
    pallas_call x1, Pallas kernels, grow(): call(functools.partial(grow_kernel, bounds), [jax.ShapeDtypeStruct((8, 12...  6.4 us
    ppermute x3, waiting for transfers between devices, pass_on(): lax.ppermute(grown[1], axes, second)  5.02 us
    pallas_call x3, Pallas kernels, first_apply(): call(functools.partial(first_kernel, chunk, is_first, is_last, groups), o...  4.35 us
    ppermute x3, starting transfers between devices, pass_on(): lax.ppermute(grown[1], axes, second)  4.01 us
    ppermute x4, starting transfers between devices, exchange(): lax.ppermute(send, 'sector', [(i, i ^ 1 << stage) for i in range(sectors)])  3.87 us
  transfers between devices with their start and end apart: 12, of which 9 were waited for; matrix products, arithmetic and copies ran while one was open for 0% of the time, Pallas kernels for 17%

profile of v8, /device:TPU:0, one launch (start us, length us, event | category | flops | bytes accessed | tf_op | source)
XLA Modules:
  0.0 67.2 jit_solution(15135279904574766946)
XLA Ops:
  0.7 1.4 %slice_bitcast_fusion = (bf16[2,9,128,128]{3,2,1,0:T(8,128)(2,1)S(1)}, bf16[2,9,128,128]{3,2,1,0:T(8,128)(2,1)S(1)}) fusion(bf16[1,2,30,128,128]{4,3,2,1,0:T(8,128)(2,1)} %right_hbm.3, bf16[1,2,30,128,128]{4,3,2,1,0:T(8,128)(2,1)} %left_hbm.3), kind=kLoop, calls=%fused_computation.4 | loop fusion | bytes 2359296 | tf_op jit(solution)/shard_map/squeeze | solution.py:152
  2.1 0.1 broadcast_select_fusion
  2.2 5.0 %collective-permute-start = (bf16[2,10,128,128]{3,2,1,0:T(8,128)(2,1)S(1)}, bf16[2,10,128,128]{3,2,1,0:T(8,128)(2,1)S(1)}, u32[]{:S(2)}, u32[]{:S(2)}) collective-permute-start(bf16[2,10,128,128]{3,2,1,0:T(8,128)(2,1)S(1)} %get-tuple-element.75.rest_0_), channel_id=1, source_target_pairs={{0,4},{5,1},{2,6},{7,3},{4,8},{9,5},{6,10},{11,7},{8,12},{13,9},{1... | collective-permute-start | bytes 1966088 | tf_op jit(solution)/shard_map/ppermute | solution.py:565
  7.3 1.4 %collective-permute-start.1 = (bf16[2,10,128,128]{3,2,1,0:T(8,128)(2,1)S(1)}, bf16[2,10,128,128]{3,2,1,0:T(8,128)(2,1)S(1)}, u32[]{:S(2)}, u32[]{:S(2)}) collective-permute-start(bf16[2,10,128,128]{3,2,1,0:T(8,128)(2,1)S(1)} %get-tuple-element.74), channel_id=1, source_target_pairs={{4,0},{1,5},{6,2},{3,7},{8,4},{5,9},{10,6},{7,11},{12,8},{9,13},{1... | collective-permute-start | bytes 1966088 | tf_op jit(solution)/shard_map/ppermute | solution.py:565
  8.7 6.4 %shard_map.104 = (f32[8,128]{1,0:T(8,128)}, bf16[2,18,128,128]{3,2,1,0:T(8,128)(2,1)}, bf16[2,18,128,128]{3,2,1,0:T(8,128)(2,1)}, bf16[2,3,128,128]{3,2,1,0:T(8,128)(2,1)}, bf16[2,3,128,128]{3,2,1,0:T(8,128)(2,1)}) custom-call(bf16[1,2,30,128,128]{4,3,2,1,0:T(8,128)(2,1)} %left_hbm.3, bf16[1,2,30,128,128]{4,3,2,1,0:T(8,128)(2,1)} %right_hbm.3, ...), custom_call_target="tpu_custom_call" | custom-call | flops 704643072 | bytes 5505024 | tf_op jit(solution)/shard_map/pallas_call | solution.py:134
  15.1 4.7 %collective-permute-start.2 = (bf16[2,18,128,128]{3,2,1,0:T(8,128)(2,1)}, bf16[2,18,128,128]{3,2,1,0:T(8,128)(2,1)S(1)}, u32[]{:S(2)}, u32[]{:S(2)}) collective-permute-start(bf16[2,18,128,128]{3,2,1,0:T(8,128)(2,1)} %get-tuple-element.46), channel_id=1, source_target_pairs={{0,4},{5,1},{2,6},{7,3},{4,8},{9,5},{6,10},{11,7},{8,12},{13,9},{1... | collective-permute-start | bytes 3538952 | tf_op jit(solution)/shard_map/ppermute | solution.py:565
  19.9 1.3 %collective-permute-start.3 = (bf16[2,18,128,128]{3,2,1,0:T(8,128)(2,1)}, bf16[2,18,128,128]{3,2,1,0:T(8,128)(2,1)S(1)}, u32[]{:S(2)}, u32[]{:S(2)}) collective-permute-start(bf16[2,18,128,128]{3,2,1,0:T(8,128)(2,1)} %get-tuple-element.47), channel_id=1, source_target_pairs={{4,0},{1,5},{6,2},{3,7},{8,4},{5,9},{10,6},{7,11},{12,8},{9,13},{1... | collective-permute-start | bytes 3538952 | tf_op jit(solution)/shard_map/ppermute | solution.py:565
  21.2 0.1 collective-permute-done.refs_2_.got_x
  21.3 2.2 %collective-permute-done.1.refs_3_.got_y = bf16[2,10,128,128]{3,2,1,0:T(8,128)(2,1)S(1)} collective-permute-done((bf16[2,10,128,128]{3,2,1,0:T(8,128)(2,1)S(1)}, bf16[2,10,128,128]{3,2,1,0:T(8,128)(2,1)S(1)}, u32[]{:S(2)}, u32[]{:S(2)}) %collective-permute-start.1) | collective-permute-done | bytes 655392 | tf_op jit(solution)/shard_map/ppermute | solution.py:565
  23.5 1.0 %shard_map.106 = (bf16[2,128,128]{2,1,0:T(8,128)(2,1)S(1)}, f32[2,128,128]{2,1,0:T(8,128)S(1)}, f32[2,30,8,128]{3,2,1,0:T(8,128)S(1)}, f32[2,8,128]{2,1,0:T(8,128)S(1)}) custom-call(bf16[1,2,128,128]{3,2,1,0:T(8,128)(2,1)S(1)} %copy-done.2, f32[1,2,30]{2,1,0:T(2,128)S(1)} %copy-done.4, f32[1,2]{1,0:T(1,128)S(1)} %copy-done.5, s32[2]{0:T(128)S(1)} %copy-done.6, ...), custom_call_target="tpu_custom_call" | custom-call | bytes 131072 | tf_op jit(solution)/shard_map/pallas_call | solution.py:240
  24.6 0.1 collective-permute-start.6
  24.6 4.2 %collective-permute-start.4 = (bf16[2,3,128,128]{3,2,1,0:T(8,128)(2,1)}, bf16[2,3,128,128]{3,2,1,0:T(8,128)(2,1)S(1)}, u32[]{:S(2)}, u32[]{:S(2)}) collective-permute-start(bf16[2,3,128,128]{3,2,1,0:T(8,128)(2,1)} %get-tuple-element.50), channel_id=1, source_target_pairs={{0,4},{5,1},{2,6},{7,3},{4,8},{9,5},{6,10},{11,7},{8,12},{13,9},{1... | collective-permute-start | bytes 589832 | tf_op jit(solution)/shard_map/ppermute | solution.py:565
  28.8 1.3 %collective-permute-start.5 = (bf16[2,3,128,128]{3,2,1,0:T(8,128)(2,1)}, bf16[2,3,128,128]{3,2,1,0:T(8,128)(2,1)S(1)}, u32[]{:S(2)}, u32[]{:S(2)}) collective-permute-start(bf16[2,3,128,128]{3,2,1,0:T(8,128)(2,1)} %get-tuple-element.51), channel_id=1, source_target_pairs={{4,0},{1,5},{6,2},{3,7},{8,4},{5,9},{10,6},{7,11},{12,8},{9,13},{1... | collective-permute-start | bytes 589832 | tf_op jit(solution)/shard_map/ppermute | solution.py:565
  30.2 1.8 %collective-permute-start.7 = (bf16[2,2,128,128]{3,2,1,0:T(8,128)(2,1)S(1)}, bf16[2,2,128,128]{3,2,1,0:T(8,128)(2,1)S(1)}, u32[]{:S(2)}, u32[]{:S(2)}) collective-permute-start(bf16[2,2,128,128]{3,2,1,0:T(8,128)(2,1)S(1)} %pad_maximum_fusion.2), channel_id=1, source_target_pairs={{0,2},{1,3},{2,0},{3,1},{4,6},{5,7},{6,4},{7,5},{8,10},{9,11},{10,... | collective-permute-start | bytes 393224 | tf_op jit(solution)/shard_map/ppermute | solution.py:540
  32.0 0.6 shard_map.107
  32.5 1.6 %shard_map.108 = (bf16[2,9,128,128]{3,2,1,0:T(8,128)(2,1)S(1)}, bf16[2,9,128,128]{3,2,1,0:T(8,128)(2,1)S(1)}, f32[8,128,128]{2,1,0:T(8,128)S(1)}) custom-call(bf16[2,30,128,128]{3,2,1,0:T(8,128)(2,1)S(1)} %get-tuple-element.42.own_l, bf16[2,30,128,128]{3,2,1,0:T(8,128)(2,1)S(1)} %get-tuple-element.43.own_r, ...), custom_call_target="tpu_custom_call" | custom-call | flops 150994944 | bytes 1179648 | tf_op jit(solution)/shard_map/pallas_call | solution.py:399
  34.1 12.6 %collective-permute-done.2.got_x = bf16[2,18,128,128]{3,2,1,0:T(8,128)(2,1)S(1)} collective-permute-done((bf16[2,18,128,128]{3,2,1,0:T(8,128)(2,1)}, bf16[2,18,128,128]{3,2,1,0:T(8,128)(2,1)S(1)}, u32[]{:S(2)}, u32[]{:S(2)}) %collective-permute-start.2) | collective-permute-done | bytes 1179680 | tf_op jit(solution)/shard_map/ppermute | solution.py:565
  46.7 2.6 %collective-permute-done.3.got_y = bf16[2,18,128,128]{3,2,1,0:T(8,128)(2,1)S(1)} collective-permute-done((bf16[2,18,128,128]{3,2,1,0:T(8,128)(2,1)}, bf16[2,18,128,128]{3,2,1,0:T(8,128)(2,1)S(1)}, u32[]{:S(2)}, u32[]{:S(2)}) %collective-permute-start.3) | collective-permute-done | bytes 1179680 | tf_op jit(solution)/shard_map/ppermute | solution.py:565
  49.3 1.9 %shard_map.109 = (bf16[2,18,128,128]{3,2,1,0:T(8,128)(2,1)S(1)}, bf16[2,18,128,128]{3,2,1,0:T(8,128)(2,1)S(1)}, f32[8,128,128]{2,1,0:T(8,128)S(1)}) custom-call(bf16[2,30,128,128]{3,2,1,0:T(8,128)(2,1)S(1)} %get-tuple-element.42.own_l, bf16[2,30,128,128]{3,2,1,0:T(8,128)(2,1)S(1)} %get-tuple-element.43.own_r, ...), custom_call_target="tpu_custom_call" | custom-call | flops 301989888 | bytes 2359296 | tf_op jit(solution)/shard_map/pallas_call | solution.py:399
  51.2 0.2 collective-permute-done.5.got_y
  51.4 0.9 %shard_map.110 = (bf16[2,3,128,128]{3,2,1,0:T(8,128)(2,1)S(1)}, bf16[2,3,128,128]{3,2,1,0:T(8,128)(2,1)S(1)}, bf16[544,128]{1,0:T(8,128)(2,1)S(1)}, f32[4,128,12...) custom-call(bf16[2,30,128,128]{3,2,1,0:T(8,128)(2,1)S(1)} %get-tuple-element.42.own_l, ...), custom_call_target="tpu_custom_call" | custom-call | flops 50331648 | bytes 393216 | tf_op jit(solution)/shard_map/pallas_call | solution.py:399
  52.3 0.7 %collective-permute-start.8 = (bf16[544,128]{1,0:T(8,128)(2,1)S(1)}, bf16[544,128]{1,0:T(8,128)(2,1)S(1)}, u32[]{:S(2)}, u32[]{:S(2)}) collective-permute-start(bf16[544,128]{1,0:T(8,128)(2,1)S(1)} %get-tuple-element.60), channel_id=1, source_target_pairs={{0,1},{1,0},{2,3},{3,2},{4,5},{5,4},{6,7},{7,6},{8,9},{9,8},{10,11... | collective-permute-start | bytes 417800 | tf_op jit(solution)/shard_map/ppermute | solution.py:444
  53.0 1.0 %collective-permute-done.8.got = bf16[544,128]{1,0:T(8,128)(2,1)S(1)} collective-permute-done((bf16[544,128]{1,0:T(8,128)(2,1)S(1)}, bf16[544,128]{1,0:T(8,128)(2,1)S(1)}, u32[]{:S(2)}, u32[]{:S(2)}) %collective-permute-start.8) | collective-permute-done | bytes 139296 | tf_op jit(solution)/shard_map/ppermute | solution.py:444
  54.0 1.6 %collective-permute-start.9 = (bf16[288,128]{1,0:T(8,128)(2,1)S(1)}, bf16[288,128]{1,0:T(8,128)(2,1)S(1)}, u32[]{:S(2)}, u32[]{:S(2)}) collective-permute-start(bf16[288,128]{1,0:T(8,128)(2,1)S(1)} %get-tuple-element.63), channel_id=1, source_target_pairs={{0,2},{1,3},{2,0},{3,1},{4,6},{5,7},{6,4},{7,5},{8,10},{9,11},{10,... | collective-permute-start | bytes 221192 | tf_op jit(solution)/shard_map/ppermute | solution.py:444
  55.6 3.0 %collective-permute-done.9.rest_12_ = bf16[288,128]{1,0:T(8,128)(2,1)S(1)} collective-permute-done((bf16[288,128]{1,0:T(8,128)(2,1)S(1)}, bf16[288,128]{1,0:T(8,128)(2,1)S(1)}, u32[]{:S(2)}, u32[]{:S(2)}) %collective-permute-start.9) | collective-permute-done | bytes 73760 | tf_op jit(solution)/shard_map/ppermute | solution.py:444
  58.6 1.9 %shard_map.112 = (bf16[1,2,128,128]{3,2,1,0:T(8,128)(2,1)}, bf16[2,128,128]{2,1,0:T(8,128)(2,1)S(1)}, bf16[544,128]{1,0:T(8,128)(2,1)S(1)}, f32[4,128,128]{2,1,0:T(8,128)S(1)}, f32[8,128]{1,0:T(8,128)S(1)}) custom-call(bf16[2,9,128,128]{3,2,1,0:T(8,128)(2,1)S(1)} %get-tuple-element.45.rest_0_, bf16[2,18,128,128]{3,2,1,0:T(8,128)(2,1)S(1)} %get-tuple-element.49.rest_1_, ...), custom_call_target="tpu_custom_call" | custom-call | flops 503316480 | bytes 3932160 | tf_op jit(solution)/shard_map/pallas_call | solution.py:494
  60.5 0.1 collective-permute-start.10
  60.6 1.3 %collective-permute-done.10.got = bf16[544,128]{1,0:T(8,128)(2,1)S(1)} collective-permute-done((bf16[544,128]{1,0:T(8,128)(2,1)S(1)}, bf16[544,128]{1,0:T(8,128)(2,1)S(1)}, u32[]{:S(2)}, u32[]{:S(2)}) %collective-permute-start.10) | collective-permute-done | bytes 139296 | tf_op jit(solution)/shard_map/ppermute | solution.py:444
  62.0 0.1 shard_map.113
  62.0 1.5 %collective-permute-start.11 = (bf16[288,128]{1,0:T(8,128)(2,1)S(1)}, bf16[288,128]{1,0:T(8,128)(2,1)S(1)}, u32[]{:S(2)}, u32[]{:S(2)}) collective-permute-start(bf16[288,128]{1,0:T(8,128)(2,1)S(1)} %get-tuple-element.72), channel_id=1, source_target_pairs={{0,2},{1,3},{2,0},{3,1},{4,6},{5,7},{6,4},{7,5},{8,10},{9,11},{10,... | collective-permute-start | bytes 221192 | tf_op jit(solution)/shard_map/ppermute | solution.py:444
  63.6 2.9 %collective-permute-done.11.got = bf16[288,128]{1,0:T(8,128)(2,1)S(1)} collective-permute-done((bf16[288,128]{1,0:T(8,128)(2,1)S(1)}, bf16[288,128]{1,0:T(8,128)(2,1)S(1)}, u32[]{:S(2)}, u32[]{:S(2)}) %collective-permute-start.11) | collective-permute-done | bytes 73760 | tf_op jit(solution)/shard_map/ppermute | solution.py:444
  66.4 0.8 %shard_map.114 = bf16[1,2,128,128]{3,2,1,0:T(8,128)(2,1)} custom-call(bf16[2,128,128]{2,1,0:T(8,128)(2,1)S(1)} %get-tuple-element.67.resid, f32[2,8,128]{2,1,0:T(8,128)S(1)} %get-tuple-element.53.rest_1_.rest_9_.energy, f32[2,128,128]{2,1,0:T(8,128)S(1)} %get-tuple-element.58.rest_10_.live, f32[2,128,128]{2,1,0:T(8,128)S(1)} %get-tuple-element.71.keep, ...), custom_call_target="tpu_custom_call" | custom-call | bytes 262144 | tf_op jit(solution)/shard_map/pallas_call | solution.py:526
  (26 shorter events, 0.1 us)
Async XLA Ops:
  0.6 1.4 %copy-start.8 = (bf16[1,2,128,128]{3,2,1,0:T(8,128)(2,1)S(1)}, bf16[1,2,128,128]{3,2,1,0:T(8,128)(2,1)}, u32[]{:S(2)}) copy-start(bf16[1,2,128,128]{3,2,1,0:T(8,128)(2,1)} %edge_l_hbm.1) | copy-start | bytes 196612
  0.6 1.4 %copy-start.9 = (bf16[1,2,128,128]{3,2,1,0:T(8,128)(2,1)S(1)}, bf16[1,2,128,128]{3,2,1,0:T(8,128)(2,1)}, u32[]{:S(2)}) copy-start(bf16[1,2,128,128]{3,2,1,0:T(8,128)(2,1)} %edge_r_hbm.1) | copy-start | bytes 196612
  2.2 6.5 %copy-start.7 = (bf16[2,10,128,128]{3,2,1,0:T(8,128)(2,1)}, bf16[2,10,128,128]{3,2,1,0:T(8,128)(2,1)S(1)}, u32[]{:S(2)}) copy-start(bf16[2,10,128,128]{3,2,1,0:T(8,128)(2,1)S(1)} %get-tuple-element.75.rest_0_) | copy-start | bytes 1966084
  2.2 19.1 %collective-permute-start = (bf16[2,10,128,128]{3,2,1,0:T(8,128)(2,1)S(1)}, bf16[2,10,128,128]{3,2,1,0:T(8,128)(2,1)S(1)}, u32[]{:S(2)}, u32[]{:S(2)}) collective-permute-start(bf16[2,10,128,128]{3,2,1,0:T(8,128)(2,1)S(1)} %get-tuple-element.75.rest_0_), channel_id=1, source_target_pairs={{0,4},{5,1},{2,6},{7,3},{4,8},{9,5},{6,10},{11,7},{8,12},{13,9},{1... | collective-permute-start | bytes 1966088 | tf_op jit(solution)/shard_map/ppermute | solution.py:565
  7.2 16.3 %copy-start.2 = (bf16[1,2,128,128]{3,2,1,0:T(8,128)(2,1)S(1)}, bf16[1,2,128,128]{3,2,1,0:T(8,128)(2,1)}, u32[]{:S(2)}) copy-start(bf16[1,2,128,128]{3,2,1,0:T(8,128)(2,1)} %wave.1) | copy-start | bytes 196612
  7.2 16.3 %copy-start.4 = (f32[1,2,30]{2,1,0:T(2,128)S(1)}, f32[1,2,30]{2,1,0:T(2,128)}, u32[]{:S(2)}) copy-start(f32[1,2,30]{2,1,0:T(2,128)} %coef.1) | copy-start | bytes 724
  7.2 16.3 %copy-start.5 = (f32[1,2]{1,0:T(1,128)S(1)}, f32[1,2]{1,0:T(1,128)}, u32[]{:S(2)}) copy-start(f32[1,2]{1,0:T(1,128)} %onsite.1) | copy-start | bytes 28
  7.2 16.3 %copy-start.6 = (s32[2]{0:T(128)S(1)}, s32[2]{0:T(128)}, u32[]{:S(2)}) copy-start(s32[2]{0:T(128)} %sizes.1) | copy-start | bytes 28
  7.3 16.3 %collective-permute-start.1 = (bf16[2,10,128,128]{3,2,1,0:T(8,128)(2,1)S(1)}, bf16[2,10,128,128]{3,2,1,0:T(8,128)(2,1)S(1)}, u32[]{:S(2)}, u32[]{:S(2)}) collective-permute-start(bf16[2,10,128,128]{3,2,1,0:T(8,128)(2,1)S(1)} %get-tuple-element.74), channel_id=1, source_target_pairs={{4,0},{1,5},{6,2},{3,7},{8,4},{5,9},{10,6},{7,11},{12,8},{9,13},{1... | collective-permute-start | bytes 1966088 | tf_op jit(solution)/shard_map/ppermute | solution.py:565
  8.7 23.3 %copy-start.1 = (bf16[1,2,30,128,128]{4,3,2,1,0:T(8,128)(2,1)S(1)}, bf16[1,2,30,128,128]{4,3,2,1,0:T(8,128)(2,1)}, u32[]{:S(2)}) copy-start(bf16[1,2,30,128,128]{4,3,2,1,0:T(8,128)(2,1)} %right_hbm.3) | copy-start | bytes 5898244
  15.1 16.8 %copy-start = (bf16[1,2,30,128,128]{4,3,2,1,0:T(8,128)(2,1)S(1)}, bf16[1,2,30,128,128]{4,3,2,1,0:T(8,128)(2,1)}, u32[]{:S(2)}) copy-start(bf16[1,2,30,128,128]{4,3,2,1,0:T(8,128)(2,1)} %left_hbm.3) | copy-start | bytes 5898244
  15.1 31.6 %collective-permute-start.2 = (bf16[2,18,128,128]{3,2,1,0:T(8,128)(2,1)}, bf16[2,18,128,128]{3,2,1,0:T(8,128)(2,1)S(1)}, u32[]{:S(2)}, u32[]{:S(2)}) collective-permute-start(bf16[2,18,128,128]{3,2,1,0:T(8,128)(2,1)} %get-tuple-element.46), channel_id=1, source_target_pairs={{0,4},{5,1},{2,6},{7,3},{4,8},{9,5},{6,10},{11,7},{8,12},{13,9},{1... | collective-permute-start | bytes 3538952 | tf_op jit(solution)/shard_map/ppermute | solution.py:565
  19.9 29.4 %collective-permute-start.3 = (bf16[2,18,128,128]{3,2,1,0:T(8,128)(2,1)}, bf16[2,18,128,128]{3,2,1,0:T(8,128)(2,1)S(1)}, u32[]{:S(2)}, u32[]{:S(2)}) collective-permute-start(bf16[2,18,128,128]{3,2,1,0:T(8,128)(2,1)} %get-tuple-element.47), channel_id=1, source_target_pairs={{4,0},{1,5},{6,2},{3,7},{8,4},{5,9},{10,6},{7,11},{12,8},{9,13},{1... | collective-permute-start | bytes 3538952 | tf_op jit(solution)/shard_map/ppermute | solution.py:565
  24.6 5.6 %collective-permute-start.6 = (bf16[1,2,128,128]{3,2,1,0:T(8,128)(2,1)S(1)}, bf16[1,2,128,128]{3,2,1,0:T(8,128)(2,1)S(1)}, u32[]{:S(2)}, u32[]{:S(2)}) collective-permute-start(bf16[1,2,128,128]{3,2,1,0:T(8,128)(2,1)S(1)} %bitcast.7), channel_id=1, source_target_pairs={{0,1},{1,0},{2,3},{3,2},{4,5},{5,4},{6,7},{7,6},{8,9},{9,8},{10,11... | collective-permute-start | bytes 196616 | tf_op jit(solution)/shard_map/ppermute | solution.py:540
  24.6 26.5 %collective-permute-start.4 = (bf16[2,3,128,128]{3,2,1,0:T(8,128)(2,1)}, bf16[2,3,128,128]{3,2,1,0:T(8,128)(2,1)S(1)}, u32[]{:S(2)}, u32[]{:S(2)}) collective-permute-start(bf16[2,3,128,128]{3,2,1,0:T(8,128)(2,1)} %get-tuple-element.50), channel_id=1, source_target_pairs={{0,4},{5,1},{2,6},{7,3},{4,8},{9,5},{6,10},{11,7},{8,12},{13,9},{1... | collective-permute-start | bytes 589832 | tf_op jit(solution)/shard_map/ppermute | solution.py:565
  28.8 22.5 %collective-permute-start.5 = (bf16[2,3,128,128]{3,2,1,0:T(8,128)(2,1)}, bf16[2,3,128,128]{3,2,1,0:T(8,128)(2,1)S(1)}, u32[]{:S(2)}, u32[]{:S(2)}) collective-permute-start(bf16[2,3,128,128]{3,2,1,0:T(8,128)(2,1)} %get-tuple-element.51), channel_id=1, source_target_pairs={{4,0},{1,5},{6,2},{3,7},{8,4},{5,9},{10,6},{7,11},{12,8},{9,13},{1... | collective-permute-start | bytes 589832 | tf_op jit(solution)/shard_map/ppermute | solution.py:565
  30.2 2.3 %copy-start.3 = (s32[1,2,30]{2,1,0:T(2,128)S(1)}, s32[1,2,30]{2,1,0:T(2,128)}, u32[]{:S(2)}) copy-start(s32[1,2,30]{2,1,0:T(2,128)} %rest_8_.1) | copy-start | bytes 724
  30.2 21.0 %collective-permute-start.7 = (bf16[2,2,128,128]{3,2,1,0:T(8,128)(2,1)S(1)}, bf16[2,2,128,128]{3,2,1,0:T(8,128)(2,1)S(1)}, u32[]{:S(2)}, u32[]{:S(2)}) collective-permute-start(bf16[2,2,128,128]{3,2,1,0:T(8,128)(2,1)S(1)} %pad_maximum_fusion.2), channel_id=1, source_target_pairs={{0,2},{1,3},{2,0},{3,1},{4,6},{5,7},{6,4},{7,5},{8,10},{9,11},{10,... | collective-permute-start | bytes 393224 | tf_op jit(solution)/shard_map/ppermute | solution.py:540
  52.3 1.7 %collective-permute-start.8 = (bf16[544,128]{1,0:T(8,128)(2,1)S(1)}, bf16[544,128]{1,0:T(8,128)(2,1)S(1)}, u32[]{:S(2)}, u32[]{:S(2)}) collective-permute-start(bf16[544,128]{1,0:T(8,128)(2,1)S(1)} %get-tuple-element.60), channel_id=1, source_target_pairs={{0,1},{1,0},{2,3},{3,2},{4,5},{5,4},{6,7},{7,6},{8,9},{9,8},{10,11... | collective-permute-start | bytes 417800 | tf_op jit(solution)/shard_map/ppermute | solution.py:444
  54.0 4.6 %collective-permute-start.9 = (bf16[288,128]{1,0:T(8,128)(2,1)S(1)}, bf16[288,128]{1,0:T(8,128)(2,1)S(1)}, u32[]{:S(2)}, u32[]{:S(2)}) collective-permute-start(bf16[288,128]{1,0:T(8,128)(2,1)S(1)} %get-tuple-element.63), channel_id=1, source_target_pairs={{0,2},{1,3},{2,0},{3,1},{4,6},{5,7},{6,4},{7,5},{8,10},{9,11},{10,... | collective-permute-start | bytes 221192 | tf_op jit(solution)/shard_map/ppermute | solution.py:444
  60.5 1.4 %collective-permute-start.10 = (bf16[544,128]{1,0:T(8,128)(2,1)S(1)}, bf16[544,128]{1,0:T(8,128)(2,1)S(1)}, u32[]{:S(2)}, u32[]{:S(2)}) collective-permute-start(bf16[544,128]{1,0:T(8,128)(2,1)S(1)} %get-tuple-element.69), channel_id=1, source_target_pairs={{0,1},{1,0},{2,3},{3,2},{4,5},{5,4},{6,7},{7,6},{8,9},{9,8},{10,11... | collective-permute-start | bytes 417800 | tf_op jit(solution)/shard_map/ppermute | solution.py:444
  62.0 4.4 %collective-permute-start.11 = (bf16[288,128]{1,0:T(8,128)(2,1)S(1)}, bf16[288,128]{1,0:T(8,128)(2,1)S(1)}, u32[]{:S(2)}, u32[]{:S(2)}) collective-permute-start(bf16[288,128]{1,0:T(8,128)(2,1)S(1)} %get-tuple-element.72), channel_id=1, source_target_pairs={{0,2},{1,3},{2,0},{3,1},{4,6},{5,7},{6,4},{7,5},{8,10},{9,11},{10,... | collective-permute-start | bytes 221192 | tf_op jit(solution)/shard_map/ppermute | solution.py:444

commit v9 on v7

--- a/solution.py
+++ b/solution.py
@@ -42,7 +42,7 @@
 
 
 def chunk_sizes(channels):
-    first, last = max(1, channels * 3 // 10), max(1, channels // 10)
+    first, last = max(1, channels * 11 // 30), max(1, channels * 3 // 30)
     return [c for c in (first, channels - first - last, last) if c > 0]
 
 
@@ -147,6 +147,78 @@
     return res[0], [(res[2 * i + 1], res[2 * i + 2]) for i in range(n)]
 
 
+def raw(env_left, env_right, edge_left, edge_right, count):
+    left = jnp.concatenate([env_left[0, :, :count], edge_left[0][:, None]], axis=1)
+    right = jnp.concatenate([env_right[0, :, :count], edge_right[0][:, None]], axis=1)
+    return jnp.where(up_first(), left, right)
+
+
+def other_kernel(count, left_hbm, right_hbm, edge_l_hbm, edge_r_hbm, after, token, out, buf, edge, res, sems, out_sems):
+    pd = buf.shape[0]
+
+    def copies(env, src):
+        made = [pltpu.make_async_copy(src.at[0], edge, sems.at[0])]
+        for k in range(pd):
+            made.append(pltpu.make_async_copy(env.at[0, k, pl.ds(0, count)], buf.at[k], sems.at[k + 1]))
+        return made
+
+    @pl.when(up_first())
+    def _():
+        for c in copies(right_hbm, edge_r_hbm):
+            c.start()
+
+    @pl.when(jnp.logical_not(up_first()))
+    def _():
+        for c in copies(left_hbm, edge_l_hbm):
+            c.start()
+
+    token[...] = jnp.zeros_like(token)
+    for c in copies(left_hbm, edge_l_hbm):
+        c.wait()
+    sends = [pltpu.make_async_copy(res.at[k], out.at[k], out_sems.at[k]) for k in range(pd)]
+
+    @pl.when(up_first())
+    def _():
+        for k in range(pd):
+            res[k] = grown_right(edge[k], buf[k])
+            sends[k].start()
+
+    @pl.when(jnp.logical_not(up_first()))
+    def _():
+        for k in range(pd):
+            res[k] = grown_left(edge[k], buf[k])
+            sends[k].start()
+
+    for c in sends:
+        c.wait()
+
+
+def grown_left(e, x):
+    e_t = e.T
+    inner = jnp.concatenate([dot(e_t, x[u]).astype(bf16) for u in range(x.shape[0])], axis=0)
+    return dot(inner, e).astype(bf16).reshape(x.shape)
+
+
+def grown_right(f, x):
+    inner = [dot(f, x[u]).astype(bf16) for u in range(x.shape[0])]
+    return jnp.stack([dot_t(f, i).astype(bf16) for i in inner])
+
+
+def other(env_left, env_right, edge_left, edge_right, count, after):
+    _, pd, _, b, _ = env_left.shape
+    buf = pltpu.VMEM((pd, count, b, b), bf16)
+    return call(
+        functools.partial(other_kernel, count),
+        [jax.ShapeDtypeStruct((8, 128), f32), jax.ShapeDtypeStruct((pd, count, b, b), bf16)],
+        [HB] * 5,
+        [buf, pltpu.VMEM((pd, b, b), bf16), buf, pltpu.SemaphoreType.DMA((pd + 1,)), pltpu.SemaphoreType.DMA((pd,))],
+        flops=4 * pd * count * b**3,
+        moved=4 * pd * count * b * b,
+        out_specs=[VM, HB],
+        vmem=VMEM_LARGE,
+    )(env_left, env_right, edge_left, edge_right, after)
+
+
 def gate_kernel(*refs):
     refs[-1][...] = jnp.zeros_like(refs[-1])
 
@@ -201,7 +273,7 @@
     shape = jax.ShapeDtypeStruct((pd, channels, b, b), bf16)
     return call(
         own_kernel, [shape, shape], [HB, HB, HB], [pltpu.SemaphoreType.DMA],
-        flops=10**10, moved=10**6,
+        flops=7 * 10**9, moved=10**6,
     )(env_left, env_right, after)
 
 
@@ -327,8 +399,12 @@
     def load(k, at, unit):
         here, there = pl.ds(at, unit), pl.ds(start + at, unit)
         got_first, got_second = got_x[k, here], got_y[k, here]
-        left = jnp.where(up, got_first, got_second) + own_l[k, there]
-        right = jnp.where(up, got_second, got_first) + own_r[k, there]
+        as_left, as_right = got_first, got_first
+        if is_first:
+            edge = got_x[k, count]
+            as_left, as_right = grown_left(edge, got_first), grown_right(edge, got_first)
+        left, right = jnp.where(up, as_left, got_second), jnp.where(up, got_second, as_right)
+        left, right = left + own_l[k, there], right + own_r[k, there]
         new_l[k, here] = left
         new_r[k, here] = right
         return left, right
@@ -549,7 +625,9 @@
         axes = ("section", "sector")
         return lax.ppermute(grown[0], axes, first), lax.ppermute(grown[1], axes, second)
 
-    token, (head,) = grow(env_left, env_right, edge_left, edge_right, bounds[:1], (), VMEM_LARGE)
+    whole = raw(env_left, env_right, edge_left, edge_right, bounds[0][1])
+    token, half = other(env_left, env_right, edge_left, edge_right, bounds[0][1], whole)
+    head = (whole, half)
     got = [pass_on(head)]
     _, (middle, last) = grow(env_left, env_right, edge_left, edge_right, bounds[1:], (token,), VMEM_LARGE)
     got.append(pass_on(middle))

time: 68.5 us -> 67 us (0.978)
  waiting for transfers between devices: 22.8 us -> 19.3 us
  local copies, waits for them, and re-layouts: 3.27 us -> 4.8 us
    pallas_call x2 -> x1, Pallas kernels: 10.2 us -> 6.27 us  [grow(): call(functools.partial(grow_kernel, bounds), [jax.ShapeDtypeStruct((8, 12...]
    pallas_call x0 -> x1, Pallas kernels: none -> 3.35 us  [other(): call(functools.partial(other_kernel, count), [jax.ShapeDtypeStruct((8, 12...]
    ppermute x3, waiting for transfers between devices: 12.2 us -> 8.86 us  [pass_on(): lax.ppermute(grown[0], axes, first)]
    squeeze x0 -> x1, local copies, waits for them, and re-layouts: none -> 1.51 us  [raw(): env_right[0, :, :count]]
    pallas_call x3, Pallas kernels: 3.65 us -> 4.47 us  [first_apply(): call(functools.partial(first_kernel, chunk, is_first, is_last, groups), o...]
    unnamed x22 -> x28, local copies, waits for them, and re-layouts: 3.27 us -> 3.29 us
  transfers between devices with their start and end apart: 12 -> 12, of which waited for: 8 -> 8; matrix products, arithmetic and copies ran while one was open for 0% -> 0% of each run, Pallas kernels for 16% -> 22%
where the time goes in v9:
time: 67 us; the launch traced here: 66.6 us
  starting transfers between devices  22.9 us (34%)
  waiting for transfers between devices  19.3 us (29%)
  Pallas kernels  18.4 us (27%)
  local copies, waits for them, and re-layouts  4.8 us (7%)
  between operations  0.94 us (1%)
    ppermute x3, starting transfers between devices, pass_on(): lax.ppermute(grown[0], axes, first)  14 us
    ppermute x3, waiting for transfers between devices, pass_on(): lax.ppermute(grown[0], axes, first)  8.86 us
    ppermute x4, waiting for transfers between devices, exchange(): lax.ppermute(send, 'sector', [(i, i ^ 1 << stage) for i in range(sectors)])  8.26 us
    pallas_call x1, Pallas kernels, grow(): call(functools.partial(grow_kernel, bounds), [jax.ShapeDtypeStruct((8, 12...  6.27 us
    pallas_call x3, Pallas kernels, first_apply(): call(functools.partial(first_kernel, chunk, is_first, is_last, groups), o...  4.47 us
    ppermute x3, starting transfers between devices, pass_on(): lax.ppermute(grown[1], axes, second)  3.88 us
    ppermute x4, starting transfers between devices, exchange(): lax.ppermute(send, 'sector', [(i, i ^ 1 << stage) for i in range(sectors)])  3.48 us
    pallas_call x1, Pallas kernels, other(): call(functools.partial(other_kernel, count), [jax.ShapeDtypeStruct((8, 12...  3.35 us
  transfers between devices with their start and end apart: 12, of which 8 were waited for; matrix products, arithmetic and copies ran while one was open for 0% of the time, Pallas kernels for 22%

profile of v9, /device:TPU:0, one launch (start us, length us, event | category | flops | bytes accessed | tf_op | source)
XLA Modules:
  0.0 66.6 jit_solution(12377341521829662038)
XLA Ops:
  0.7 1.5 %slice_bitcast_fusion = (bf16[2,11,128,128]{3,2,1,0:T(8,128)(2,1)S(1)}, bf16[2,11,128,128]{3,2,1,0:T(8,128)(2,1)S(1)}) fusion(bf16[1,2,30,128,128]{4,3,2,1,0:T(8,128)(2,1)} %right_hbm.5, bf16[1,2,30,128,128]{4,3,2,1,0:T(8,128)(2,1)} %left_hbm.5), kind=kLoop, calls=%fused_computation.1 | loop fusion | bytes 2883584 | tf_op jit(solution)/shard_map/squeeze | solution.py:152
  2.4 5.0 %collective-permute-start = (bf16[2,12,128,128]{3,2,1,0:T(8,128)(2,1)S(1)}, bf16[2,12,128,128]{3,2,1,0:T(8,128)(2,1)S(1)}, u32[]{:S(2)}, u32[]{:S(2)}) collective-permute-start(bf16[2,12,128,128]{3,2,1,0:T(8,128)(2,1)S(1)} %maximum_select_fusion.after), channel_id=1, source_target_pairs={{0,4},{5,1},{2,6},{7,3},{4,8},{9,5},{6,10},{11,7},{8,12},{13,9},{1... | collective-permute-start | bytes 2359304 | tf_op jit(solution)/shard_map/ppermute | solution.py:626
  7.3 3.3 %shard_map.104 = (f32[8,128]{1,0:T(8,128)}, bf16[2,11,128,128]{3,2,1,0:T(8,128)(2,1)}) custom-call(bf16[1,2,30,128,128]{4,3,2,1,0:T(8,128)(2,1)} %left_hbm.5, bf16[1,2,30,128,128]{4,3,2,1,0:T(8,128)(2,1)} %right_hbm.5, bf16[1,2,128,128]{3,2,1,0:T(8,128)(2,1)} %edge_l_hbm.3, bf16[1,2,128,128]{3,2,1,0:T(8,128)(2,1)} %edge_r_hbm.3, ...), custom_call_target="tpu_custom_call" | custom-call | flops 184549376 | bytes 1441792 | tf_op jit(solution)/shard_map/pallas_call | solution.py:210
  10.7 1.3 %collective-permute-start.1 = (bf16[2,11,128,128]{3,2,1,0:T(8,128)(2,1)}, bf16[2,11,128,128]{3,2,1,0:T(8,128)(2,1)S(1)}, u32[]{:S(2)}, u32[]{:S(2)}) collective-permute-start(bf16[2,11,128,128]{3,2,1,0:T(8,128)(2,1)} %get-tuple-element.43), channel_id=1, source_target_pairs={{4,0},{1,5},{6,2},{3,7},{8,4},{5,9},{10,6},{7,11},{12,8},{9,13},{1... | collective-permute-start | bytes 2162696 | tf_op jit(solution)/shard_map/ppermute | solution.py:626
  12.1 6.3 %shard_map.105 = (f32[8,128]{1,0:T(8,128)}, bf16[2,16,128,128]{3,2,1,0:T(8,128)(2,1)}, bf16[2,16,128,128]{3,2,1,0:T(8,128)(2,1)}, bf16[2,3,128,128]{3,2,1,0:T(8,128)(2,1)}, bf16[2,3,128,128]{3,2,1,0:T(8,128)(2,1)}) custom-call(bf16[1,2,30,128,128]{4,3,2,1,0:T(8,128)(2,1)} %left_hbm.5, bf16[1,2,30,128,128]{4,3,2,1,0:T(8,128)(2,1)} %right_hbm.5, ...), custom_call_target="tpu_custom_call" | custom-call | flops 637534208 | bytes 4980736 | tf_op jit(solution)/shard_map/pallas_call | solution.py:134
  18.4 4.7 %collective-permute-start.2 = (bf16[2,16,128,128]{3,2,1,0:T(8,128)(2,1)}, bf16[2,16,128,128]{3,2,1,0:T(8,128)(2,1)S(1)}, u32[]{:S(2)}, u32[]{:S(2)}) collective-permute-start(bf16[2,16,128,128]{3,2,1,0:T(8,128)(2,1)} %get-tuple-element.50), channel_id=1, source_target_pairs={{0,4},{5,1},{2,6},{7,3},{4,8},{9,5},{6,10},{11,7},{8,12},{13,9},{1... | collective-permute-start | bytes 3145736 | tf_op jit(solution)/shard_map/ppermute | solution.py:626
  23.1 1.3 %collective-permute-start.3 = (bf16[2,16,128,128]{3,2,1,0:T(8,128)(2,1)}, bf16[2,16,128,128]{3,2,1,0:T(8,128)(2,1)S(1)}, u32[]{:S(2)}, u32[]{:S(2)}) collective-permute-start(bf16[2,16,128,128]{3,2,1,0:T(8,128)(2,1)} %get-tuple-element.51), channel_id=1, source_target_pairs={{4,0},{1,5},{6,2},{3,7},{8,4},{5,9},{10,6},{7,11},{12,8},{9,13},{1... | collective-permute-start | bytes 3145736 | tf_op jit(solution)/shard_map/ppermute | solution.py:626
  24.4 0.5 collective-permute-done.1.refs_3_.got_y
  24.9 0.9 %copy-done.2 = bf16[2,3,128,128]{3,2,1,0:T(8,128)(2,1)S(1)} copy-done((bf16[2,3,128,128]{3,2,1,0:T(8,128)(2,1)S(1)}, bf16[2,3,128,128]{3,2,1,0:T(8,128)(2,1)}, u32[]{:S(2)}) %copy-start.2) | copy-done | bytes 196632
  25.8 0.9 %copy-done.4 = bf16[2,3,128,128]{3,2,1,0:T(8,128)(2,1)S(1)} copy-done((bf16[2,3,128,128]{3,2,1,0:T(8,128)(2,1)S(1)}, bf16[2,3,128,128]{3,2,1,0:T(8,128)(2,1)}, u32[]{:S(2)}) %copy-start.4) | copy-done | bytes 196632
  26.7 0.7 %copy-done.3 = bf16[2,3,128,128]{3,2,1,0:T(8,128)(2,1)} copy-done((bf16[2,3,128,128]{3,2,1,0:T(8,128)(2,1)}, bf16[2,3,128,128]{3,2,1,0:T(8,128)(2,1)S(1)}, u32[]{:S(2)}) %copy-start.3) | copy-done | bytes 196632
  27.4 0.7 %copy-done.5 = bf16[2,3,128,128]{3,2,1,0:T(8,128)(2,1)} copy-done((bf16[2,3,128,128]{3,2,1,0:T(8,128)(2,1)}, bf16[2,3,128,128]{3,2,1,0:T(8,128)(2,1)S(1)}, u32[]{:S(2)}) %copy-start.5) | copy-done | bytes 196632
  28.1 1.0 %shard_map.107 = (bf16[2,128,128]{2,1,0:T(8,128)(2,1)S(1)}, f32[2,128,128]{2,1,0:T(8,128)S(1)}, f32[2,30,8,128]{3,2,1,0:T(8,128)S(1)}, f32[2,8,128]{2,1,0:T(8,128)S(1)}) custom-call(bf16[1,2,128,128]{3,2,1,0:T(8,128)(2,1)S(1)} %copy-done.6, f32[1,2,30]{2,1,0:T(2,128)S(1)} %copy-done.8, f32[1,2]{1,0:T(1,128)S(1)} %copy-done.9, s32[2]{0:T(128)S(1)} %copy-done.10, ...), custom_call_target="tpu_custom_call" | custom-call | bytes 131072 | tf_op jit(solution)/shard_map/pallas_call | solution.py:305
  29.2 4.3 %collective-permute-start.4 = (bf16[2,3,128,128]{3,2,1,0:T(8,128)(2,1)}, bf16[2,3,128,128]{3,2,1,0:T(8,128)(2,1)S(1)}, u32[]{:S(2)}, u32[]{:S(2)}) collective-permute-start(bf16[2,3,128,128]{3,2,1,0:T(8,128)(2,1)} %copy-done.3), channel_id=1, source_target_pairs={{0,4},{5,1},{2,6},{7,3},{4,8},{9,5},{6,10},{11,7},{8,12},{13,9},{1... | collective-permute-start | bytes 589832 | tf_op jit(solution)/shard_map/ppermute | solution.py:626
  33.5 1.3 %collective-permute-start.5 = (bf16[2,3,128,128]{3,2,1,0:T(8,128)(2,1)}, bf16[2,3,128,128]{3,2,1,0:T(8,128)(2,1)S(1)}, u32[]{:S(2)}, u32[]{:S(2)}) collective-permute-start(bf16[2,3,128,128]{3,2,1,0:T(8,128)(2,1)} %copy-done.5), channel_id=1, source_target_pairs={{4,0},{1,5},{6,2},{3,7},{8,4},{5,9},{10,6},{7,11},{12,8},{9,13},{1... | collective-permute-start | bytes 589832 | tf_op jit(solution)/shard_map/ppermute | solution.py:626
  34.8 1.5 %collective-permute-start.7 = (bf16[2,2,128,128]{3,2,1,0:T(8,128)(2,1)S(1)}, bf16[2,2,128,128]{3,2,1,0:T(8,128)(2,1)S(1)}, u32[]{:S(2)}, u32[]{:S(2)}) collective-permute-start(bf16[2,2,128,128]{3,2,1,0:T(8,128)(2,1)S(1)} %pad_maximum_fusion), channel_id=1, source_target_pairs={{0,2},{1,3},{2,0},{3,1},{4,6},{5,7},{6,4},{7,5},{8,10},{9,11},{10,... | collective-permute-start | bytes 393224 | tf_op jit(solution)/shard_map/ppermute | solution.py:601
  36.4 0.6 shard_map.108
  36.9 1.8 %shard_map.109 = (bf16[2,11,128,128]{3,2,1,0:T(8,128)(2,1)S(1)}, bf16[2,11,128,128]{3,2,1,0:T(8,128)(2,1)S(1)}, f32[8,128,128]{2,1,0:T(8,128)S(1)}) custom-call(bf16[2,30,128,128]{3,2,1,0:T(8,128)(2,1)S(1)} %get-tuple-element.46.own_l, bf16[2,30,128,128]{3,2,1,0:T(8,128)(2,1)S(1)} %get-tuple-element.47.own_r, ...), custom_call_target="tpu_custom_call" | custom-call | flops 184549376 | bytes 1441792 | tf_op jit(solution)/shard_map/pallas_call | solution.py:460
  38.8 8.2 %collective-permute-done.2.got_x = bf16[2,16,128,128]{3,2,1,0:T(8,128)(2,1)S(1)} collective-permute-done((bf16[2,16,128,128]{3,2,1,0:T(8,128)(2,1)}, bf16[2,16,128,128]{3,2,1,0:T(8,128)(2,1)S(1)}, u32[]{:S(2)}, u32[]{:S(2)}) %collective-permute-start.2) | collective-permute-done | bytes 1048608 | tf_op jit(solution)/shard_map/ppermute | solution.py:626
  46.9 1.7 %collective-permute-done.3.got_y = bf16[2,16,128,128]{3,2,1,0:T(8,128)(2,1)S(1)} collective-permute-done((bf16[2,16,128,128]{3,2,1,0:T(8,128)(2,1)}, bf16[2,16,128,128]{3,2,1,0:T(8,128)(2,1)S(1)}, u32[]{:S(2)}, u32[]{:S(2)}) %collective-permute-start.3) | collective-permute-done | bytes 1048608 | tf_op jit(solution)/shard_map/ppermute | solution.py:626
  48.7 1.7 %shard_map.110 = (bf16[2,16,128,128]{3,2,1,0:T(8,128)(2,1)S(1)}, bf16[2,16,128,128]{3,2,1,0:T(8,128)(2,1)S(1)}, f32[8,128,128]{2,1,0:T(8,128)S(1)}) custom-call(bf16[2,30,128,128]{3,2,1,0:T(8,128)(2,1)S(1)} %get-tuple-element.46.own_l, bf16[2,30,128,128]{3,2,1,0:T(8,128)(2,1)S(1)} %get-tuple-element.47.own_r, ...), custom_call_target="tpu_custom_call" | custom-call | flops 268435456 | bytes 2097152 | tf_op jit(solution)/shard_map/pallas_call | solution.py:460
  50.5 0.7 %collective-permute-done.4.got_x = bf16[2,3,128,128]{3,2,1,0:T(8,128)(2,1)S(1)} collective-permute-done((bf16[2,3,128,128]{3,2,1,0:T(8,128)(2,1)}, bf16[2,3,128,128]{3,2,1,0:T(8,128)(2,1)S(1)}, u32[]{:S(2)}, u32[]{:S(2)}) %collective-permute-start.4) | collective-permute-done | bytes 196640 | tf_op jit(solution)/shard_map/ppermute | solution.py:626
  51.2 0.9 %shard_map.111 = (bf16[2,3,128,128]{3,2,1,0:T(8,128)(2,1)S(1)}, bf16[2,3,128,128]{3,2,1,0:T(8,128)(2,1)S(1)}, bf16[544,128]{1,0:T(8,128)(2,1)S(1)}, f32[4,128,12...) custom-call(bf16[2,30,128,128]{3,2,1,0:T(8,128)(2,1)S(1)} %get-tuple-element.46.own_l, ...), custom_call_target="tpu_custom_call" | custom-call | flops 50331648 | bytes 393216 | tf_op jit(solution)/shard_map/pallas_call | solution.py:460
  52.1 0.3 collective-permute-start.8
  52.4 1.1 %collective-permute-done.8.got = bf16[544,128]{1,0:T(8,128)(2,1)S(1)} collective-permute-done((bf16[544,128]{1,0:T(8,128)(2,1)S(1)}, bf16[544,128]{1,0:T(8,128)(2,1)S(1)}, u32[]{:S(2)}, u32[]{:S(2)}) %collective-permute-start.8) | collective-permute-done | bytes 139296 | tf_op jit(solution)/shard_map/ppermute | solution.py:505
  53.5 1.5 %collective-permute-start.9 = (bf16[288,128]{1,0:T(8,128)(2,1)S(1)}, bf16[288,128]{1,0:T(8,128)(2,1)S(1)}, u32[]{:S(2)}, u32[]{:S(2)}) collective-permute-start(bf16[288,128]{1,0:T(8,128)(2,1)S(1)} %get-tuple-element.67), channel_id=1, source_target_pairs={{0,2},{1,3},{2,0},{3,1},{4,6},{5,7},{6,4},{7,5},{8,10},{9,11},{10,... | collective-permute-start | bytes 221192 | tf_op jit(solution)/shard_map/ppermute | solution.py:505
  55.1 2.9 %collective-permute-done.9.rest_12_ = bf16[288,128]{1,0:T(8,128)(2,1)S(1)} collective-permute-done((bf16[288,128]{1,0:T(8,128)(2,1)S(1)}, bf16[288,128]{1,0:T(8,128)(2,1)S(1)}, u32[]{:S(2)}, u32[]{:S(2)}) %collective-permute-start.9) | collective-permute-done | bytes 73760 | tf_op jit(solution)/shard_map/ppermute | solution.py:505
  58.0 1.9 %shard_map.113 = (bf16[1,2,128,128]{3,2,1,0:T(8,128)(2,1)}, bf16[2,128,128]{2,1,0:T(8,128)(2,1)S(1)}, bf16[544,128]{1,0:T(8,128)(2,1)S(1)}, f32[4,128,128]{2,1,0:T(8,128)S(1)}, f32[8,128]{1,0:T(8,128)S(1)}) custom-call(bf16[2,11,128,128]{3,2,1,0:T(8,128)(2,1)S(1)} %get-tuple-element.49.rest_0_, bf16[2,16,128,128]{3,2,1,0:T(8,128)(2,1)S(1)} %get-tuple-element.53.rest_1_, ...), custom_call_target="tpu_custom_call" | custom-call | flops 503316480 | bytes 3932160 | tf_op jit(solution)/shard_map/pallas_call | solution.py:555
  60.0 1.3 %collective-permute-done.10.got = bf16[544,128]{1,0:T(8,128)(2,1)S(1)} collective-permute-done((bf16[544,128]{1,0:T(8,128)(2,1)S(1)}, bf16[544,128]{1,0:T(8,128)(2,1)S(1)}, u32[]{:S(2)}, u32[]{:S(2)}) %collective-permute-start.10) | collective-permute-done | bytes 139296 | tf_op jit(solution)/shard_map/ppermute | solution.py:505
  61.4 1.6 %collective-permute-start.11 = (bf16[288,128]{1,0:T(8,128)(2,1)S(1)}, bf16[288,128]{1,0:T(8,128)(2,1)S(1)}, u32[]{:S(2)}, u32[]{:S(2)}) collective-permute-start(bf16[288,128]{1,0:T(8,128)(2,1)S(1)} %get-tuple-element.76), channel_id=1, source_target_pairs={{0,2},{1,3},{2,0},{3,1},{4,6},{5,7},{6,4},{7,5},{8,10},{9,11},{10,... | collective-permute-start | bytes 221192 | tf_op jit(solution)/shard_map/ppermute | solution.py:505
  63.0 2.9 %collective-permute-done.11.got = bf16[288,128]{1,0:T(8,128)(2,1)S(1)} collective-permute-done((bf16[288,128]{1,0:T(8,128)(2,1)S(1)}, bf16[288,128]{1,0:T(8,128)(2,1)S(1)}, u32[]{:S(2)}, u32[]{:S(2)}) %collective-permute-start.11) | collective-permute-done | bytes 73760 | tf_op jit(solution)/shard_map/ppermute | solution.py:505
  65.8 0.8 %shard_map.115 = bf16[1,2,128,128]{3,2,1,0:T(8,128)(2,1)} custom-call(bf16[2,128,128]{2,1,0:T(8,128)(2,1)S(1)} %get-tuple-element.71.resid, f32[2,8,128]{2,1,0:T(8,128)S(1)} %get-tuple-element.57.rest_1_.rest_9_.energy, f32[2,128,128]{2,1,0:T(8,128)S(1)} %get-tuple-element.62.rest_10_.live, f32[2,128,128]{2,1,0:T(8,128)S(1)} %get-tuple-element.75.keep, ...), custom_call_target="tpu_custom_call" | custom-call | bytes 262144 | tf_op jit(solution)/shard_map/pallas_call | solution.py:587
  (35 shorter events, 0.5 us)
Async XLA Ops:
  0.6 1.6 %copy-start.12 = (bf16[1,2,128,128]{3,2,1,0:T(8,128)(2,1)S(1)}, bf16[1,2,128,128]{3,2,1,0:T(8,128)(2,1)}, u32[]{:S(2)}) copy-start(bf16[1,2,128,128]{3,2,1,0:T(8,128)(2,1)} %edge_l_hbm.3) | copy-start | bytes 196612
  0.6 1.6 %copy-start.13 = (bf16[1,2,128,128]{3,2,1,0:T(8,128)(2,1)S(1)}, bf16[1,2,128,128]{3,2,1,0:T(8,128)(2,1)}, u32[]{:S(2)}) copy-start(bf16[1,2,128,128]{3,2,1,0:T(8,128)(2,1)} %edge_r_hbm.3) | copy-start | bytes 196612
  2.3 5.0 %copy-start.11 = (bf16[2,12,128,128]{3,2,1,0:T(8,128)(2,1)}, bf16[2,12,128,128]{3,2,1,0:T(8,128)(2,1)S(1)}, u32[]{:S(2)}) copy-start(bf16[2,12,128,128]{3,2,1,0:T(8,128)(2,1)S(1)} %maximum_select_fusion.after) | copy-start | bytes 2359300
  2.4 22.5 %collective-permute-start = (bf16[2,12,128,128]{3,2,1,0:T(8,128)(2,1)S(1)}, bf16[2,12,128,128]{3,2,1,0:T(8,128)(2,1)S(1)}, u32[]{:S(2)}, u32[]{:S(2)}) collective-permute-start(bf16[2,12,128,128]{3,2,1,0:T(8,128)(2,1)S(1)} %maximum_select_fusion.after), channel_id=1, source_target_pairs={{0,4},{5,1},{2,6},{7,3},{4,8},{9,5},{6,10},{11,7},{8,12},{13,9},{1... | collective-permute-start | bytes 2359304 | tf_op jit(solution)/shard_map/ppermute | solution.py:626
  10.7 14.2 %collective-permute-start.1 = (bf16[2,11,128,128]{3,2,1,0:T(8,128)(2,1)}, bf16[2,11,128,128]{3,2,1,0:T(8,128)(2,1)S(1)}, u32[]{:S(2)}, u32[]{:S(2)}) collective-permute-start(bf16[2,11,128,128]{3,2,1,0:T(8,128)(2,1)} %get-tuple-element.43), channel_id=1, source_target_pairs={{4,0},{1,5},{6,2},{3,7},{8,4},{5,9},{10,6},{7,11},{12,8},{9,13},{1... | collective-permute-start | bytes 2162696 | tf_op jit(solution)/shard_map/ppermute | solution.py:626
  12.0 16.1 %copy-start.6 = (bf16[1,2,128,128]{3,2,1,0:T(8,128)(2,1)S(1)}, bf16[1,2,128,128]{3,2,1,0:T(8,128)(2,1)}, u32[]{:S(2)}) copy-start(bf16[1,2,128,128]{3,2,1,0:T(8,128)(2,1)} %wave.1) | copy-start | bytes 196612
  12.0 16.1 %copy-start.8 = (f32[1,2,30]{2,1,0:T(2,128)S(1)}, f32[1,2,30]{2,1,0:T(2,128)}, u32[]{:S(2)}) copy-start(f32[1,2,30]{2,1,0:T(2,128)} %coef.1) | copy-start | bytes 724
  12.0 16.1 %copy-start.9 = (f32[1,2]{1,0:T(1,128)S(1)}, f32[1,2]{1,0:T(1,128)}, u32[]{:S(2)}) copy-start(f32[1,2]{1,0:T(1,128)} %onsite.1) | copy-start | bytes 28
  12.0 16.1 %copy-start.10 = (s32[2]{0:T(128)S(1)}, s32[2]{0:T(128)}, u32[]{:S(2)}) copy-start(s32[2]{0:T(128)} %sizes.1) | copy-start | bytes 28
  12.0 24.3 %copy-start.1 = (bf16[1,2,30,128,128]{4,3,2,1,0:T(8,128)(2,1)S(1)}, bf16[1,2,30,128,128]{4,3,2,1,0:T(8,128)(2,1)}, u32[]{:S(2)}) copy-start(bf16[1,2,30,128,128]{4,3,2,1,0:T(8,128)(2,1)} %right_hbm.5) | copy-start | bytes 5898244
  18.3 18.0 %copy-start = (bf16[1,2,30,128,128]{4,3,2,1,0:T(8,128)(2,1)S(1)}, bf16[1,2,30,128,128]{4,3,2,1,0:T(8,128)(2,1)}, u32[]{:S(2)}) copy-start(bf16[1,2,30,128,128]{4,3,2,1,0:T(8,128)(2,1)} %left_hbm.5) | copy-start | bytes 5898244
  18.4 28.6 %collective-permute-start.2 = (bf16[2,16,128,128]{3,2,1,0:T(8,128)(2,1)}, bf16[2,16,128,128]{3,2,1,0:T(8,128)(2,1)S(1)}, u32[]{:S(2)}, u32[]{:S(2)}) collective-permute-start(bf16[2,16,128,128]{3,2,1,0:T(8,128)(2,1)} %get-tuple-element.50), channel_id=1, source_target_pairs={{0,4},{5,1},{2,6},{7,3},{4,8},{9,5},{6,10},{11,7},{8,12},{13,9},{1... | collective-permute-start | bytes 3145736 | tf_op jit(solution)/shard_map/ppermute | solution.py:626
  23.1 25.6 %collective-permute-start.3 = (bf16[2,16,128,128]{3,2,1,0:T(8,128)(2,1)}, bf16[2,16,128,128]{3,2,1,0:T(8,128)(2,1)S(1)}, u32[]{:S(2)}, u32[]{:S(2)}) collective-permute-start(bf16[2,16,128,128]{3,2,1,0:T(8,128)(2,1)} %get-tuple-element.51), channel_id=1, source_target_pairs={{4,0},{1,5},{6,2},{3,7},{8,4},{5,9},{10,6},{7,11},{12,8},{9,13},{1... | collective-permute-start | bytes 3145736 | tf_op jit(solution)/shard_map/ppermute | solution.py:626
  24.9 0.9 %copy-start.2 = (bf16[2,3,128,128]{3,2,1,0:T(8,128)(2,1)S(1)}, bf16[2,3,128,128]{3,2,1,0:T(8,128)(2,1)}, u32[]{:S(2)}) copy-start(bf16[2,3,128,128]{3,2,1,0:T(8,128)(2,1)} %get-tuple-element.41.refs_0_) | copy-start | bytes 589828
  25.8 0.9 %copy-start.4 = (bf16[2,3,128,128]{3,2,1,0:T(8,128)(2,1)S(1)}, bf16[2,3,128,128]{3,2,1,0:T(8,128)(2,1)}, u32[]{:S(2)}) copy-start(bf16[2,3,128,128]{3,2,1,0:T(8,128)(2,1)} %get-tuple-element.42.refs_1_) | copy-start | bytes 589828
  26.7 0.7 %copy-start.3 = (bf16[2,3,128,128]{3,2,1,0:T(8,128)(2,1)}, bf16[2,3,128,128]{3,2,1,0:T(8,128)(2,1)S(1)}, u32[]{:S(2)}) copy-start(bf16[2,3,128,128]{3,2,1,0:T(8,128)(2,1)S(1)} %get-tuple-element.54) | copy-start | bytes 589828
  27.4 0.7 %copy-start.5 = (bf16[2,3,128,128]{3,2,1,0:T(8,128)(2,1)}, bf16[2,3,128,128]{3,2,1,0:T(8,128)(2,1)S(1)}, u32[]{:S(2)}) copy-start(bf16[2,3,128,128]{3,2,1,0:T(8,128)(2,1)S(1)} %get-tuple-element.55) | copy-start | bytes 589828
  29.1 5.6 %collective-permute-start.6 = (bf16[1,2,128,128]{3,2,1,0:T(8,128)(2,1)S(1)}, bf16[1,2,128,128]{3,2,1,0:T(8,128)(2,1)S(1)}, u32[]{:S(2)}, u32[]{:S(2)}) collective-permute-start(bf16[1,2,128,128]{3,2,1,0:T(8,128)(2,1)S(1)} %bitcast.7), channel_id=1, source_target_pairs={{0,1},{1,0},{2,3},{3,2},{4,5},{5,4},{6,7},{7,6},{8,9},{9,8},{10,11... | collective-permute-start | bytes 196616 | tf_op jit(solution)/shard_map/ppermute | solution.py:601
  29.2 22.0 %collective-permute-start.4 = (bf16[2,3,128,128]{3,2,1,0:T(8,128)(2,1)}, bf16[2,3,128,128]{3,2,1,0:T(8,128)(2,1)S(1)}, u32[]{:S(2)}, u32[]{:S(2)}) collective-permute-start(bf16[2,3,128,128]{3,2,1,0:T(8,128)(2,1)} %copy-done.3), channel_id=1, source_target_pairs={{0,4},{5,1},{2,6},{7,3},{4,8},{9,5},{6,10},{11,7},{8,12},{13,9},{1... | collective-permute-start | bytes 589832 | tf_op jit(solution)/shard_map/ppermute | solution.py:626
  33.5 17.7 %collective-permute-start.5 = (bf16[2,3,128,128]{3,2,1,0:T(8,128)(2,1)}, bf16[2,3,128,128]{3,2,1,0:T(8,128)(2,1)S(1)}, u32[]{:S(2)}, u32[]{:S(2)}) collective-permute-start(bf16[2,3,128,128]{3,2,1,0:T(8,128)(2,1)} %copy-done.5), channel_id=1, source_target_pairs={{4,0},{1,5},{6,2},{3,7},{8,4},{5,9},{10,6},{7,11},{12,8},{9,13},{1... | collective-permute-start | bytes 589832 | tf_op jit(solution)/shard_map/ppermute | solution.py:626
  34.8 2.1 %copy-start.7 = (s32[1,2,30]{2,1,0:T(2,128)S(1)}, s32[1,2,30]{2,1,0:T(2,128)}, u32[]{:S(2)}) copy-start(s32[1,2,30]{2,1,0:T(2,128)} %rest_8_.1) | copy-start | bytes 724
  34.8 15.6 %collective-permute-start.7 = (bf16[2,2,128,128]{3,2,1,0:T(8,128)(2,1)S(1)}, bf16[2,2,128,128]{3,2,1,0:T(8,128)(2,1)S(1)}, u32[]{:S(2)}, u32[]{:S(2)}) collective-permute-start(bf16[2,2,128,128]{3,2,1,0:T(8,128)(2,1)S(1)} %pad_maximum_fusion), channel_id=1, source_target_pairs={{0,2},{1,3},{2,0},{3,1},{4,6},{5,7},{6,4},{7,5},{8,10},{9,11},{10,... | collective-permute-start | bytes 393224 | tf_op jit(solution)/shard_map/ppermute | solution.py:601
  52.1 1.4 %collective-permute-start.8 = (bf16[544,128]{1,0:T(8,128)(2,1)S(1)}, bf16[544,128]{1,0:T(8,128)(2,1)S(1)}, u32[]{:S(2)}, u32[]{:S(2)}) collective-permute-start(bf16[544,128]{1,0:T(8,128)(2,1)S(1)} %get-tuple-element.64), channel_id=1, source_target_pairs={{0,1},{1,0},{2,3},{3,2},{4,5},{5,4},{6,7},{7,6},{8,9},{9,8},{10,11... | collective-permute-start | bytes 417800 | tf_op jit(solution)/shard_map/ppermute | solution.py:505
  53.5 4.5 %collective-permute-start.9 = (bf16[288,128]{1,0:T(8,128)(2,1)S(1)}, bf16[288,128]{1,0:T(8,128)(2,1)S(1)}, u32[]{:S(2)}, u32[]{:S(2)}) collective-permute-start(bf16[288,128]{1,0:T(8,128)(2,1)S(1)} %get-tuple-element.67), channel_id=1, source_target_pairs={{0,2},{1,3},{2,0},{3,1},{4,6},{5,7},{6,4},{7,5},{8,10},{9,11},{10,... | collective-permute-start | bytes 221192 | tf_op jit(solution)/shard_map/ppermute | solution.py:505
  60.0 1.4 %collective-permute-start.10 = (bf16[544,128]{1,0:T(8,128)(2,1)S(1)}, bf16[544,128]{1,0:T(8,128)(2,1)S(1)}, u32[]{:S(2)}, u32[]{:S(2)}) collective-permute-start(bf16[544,128]{1,0:T(8,128)(2,1)S(1)} %get-tuple-element.73), channel_id=1, source_target_pairs={{0,1},{1,0},{2,3},{3,2},{4,5},{5,4},{6,7},{7,6},{8,9},{9,8},{10,11... | collective-permute-start | bytes 417800 | tf_op jit(solution)/shard_map/ppermute | solution.py:505
  61.4 4.4 %collective-permute-start.11 = (bf16[288,128]{1,0:T(8,128)(2,1)S(1)}, bf16[288,128]{1,0:T(8,128)(2,1)S(1)}, u32[]{:S(2)}, u32[]{:S(2)}) collective-permute-start(bf16[288,128]{1,0:T(8,128)(2,1)S(1)} %get-tuple-element.76), channel_id=1, source_target_pairs={{0,2},{1,3},{2,0},{3,1},{4,6},{5,7},{6,4},{7,5},{8,10},{9,11},{10,... | collective-permute-start | bytes 221192 | tf_op jit(solution)/shard_map/ppermute | solution.py:505
